TPU v7x, 128 devices: a whole 4x4x4 slice. The times are simulated.
128 devices in a mesh: trial: 32 (over z_hi, y, x), batch: 4 (over z_lo, core).
Axes of the slice: x: 4, y: 4, z: 4 (z_hi: 2, z_lo: 2; z = z_hi * 2 + z_lo), core: 2. Of those that a mesh axis runs over, the one named last changes fastest.
Arguments:
- features16: bfloat16 [32, 4, 1024, 512], P('trial', 'batch'), may hold values from -6 to 6
- features32: bfloat16 [32, 4, 2048, 128], P('trial', 'batch'), may hold values from -6 to 6
- labels: int32 [32, 4, 512], P(None, 'batch'), may hold values from 0 to 18
- plan: int32 [4], replicated, may hold values from 0 to 31, as said below
- lr_index: int32 [32], P('trial'), may hold values from 0 to 1073741823
- w_plain: float32 [32, 256, 1024], P('trial'), may hold values from -0.1875 to 0.1875
- w_depth: float32 [32, 3, 9, 1024], P('trial'), may hold values from -2 to 2
- w_point: float32 [32, 3, 256, 1024], P('trial'), may hold values from -0.1875 to 0.1875
- w_pool: float32 [32, 256, 2048], P('trial'), may hold values from -0.125 to 0.125
- b_branch: float32 [32, 5, 256], P('trial'), may hold values from -3 to 3
- w_proj: float32 [32, 256, 1280], P('trial'), may hold values from -0.15625 to 0.15625
- b_proj: float32 [32, 256], P('trial'), may hold values from -3 to 3
- w_class: float32 [32, 19, 256], P('trial'), may hold values from -1 to 4
- b_class: float32 [32, 19], P('trial'), may hold values from -4 to 4
Outputs:
- new_w_plain: float32 [32, 256, 1024], P('trial')
- new_w_depth: float32 [32, 3, 9, 1024], P('trial')
- new_w_point: float32 [32, 3, 256, 1024], P('trial')
- new_w_pool: float32 [32, 256, 2048], P('trial')
- new_b_branch: float32 [32, 5, 256], P('trial')
- new_w_proj: float32 [32, 256, 1280], P('trial')
- new_b_proj: float32 [32, 256], P('trial')
- new_w_class: float32 [32, 19, 256], P('trial')
- new_b_class: float32 [32, 19], P('trial')
Inputs may be any that keep to these rules, and one draw needn't show every extreme that they name: `plan`: the 4 entries are distinct trial indices; 0 and 31 are always among them.
All inputs are finite; a program needn't handle non-finite values.
Results may differ from a plain program's by a relative error of at most 0.014.
The roundings to bfloat16 on the way count: a program that leaves them out, or rounds other values in their place, can miss the bound.
Values may be sent and summed in bfloat16 or wider, within the bound.
No kernel may reach another device: no remote copies, remote signals or barrier semaphores. Data moves between devices by JAX's collectives and lax.ppermute only.
A program may use at most 128 MiB of HBM per device.

v0:
```python
import functools

import jax
import jax.numpy as jnp
from jax import lax
from jax.experimental import pallas as pl
from jax.experimental.pallas import tpu as pltpu
from jax.sharding import PartitionSpec as P

W16 = 32
HID = 256
PAD = 24
DILATIONS = (6, 12, 18)
LANES = 128
RELATIVE = (0, -1, 1, 2)
BF16 = jnp.bfloat16
F32 = jnp.float32


def dot_nt(a, b):
    return lax.dot_general(a, b, (((1,), (1,)), ((), ())), preferred_element_type=F32)


def dot_nn(a, b):
    return lax.dot_general(a, b, (((1,), (0,)), ((), ())), preferred_element_type=F32)


def dot_exact(a, b):
    return lax.dot_general(
        a,
        b,
        (((1,), (0,)), ((), ())),
        precision=lax.Precision.HIGHEST,
        preferred_element_type=F32,
    )


def dot_exact_nt(a, b):
    return lax.dot_general(
        a,
        b,
        (((1,), (1,)), ((), ())),
        precision=lax.Precision.HIGHEST,
        preferred_element_type=F32,
    )


def dot_tn(a, b):
    return lax.dot_general(a, b, (((0,), (0,)), ((), ())), preferred_element_type=F32)


def taps_of_row(row, rows, dilation):
    taps = []
    for a in (-1, 0, 1):
        source = row + a * dilation
        if 0 <= source < rows:
            for b in (-1, 0, 1):
                taps.append((3 * (a + 1) + (b + 1), source, b * dilation))
    return taps


def clear_margins(padded):
    rows = padded.shape[0]
    blank = jnp.zeros((rows, PAD, LANES), F32)
    padded[:, 0:PAD, :] = blank
    padded[:, PAD + W16 : 2 * PAD + W16, :] = blank


def fill_padded(padded, x_ref, lanes):
    for row in range(padded.shape[0]):
        padded[row, PAD : PAD + W16, :] = x_ref[row * W16 : (row + 1) * W16, lanes].astype(F32)


def front_kernel(
    order,
    where_ref,
    piece0,
    piece1,
    piece2,
    piece3,
    marks,
    w_plain,
    w_depth,
    w_point,
    bias,
    w_proj,
    proj_bias,
    w_class,
    class_bias,
    maps_ref,
    joined_ref,
    dpre_ref,
    dz_ref,
    sums_ref,
    dclass_ref,
    padded,
):
    x_ref = maps_ref.at[0]
    x, y, z = where_ref[0], where_ref[1], where_ref[2]
    for outer, piece in enumerate((piece0, piece1, piece2, piece3)):
        for inner in range(4):
            far, near = RELATIVE[outer] + 4, RELATIVE[inner] + 4
            if order == 0:
                xx, yy = lax.rem(x + far, 4), lax.rem(y + near, 4)
            else:
                xx, yy = lax.rem(x + near, 4), lax.rem(y + far, 4)
            for k in range(2):
                zz = z if k == 0 else 1 - z
                start = pl.multiple_of((zz * 16 + yy * 4 + xx) * 16, 16)
                x_ref[pl.ds(start, 16), :] = piece[pl.ds((2 * inner + k) * 16, 16), :]
    rows = padded.shape[0]
    clear_margins(padded)

    def chunk(j, carry):
        lanes = pl.ds(pl.multiple_of(j * LANES, LANES), LANES)
        fill_padded(padded, x_ref, lanes)
        for k, dilation in enumerate(DILATIONS):
            for row in range(rows):
                total = jnp.zeros((W16, LANES), F32)
                for tap, source, shift in taps_of_row(row, rows, dilation):
                    weight = w_depth[9 * k + tap, :, lanes]
                    total = total + weight * padded[source, PAD + shift : PAD + shift + W16, :]
                maps_ref[k + 1, row * W16 : (row + 1) * W16, lanes] = total.astype(BF16)
        return carry

    lax.fori_loop(0, x_ref.shape[1] // LANES, chunk, 0)

    for branch in range(4):
        columns = slice(branch * HID, (branch + 1) * HID)
        if branch == 0:
            pre = dot_nt(x_ref[...], w_plain[...])
        else:
            pre = dot_nt(maps_ref[branch], w_point[branch - 1])
        joined_ref[:, columns] = jnp.maximum(pre + bias[:, columns], 0.0).astype(BF16)
    hidden = jnp.maximum(dot_nt(joined_ref[...], w_proj[...]) + proj_bias[...], 0.0).astype(BF16)
    logits = dot_nt(w_class[...], hidden) + class_bias[...]
    top = jnp.max(logits, axis=0, keepdims=True)
    raised = jnp.exp(logits - top)
    share = raised / jnp.sum(raised, axis=0, keepdims=True)
    class_ids = lax.broadcasted_iota(jnp.int32, logits.shape, 0)
    dlogits = share - jnp.where(class_ids == marks[...], 1.0, 0.0)
    square = (logits.shape[0], LANES)
    column = jnp.broadcast_to(jnp.sum(dlogits, axis=1, keepdims=True), square)
    on_diagonal = lax.broadcasted_iota(jnp.int32, square, 0) == lax.broadcasted_iota(
        jnp.int32, square, 1
    )
    short = dlogits.astype(BF16)
    dclass_ref[...] = dot_nn(short, hidden)
    dhidden = dot_tn(short, w_class[...])
    dpre = jnp.where(hidden.astype(F32) > 0, dhidden, 0.0)
    dpre_short = dpre.astype(BF16)
    dpre_ref[...] = dpre_short
    sums_ref[...] = jnp.zeros(sums_ref.shape, F32)
    sums_ref[3:4, 0:LANES] = jnp.sum(jnp.where(on_diagonal, column, 0.0), axis=0, keepdims=True)
    sums_ref[1:2, 0:HID] = jnp.sum(dpre_short.astype(F32), axis=0, keepdims=True)
    for branch in range(4):
        columns = slice(branch * HID, (branch + 1) * HID)
        djoined = dot_nn(dpre_short, w_proj[:, columns])
        dz = jnp.where(joined_ref[:, columns].astype(F32) > 0, djoined, 0.0).astype(BF16)
        dz_ref[:, columns] = dz
        sums_ref[0:1, columns] = jnp.sum(dz.astype(F32), axis=0, keepdims=True)


VMEM = pl.BlockSpec(memory_space=pltpu.VMEM)
SMEM = pl.BlockSpec(memory_space=pltpu.SMEM)


def front(order, where, pieces, marks, weights):
    pixels, channels = marks.shape[1], weights[0].shape[1]
    shapes = (
        ((4, pixels, channels), BF16),
        ((pixels, 4 * HID), BF16),
        ((pixels, HID), BF16),
        ((pixels, 4 * HID), BF16),
        ((8, 4 * HID), F32),
        ((32, HID), F32),
    )
    return pl.pallas_call(
        functools.partial(front_kernel, order),
        name="front",
        out_shape=[pltpu.VMEM(*shape) for shape in shapes],
        in_specs=[SMEM] + [VMEM] * (4 + 1 + len(weights)),
        out_specs=[VMEM] * len(shapes),
        scratch_shapes=[pltpu.VMEM((pixels // W16, 2 * PAD + W16, LANES), F32)],
        compiler_params=pltpu.CompilerParams(vmem_limit_bytes=16 * 2**20),
        cost_estimate=pl.CostEstimate(
            flops=6_700_000_000, bytes_accessed=12_000_000, transcendentals=16384
        ),
    )(where, *pieces, marks, *weights)


def taps_kernel(maps_ref, dz_ref, w_point, out_ref, padded, ddepth):
    x_ref = maps_ref.at[0]
    rows = padded.shape[1]
    halves = padded.shape[0]
    for half in range(halves):
        start = pl.multiple_of((pl.program_id(0) * halves + half) * LANES, LANES)
        clear_margins(padded.at[half])
        fill_padded(padded.at[half], x_ref, pl.ds(start, LANES))
    out_ref[...] = jnp.zeros(out_ref.shape, F32)
    for k, dilation in enumerate(DILATIONS):
        back = dot_nn(dz_ref[:, (k + 1) * HID : (k + 2) * HID], w_point[k])
        ddepth[k] = back.astype(BF16).astype(F32)
    for half in range(halves):
        lanes = slice(half * LANES, (half + 1) * LANES)
        for k, dilation in enumerate(DILATIONS):
            totals = {}
            for row in range(rows):
                slope = ddepth[k, row * W16 : (row + 1) * W16, lanes]
                for tap, source, shift in taps_of_row(row, rows, dilation):
                    value = slope * padded[half, source, PAD + shift : PAD + shift + W16, :]
                    value = jnp.sum(value.reshape(W16 // 8, 8, LANES), axis=0)
                    totals[tap] = value if tap not in totals else totals[tap] + value
            for tap, value in totals.items():
                out_ref[9 * k + tap : 9 * k + tap + 1, lanes] = jnp.sum(
                    value, axis=0, keepdims=True
                )


def depth_taps(maps, dz, w_point):
    pixels, channels = maps.shape[1:]
    block = 256
    return pl.pallas_call(
        taps_kernel,
        name="taps",
        grid=(channels // block,),
        out_shape=jax.ShapeDtypeStruct((32, channels), F32),
        in_specs=[
            VMEM,
            VMEM,
            pl.BlockSpec((3, HID, block), lambda j: (0, 0, j)),
        ],
        out_specs=pl.BlockSpec((32, block), lambda j: (0, j)),
        scratch_shapes=[
            pltpu.VMEM((block // LANES, pixels // W16, 2 * PAD + W16, LANES), F32),
            pltpu.VMEM((3, pixels, block), F32),
        ],
        compiler_params=pltpu.CompilerParams(vmem_limit_bytes=16 * 2**20),
        cost_estimate=pl.CostEstimate(
            flops=4_500_000_000, bytes_accessed=4_000_000, transcendentals=0
        ),
    )(maps, dz, w_point)


PRODUCT_COLUMNS = 512


def product_kernel(count, first, *refs):
    out_ref = refs[-1]
    layer, step = first + pl.program_id(0), pl.program_id(1)
    left_columns = pl.ds(pl.multiple_of(layer * HID, HID), HID)
    columns = pl.ds(pl.multiple_of(step * PRODUCT_COLUMNS, PRODUCT_COLUMNS), PRODUCT_COLUMNS)
    total = None
    for left, right in zip(refs[:count], refs[count : 2 * count]):
        right = right[layer, :, columns] if len(right.shape) == 3 else right[:, columns]
        part = dot_tn(left[:, left_columns], right)
        total = part if total is None else total + part
    out_ref[0] = total.astype(BF16)


def products(lefts, rights, first, layers):
    channels = rights[0].shape[-1]
    count = len(lefts)
    return pl.pallas_call(
        functools.partial(product_kernel, count, first),
        name="products",
        grid=(layers, channels // PRODUCT_COLUMNS),
        out_shape=jax.ShapeDtypeStruct((layers, HID, channels), BF16),
        in_specs=[VMEM] * (2 * count),
        out_specs=pl.BlockSpec((1, HID, PRODUCT_COLUMNS), lambda k, j: (k, 0, j)),
        compiler_params=pltpu.CompilerParams(vmem_limit_bytes=10 * 2**20),
        cost_estimate=pl.CostEstimate(
            flops=layers * 2_200_000_000, bytes_accessed=layers * 5_000_000, transcendentals=0
        ),
    )(*lefts, *rights)


STEPS = 4


def update_kernel(
    core_ref,
    rate_ref,
    w_plain,
    w_point,
    w_pool,
    w_proj,
    w_depth,
    b_branch,
    b_proj,
    w_class,
    b_class,
    mine0,
    rest0,
    mine1,
    rest1,
    mine2,
    rest2,
    left,
    factors,
    small,
    new_plain,
    new_point,
    new_pool,
    new_proj,
    new_depth,
    new_b_branch,
    new_b_proj,
    new_class,
    new_b_class,
    scale_ref,
):
    step = pl.program_id(0)
    pairs = ((mine0, rest0), (mine1, rest1), (mine2, rest2))
    count = factors.shape[0]
    entries = sum(
        STEPS * array[...].size for array in (w_plain, w_point, w_pool, w_proj)
    ) + sum(array[...].size for array in (w_depth, b_branch, b_proj, w_class, b_class))

    def outer_squared(a, b):
        product = dot_exact_nt(a, a) * dot_exact_nt(b, b)
        return jnp.sum(product, keepdims=True)

    @pl.when(step == 0)
    def _():
        total = jnp.zeros((16, small.shape[1]), F32)
        for mine, rest in pairs:
            for row in range(0, mine.shape[1], 16):
                for layer in range(mine.shape[0]):
                    one = mine[layer, row : row + 16, :].astype(F32)
                    other = rest[layer, row : row + 16, :].astype(F32)
                    total = total + (one * one + other * other)
        for row in range(0, small.shape[0], 16):
            total = total + jnp.square(small[row : row + 16, :])
        squares = jnp.sum(total, keepdims=True)
        squares = squares + outer_squared(factors[:, :HID], factors[:, 3 * HID :])
        squares = squares + outer_squared(
            factors[:, HID : 2 * HID], factors[:, 2 * HID : 3 * HID]
        )
        norm_scale = jnp.sqrt(squares / entries + 1e-06)
        scale_ref[...] = jnp.broadcast_to(rate_ref[0] / norm_scale, scale_ref.shape)

    scale = scale_ref[0:1, 0:1]

    def large(side):
        rows = w_plain.shape[1]
        here = pl.ds(pl.multiple_of(lax.rem(step, STEPS // 2) * rows, rows), rows)
        proj, low, high = (
            [pair[side][layer, here, :] for layer in range(pair[side].shape[0])] for pair in pairs
        )
        wide = proj[0].shape[-1]
        new_plain[0] = w_plain[0] - scale * low[0].astype(F32)
        new_point[0, 0] = w_point[0, 0] - scale * low[1].astype(F32)
        new_point[0, 1] = w_point[0, 1] - scale * high[0].astype(F32)
        new_point[0, 2] = w_point[0, 2] - scale * high[1].astype(F32)
        new_proj[0, :, :wide] = w_proj[0, :, :wide] - scale * proj[0].astype(F32)
        proj4_grad = dot_exact(left[1, :, :count], factors[:, 2 * HID : 3 * HID])
        new_proj[0, :, wide:] = w_proj[0, :, wide:] - scale * proj4_grad
        pool_grad = dot_exact(left[0, :, :count], factors[:, 3 * HID :])
        new_pool[0] = w_pool[0] - scale * pool_grad

    @pl.when(step < STEPS // 2)
    def _():
        large(0)

    @pl.when(step >= STEPS // 2)
    def _():
        large(1)

    @pl.when(step == 0)
    def _():
        for row in range(w_depth.shape[0]):
            new_depth[row] = w_depth[row] - scale * small[row : row + 1, :]
        for branch in range(5):
            row = 32 if branch < 4 else 34
            first = branch % 4 * HID
            new_b_branch[branch] = (
                b_branch[branch] - scale * small[row : row + 1, first : first + HID]
            )
        new_b_proj[...] = b_proj[...] - scale * small[33:34, :HID]
        classes = w_class.shape[0]
        for index in range(classes):
            row, first = 40 + index % 8, index // 8 * HID
            new_class[index] = w_class[index] - scale * small[row : row + 1, first : first + HID]
        new_b_class[...] = b_class[...] - scale * small[35:36, :classes]


def update(core, rate, params, halves, left, factors, small):
    w_plain, w_depth, w_point, w_pool, b_branch, w_proj, b_proj, w_class, b_class = params
    inputs = (w_plain, w_point, w_pool, w_proj) + tuple(
        array if array.ndim == 2 else array.reshape(-1, 1, array.shape[-1])
        for array in (w_depth, b_branch, b_proj, w_class, b_class)
    )
    rows, half = HID // STEPS, STEPS // 2

    def where(step, core_ref):
        return lax.rem(step + core_ref[0] * half, STEPS)

    def by_rows(shape):
        if len(shape) == 2:
            return pl.BlockSpec((rows, shape[1]), lambda j, core: (where(j, core), 0))
        if len(shape) == 3:
            return pl.BlockSpec((1, rows, shape[2]), lambda j, core: (0, where(j, core), 0))
        return pl.BlockSpec((1, shape[1], rows, shape[3]), lambda j, core: (0, 0, where(j, core), 0))

    def whole(shape):
        return pl.BlockSpec(shape, lambda j, core: (0,) * len(shape))

    specs = [by_rows(array.shape) for array in inputs[:4]] + [whole(array.shape) for array in inputs[4:]]
    new = pl.pallas_call(
        update_kernel,
        name="update",
        out_shape=[jax.ShapeDtypeStruct(array.shape, F32) for array in inputs],
        grid_spec=pltpu.PrefetchScalarGridSpec(
            num_scalar_prefetch=1,
            grid=(STEPS,),
            in_specs=[SMEM]
            + specs
            + [VMEM] * (2 * len(halves))
            + [pl.BlockSpec((2, rows, LANES), lambda j, core: (0, where(j, core), 0)), VMEM, VMEM],
            out_specs=specs,
            scratch_shapes=[pltpu.VMEM((8, LANES), F32)],
        ),
        compiler_params=pltpu.CompilerParams(vmem_limit_bytes=60 * 2**20),
        cost_estimate=pl.CostEstimate(
            flops=4_000_000, bytes_accessed=20_000_000, transcendentals=0
        ),
    )(core, rate, *inputs, *(array for pair in halves for array in pair), left, factors, small)
    order = (0, 4, 1, 2, 5, 3, 6, 7, 8)
    return tuple(new[i].reshape(param.shape) for i, param in zip(order, params))


def place(z, y, x):
    return z * 16 + (y % 4) * 4 + x % 4


EVERY = [(z, y, x) for z in range(2) for y in range(4) for x in range(4)]


def along_x(step):
    return [(place(z, y, x), place(z, y, x + step)) for z, y, x in EVERY]


def along_y(step):
    return [(place(z, y, x), place(z, y + step, x)) for z, y, x in EVERY]


ACROSS_Z = [(t, (t + 16) % 32) for t in range(32)]
CORES = [(b, b ^ 1) for b in range(4)]
CHIPS = [(b, b ^ 2) for b in range(4)]


def gather_ring(block, along):
    return (
        block,
        lax.ppermute(block, "trial", along(1)),
        lax.ppermute(block, "trial", along(-1)),
        lax.ppermute(block, "trial", along(2)),
    )


def from_batch(mine):
    return [mine] + [
        lax.ppermute(mine, "batch", [(b, b ^ other) for b in range(4)]) for other in (1, 2, 3)
    ]


def in_order(parts, core, chip):
    near, beside, across, beyond = parts
    low = jnp.where(core == 0, jnp.concatenate([near, beside]), jnp.concatenate([beside, near]))
    high = jnp.where(core == 0, jnp.concatenate([across, beyond]), jnp.concatenate([beyond, across]))
    return jnp.where(chip == 0, jnp.concatenate([low, high]), jnp.concatenate([high, low]))


def sum_cores(partial, core):
    half = partial.shape[1] // 2
    mine = lax.dynamic_slice_in_dim(partial, core * half, half, 1)
    other = lax.dynamic_slice_in_dim(partial, (1 - core) * half, half, 1)
    return (mine.astype(F32) + lax.ppermute(other, "batch", CORES).astype(F32)).astype(BF16)


def sum_chips(pair):
    return (pair.astype(F32) + lax.ppermute(pair, "batch", CHIPS).astype(F32)).astype(BF16)


def sum_batch_small(partial):
    near, beside, across, beyond = [part.astype(F32) for part in from_batch(partial)]
    return (near + beside) + (across + beyond)


def pick(table, plan, turn_ids):
    return jnp.stack(
        [lax.dynamic_index_in_dim(table, plan[m], 0, keepdims=False) for m in turn_ids]
    )


def pool_map(coarse):
    return (jnp.sum(coarse, axis=-1, dtype=F32) / coarse.shape[-1]).astype(BF16)


def on_device(
    features16,
    features32,
    labels,
    plan,
    lr_index,
    w_plain,
    w_depth,
    w_point,
    w_pool,
    b_branch,
    w_proj,
    b_proj,
    w_class,
    b_class,
):
    turns = plan.shape[0]
    trial = lax.axis_index("trial")
    batch = lax.axis_index("batch")
    core, chip = batch % 2, batch // 2
    where = jnp.stack([trial % 4, (trial // 4) % 4, trial // 16]).astype(jnp.int32)

    own = features16[0, 0].T
    channels = own.shape[1]
    pieces = lax.all_to_all(own.reshape(32, 16, channels), "trial", 0, 0, tiled=True)
    turn_lists = [list(range(order, turns, 2)) for order in range(2)]
    picked = pick(pieces, plan, turn_lists[0] + turn_lists[1])
    pooled = pool_map(features32[0, 0]).reshape(-1, 1, channels)
    pooled = jnp.where((plan == trial)[None, :, None], pooled, jnp.zeros((), BF16))
    pooled = pooled.reshape(-1, channels)
    rows = pooled.shape[0]
    across = lax.ppermute(
        jnp.concatenate([picked.reshape(-1, channels), pooled]), "trial", ACROSS_Z
    )
    pooled = pooled + across[-rows:]
    across = across[:-rows].reshape(picked.shape)
    blocks, outers = [None] * turns, [None] * turns
    for order, (inner, outer) in enumerate(((along_y, along_x), (along_x, along_y))):
        turn_ids = turn_lists[order]
        count = len(turn_ids)
        some = slice(order * len(turn_lists[0]), order * len(turn_lists[0]) + count)
        block = jnp.stack([picked[some], across[some]], axis=1).reshape(-1, channels)
        size = block.shape[0]
        if order == 0:
            block = jnp.concatenate([block, pooled])
        ring = gather_ring(block, inner)
        if order == 0:
            pooled = sum(part[size:] for part in ring)
        for place_in, m in enumerate(turn_ids):
            first, last = place_in * size // count, (place_in + 1) * size // count
            parts = [part[first:last] for part in ring]
            blocks[m] = jnp.concatenate(parts + [pooled] if m == 0 else parts)
            outers[m] = outer
    after = lax.optimization_barrier
    maps = [gather_ring(blocks[m], outers[m]) for m in range(2)]
    pooled = sum(part[4 * size // count :] for part in maps[0])
    pooled = [pooled[first : first + turns] for first in range(0, rows, turns)]

    point16 = w_point[0].astype(BF16)
    proj16 = w_proj[0].astype(BF16)
    taps = w_depth.reshape(27, 1, -1)
    classes = w_class.shape[1]
    class16 = jnp.pad(w_class[0].astype(BF16), ((0, 32 - classes), (0, 0)))
    class_bias = jnp.pad(b_class[0], (0, 32 - classes), constant_values=-1e30)[:, None]
    wide = 4 * HID
    pool16 = w_pool[0].astype(BF16)
    branch4 = sum(
        dot_nt(part, pool16[:, i * channels : (i + 1) * channels]) for i, part in enumerate(pooled)
    )
    branch4 = jax.nn.relu(branch4 + b_branch[0, 4]).astype(BF16)
    proj_bias = dot_nt(branch4, proj16[:, wide:]) + b_proj[0]
    marks = pick(labels[:, 0], plan, range(turns))

    fronts = []
    for m in range(turns):
        if m >= 2:
            maps.append(gather_ring(blocks[m], outers[m]))
        weights = (
            w_plain[0].astype(BF16),
            taps,
            point16,
            b_branch[0, :4].reshape(1, wide),
            proj16[:, :wide],
            proj_bias[m : m + 1],
            class16,
            class_bias,
        )
        if m == 0:
            maps[0], blocks[2] = after((maps[0], blocks[2]))
        fronts.append(front(m % 2, where, maps[m], marks[m : m + 1], weights))
        if m == 0:
            fronts[0], maps[1], blocks[3] = after((fronts[0], maps[1], blocks[3]))
    stacks, joined, dpres, dzs, sums, dclass = zip(*fronts)

    dbias_proj = jnp.stack([part[1, :HID] for part in sums])
    dbranch4 = dot_exact(dbias_proj, proj16[:, wide:].astype(F32))
    dbranch4 = jnp.where(branch4 > 0, dbranch4, 0.0)
    factors = [dbranch4, dbias_proj, branch4] + pooled
    factors = jnp.concatenate([part.astype(F32) for part in factors], axis=1)
    factors = from_batch(jnp.pad(factors, ((0, 8 - turns), (0, 0))))
    proj_part = products(dpres, joined, 0, 1)
    dzs, proj_part = after((dzs, proj_part))
    proj_pair = sum_cores(proj_part, core)
    low_part = products(dzs, stacks, 0, 2)
    dzs, low_part, proj_pair = after((dzs, low_part, proj_pair))
    low_pair = sum_cores(low_part, core)
    high_part = products(dzs, stacks, 2, 2)
    proj_total = sum_chips(proj_pair)
    dzs, high_part, low_pair = after((dzs, high_part, low_pair))
    high_pair = sum_cores(high_part, core)
    depth_part = depth_taps(stacks[0], dzs[0], point16)
    dzs, depth_part, high_pair, proj_total = after((dzs, depth_part, high_pair, proj_total))
    low_total = sum_chips(low_pair)
    for m in range(1, turns):
        depth_part = depth_part + depth_taps(stacks[m], dzs[m], point16)
        if m == 2:
            low_total, depth_part = after((low_total, depth_part))
    totals = [proj_total, low_total, sum_chips(high_pair)]
    halves = [(total, lax.ppermute(total, "batch", CORES)) for total in totals]

    factors, depth_part = after((factors, depth_part))
    factors = in_order(factors, core, chip)
    left = jnp.pad(factors[:, : 2 * HID].T, ((0, 0), (0, LANES - factors.shape[0])))
    left = left.reshape(2, HID, LANES)

    dclass = sum(dclass)
    bias_row = jnp.pad(jnp.sum(dbranch4, axis=0)[None], ((2, 5), (0, wide - HID)))
    small = jnp.concatenate(
        [
            depth_part,
            sum(sums) + bias_row,
            jnp.concatenate([dclass[8 * g : 8 * g + 8] for g in range(4)], axis=1),
        ]
    )
    small = sum_batch_small(small.astype(BF16))

    params = (w_plain, w_depth, w_point, w_pool, b_branch, w_proj, b_proj, w_class, b_class)

    step_rate = 0.5 * jnp.exp2(-6.0 * lr_index[0].astype(F32) / 1073741824.0)
    return update(
        core.reshape(1).astype(jnp.int32), step_rate.reshape(1), params, halves, left, factors, small
    )


def solution(mesh):
    in_specs = (
        P("trial", "batch", None, None),
        P("trial", "batch", None, None),
        P(None, "batch", None),
        P(),
        P("trial"),
        P("trial", None, None),
        P("trial", None, None, None),
        P("trial", None, None, None),
        P("trial", None, None),
        P("trial", None, None),
        P("trial", None, None),
        P("trial", None),
        P("trial", None, None),
        P("trial", None),
    )
    out_specs = (
        P("trial", None, None),
        P("trial", None, None, None),
        P("trial", None, None, None),
        P("trial", None, None),
        P("trial", None, None),
        P("trial", None, None),
        P("trial", None),
        P("trial", None, None),
        P("trial", None),
    )
    return jax.shard_map(
        on_device, mesh=mesh, in_specs=in_specs, out_specs=out_specs, check_vma=False
    )
```

profile of v0, /device:TPU:1, one launch (start us, length us, event | category | flops | bytes accessed | tf_op | source)
XLA Modules:
  0.0 172.2 jit_solution(6710225352663623249)
XLA Ops:
  0.7 2.3 %copy.32 = bf16[1,1,1024,512]{2,3,1,0:T(8,128)(2,1)} copy(bf16[1,1,1024,512]{3,2,1,0:T(8,128)(2,1)} %param.14) | data formatting | bytes 2097152 | tf_op args[0]
  3.0 11.3 %all-to-all-start = ((bf16[32,16,1024]{2,1,0:T(8,128)(2,1)}), bf16[32,16,1024]{2,1,0:T(8,128)(2,1)}, u32[]{:S(2)}, u32[]{:S(2)}) async-start(bf16[32,16,1024]{2,1,0:T(8,128)(2,1)} %bitcast.9), calls=%async_computation | async-start | bytes 2097152 | tf_op jit(solution)/shard_map/all_to_all | solution.py:525
  14.3 0.6 fusion.30
  20.6 2.2 %convert_bitcast_fusion.w_point = bf16[3,256,1024]{2,1,0:T(8,128)(2,1)S(1)} fusion(f32[1,3,256,1024]{3,2,1,0:T(8,128)} %w_point.1), kind=kLoop, calls=%fused_computation | loop fusion | flops 786432 | bytes 4718592 | tf_op jit(solution)/shard_map/convert_element_type | solution.py:559
  25.7 0.7 fusion.18
  26.4 2.7 %convert_bitcast_fusion.1 = bf16[256,2048]{1,0:T(8,128)(2,1)} fusion(f32[1,256,2048]{2,1,0:T(8,128)} %w_pool.1), kind=kLoop, calls=%fused_computation.11 | loop fusion | flops 524288 | bytes 3145728 | tf_op jit(solution)/shard_map/convert_element_type | solution.py:566
  29.1 0.9 convert_bitcast_fusion.2
  30.0 1.2 all-to-all-done
  31.2 0.8 constant_dynamic-slice_fusion.8
  32.1 1.5 collective-permute-start
  33.7 1.1 slice.255.w_proj
  35.7 2.0 %collective-permute-done = bf16[72,1024]{1,0:T(8,128)(2,1)S(1)} collective-permute-done((bf16[72,1024]{1,0:T(8,128)(2,1)S(1)}, bf16[72,1024]{1,0:T(8,128)(2,1)S(1)}, u32[]{:S(2)}, u32[]{:S(2)}) %collective-permute-start) | collective-permute-done | bytes 147488 | tf_op jit(solution)/shard_map/ppermute | solution.py:532
  37.7 0.4 collective-permute-start.7
  38.2 2.3 %collective-permute-start.8 = (bf16[64,1024]{1,0:T(8,128)(2,1)S(1)}, bf16[64,1024]{1,0:T(8,128)(2,1)S(1)}, u32[]{:S(2)}, u32[]{:S(2)}) collective-permute-start(bf16[64,1024]{1,0:T(8,128)(2,1)S(1)} %bitcast.83), channel_id=1, source_target_pairs={{0,12},{4,0},{8,4},{12,8},{16,28},{20,16},{24,20},{28,24},{32,44},... | collective-permute-start | bytes 393224 | tf_op jit(solution)/shard_map/ppermute | solution.py:457
  40.5 1.1 collective-permute-start.9
  41.7 0.4 collective-permute-start.1
  42.1 2.3 %collective-permute-start.2 = (bf16[72,1024]{1,0:T(8,128)(2,1)S(1)}, bf16[72,1024]{1,0:T(8,128)(2,1)S(1)}, u32[]{:S(2)}, u32[]{:S(2)}) collective-permute-start(bf16[72,1024]{1,0:T(8,128)(2,1)S(1)} %pad_maximum_fusion.6), channel_id=1, source_target_pairs={{0,48},{4,52},{8,56},{12,60},{16,0},{20,4},{24,8},{28,12},{32,16},... | collective-permute-start | bytes 442376 | tf_op jit(solution)/shard_map/ppermute | solution.py:457
  44.5 0.7 collective-permute-start.3
  45.3 1.7 %collective-permute-done.9 = bf16[64,1024]{1,0:T(8,128)(2,1)S(1)} collective-permute-done((bf16[64,1024]{1,0:T(8,128)(2,1)S(1)}, bf16[64,1024]{1,0:T(8,128)(2,1)S(1)}, u32[]{:S(2)}, u32[]{:S(2)}) %collective-permute-start.9) | collective-permute-done | bytes 131104 | tf_op jit(solution)/shard_map/ppermute | solution.py:458
  47.3 0.8 collective-permute-done.2
  48.1 2.8 %collective-permute-done.3 = bf16[72,1024]{1,0:T(8,128)(2,1)S(1)} collective-permute-done((bf16[72,1024]{1,0:T(8,128)(2,1)S(1)}, bf16[72,1024]{1,0:T(8,128)(2,1)S(1)}, u32[]{:S(2)}, u32[]{:S(2)}) %collective-permute-start.3) | collective-permute-done | bytes 147488 | tf_op jit(solution)/shard_map/ppermute | solution.py:458
  51.1 2.7 %collective-permute-start.5 = (bf16[136,1024]{1,0:T(8,128)(2,1)S(1)}, bf16[136,1024]{1,0:T(8,128)(2,1)S(1)}, u32[]{:S(2)}, u32[]{:S(2)}) collective-permute-start(bf16[136,1024]{1,0:T(8,128)(2,1)S(1)} %get-tuple-element.88.piece0), channel_id=1, source_target_pairs={{0,12},{4,0},{8,4},{12,8},{16,28},{20,16},{24,20},{28,24},{32,44},... | collective-permute-start | bytes 835592 | tf_op jit(solution)/shard_map/ppermute | solution.py:457
  53.9 2.7 %collective-permute-start.11 = (bf16[128,1024]{1,0:T(8,128)(2,1)S(1)}, bf16[128,1024]{1,0:T(8,128)(2,1)S(1)}, u32[]{:S(2)}, u32[]{:S(2)}) collective-permute-start(bf16[128,1024]{1,0:T(8,128)(2,1)S(1)} %pad_maximum_fusion.1.piece0), channel_id=1, source_target_pairs={{0,48},{4,52},{8,56},{12,60},{16,0},{20,4},{24,8},{28,12},{32,16},... | collective-permute-start | bytes 786440 | tf_op jit(solution)/shard_map/ppermute | solution.py:457
  56.6 1.1 collective-permute-done.4.piece1
  57.7 0.7 collective-permute-start.12
  58.4 2.1 %collective-permute-done.5.piece2 = bf16[136,1024]{1,0:T(8,128)(2,1)S(1)} collective-permute-done((bf16[136,1024]{1,0:T(8,128)(2,1)S(1)}, bf16[136,1024]{1,0:T(8,128)(2,1)S(1)}, u32[]{:S(2)}, u32[]{:S(2)}) %collective-permute-start.5) | collective-permute-done | bytes 278560 | tf_op jit(solution)/shard_map/ppermute | solution.py:457
  60.5 1.6 collective-permute-done.6.piece3
  62.6 1.1 convolution_add_fusion
  63.7 5.8 %front.4 = (bf16[4,512,1024]{2,1,0:T(8,128)(2,1)S(1)}, bf16[512,1024]{1,0:T(8,128)(2,1)S(1)}, bf16[512,256]{1,0:T(8,128)(2,1)S(1)}, bf16[512,1024]{1,0:T(8,128)(...) custom-call(s32[3]{0:T(128)S(1)} %pad_add_fusion.where_ref, bf16[136,1024]{1,0:T(8,128)(2,1)S(1)} %get-tuple-element.88.piece0, ...), custom_call_target="tpu_custom_call" | custom-call | flops 6700000256 | bytes 12000000 | tf_op jit(solution)/shard_map/front/pallas_call | solution.py:178
  69.7 2.7 %collective-permute-start.17 = (bf16[128,1024]{1,0:T(8,128)(2,1)S(1)}, bf16[128,1024]{1,0:T(8,128)(2,1)S(1)}, u32[]{:S(2)}, u32[]{:S(2)}) collective-permute-start(bf16[128,1024]{1,0:T(8,128)(2,1)S(1)} %pad_maximum_fusion.2.piece0), channel_id=1, source_target_pairs={{0,48},{4,52},{8,56},{12,60},{16,0},{20,4},{24,8},{28,12},{32,16},... | collective-permute-start | bytes 786440 | tf_op jit(solution)/shard_map/ppermute | solution.py:457
  72.4 2.7 %collective-permute-start.14 = (bf16[128,1024]{1,0:T(8,128)(2,1)S(1)}, bf16[128,1024]{1,0:T(8,128)(2,1)S(1)}, u32[]{:S(2)}, u32[]{:S(2)}) collective-permute-start(bf16[128,1024]{1,0:T(8,128)(2,1)S(1)} %pad_maximum_fusion.piece0), channel_id=1, source_target_pairs={{0,12},{4,0},{8,4},{12,8},{16,28},{20,16},{24,20},{28,24},{32,44},... | collective-permute-start | bytes 786440 | tf_op jit(solution)/shard_map/ppermute | solution.py:457
  75.0 5.8 %front.5 = (bf16[4,512,1024]{2,1,0:T(8,128)(2,1)S(1)}, bf16[512,1024]{1,0:T(8,128)(2,1)S(1)}, bf16[512,256]{1,0:T(8,128)(2,1)S(1)}, bf16[512,1024]{1,0:T(8,128)(...) custom-call(s32[3]{0:T(128)S(1)} %pad_add_fusion.where_ref, bf16[128,1024]{1,0:T(8,128)(2,1)S(1)} %pad_maximum_fusion.1.piece0, ...), custom_call_target="tpu_custom_call" | custom-call | flops 6700000256 | bytes 12000000 | tf_op jit(solution)/shard_map/front/pallas_call | solution.py:178
  80.9 0.6 collective-permute-start.15
  81.4 5.8 %front.7 = (bf16[4,512,1024]{2,1,0:T(8,128)(2,1)S(1)}, bf16[512,1024]{1,0:T(8,128)(2,1)S(1)}, bf16[512,256]{1,0:T(8,128)(2,1)S(1)}, bf16[512,1024]{1,0:T(8,128)(...) custom-call(s32[3]{0:T(128)S(1)} %pad_add_fusion.where_ref, bf16[128,1024]{1,0:T(8,128)(2,1)S(1)} %pad_maximum_fusion.2.piece0, ...), custom_call_target="tpu_custom_call" | custom-call | flops 6700000256 | bytes 12000000 | tf_op jit(solution)/shard_map/front/pallas_call | solution.py:178
  87.3 1.9 %collective-permute-done.15.piece3 = bf16[128,1024]{1,0:T(8,128)(2,1)S(1)} collective-permute-done((bf16[128,1024]{1,0:T(8,128)(2,1)S(1)}, bf16[128,1024]{1,0:T(8,128)(2,1)S(1)}, u32[]{:S(2)}, u32[]{:S(2)}) %collective-permute-start.15) | collective-permute-done | bytes 262176 | tf_op jit(solution)/shard_map/ppermute | solution.py:458
  89.2 5.8 %front.6 = (bf16[4,512,1024]{2,1,0:T(8,128)(2,1)S(1)}, bf16[512,1024]{1,0:T(8,128)(2,1)S(1)}, bf16[512,256]{1,0:T(8,128)(2,1)S(1)}, bf16[512,1024]{1,0:T(8,128)(...) custom-call(s32[3]{0:T(128)S(1)} %pad_add_fusion.where_ref, bf16[128,1024]{1,0:T(8,128)(2,1)S(1)} %pad_maximum_fusion.piece0, ...), custom_call_target="tpu_custom_call" | custom-call | flops 6700000256 | bytes 12000000 | tf_op jit(solution)/shard_map/front/pallas_call | solution.py:178
  95.0 1.1 fusion.28
  96.2 9.6 %collective-permute-start.28 = (f32[8,2816]{1,0:T(8,128)S(1)}, f32[8,2816]{1,0:T(8,128)S(1)}, u32[]{:S(2)}, u32[]{:S(2)}) collective-permute-start(f32[8,2816]{1,0:T(8,128)S(1)} %pad.22), channel_id=1, source_target_pairs={{0,1},{1,0},{2,3},{3,2},{4,5},{5,4},{6,7},{7,6},{8,9},{9,8},{10,11... | collective-permute-start | bytes 270344 | tf_op jit(solution)/shard_map/ppermute | solution.py:464
  105.7 0.8 collective-permute-start.29
  106.5 1.0 collective-permute-start.30
  107.4 1.5 products.3
  109.2 3.1 %products.4 = bf16[2,256,1024]{2,1,0:T(8,128)(2,1)S(1)} custom-call(bf16[512,1024]{1,0:T(8,128)(2,1)S(1)} %get-tuple-element.130.refs_0_.dz_ref, bf16[512,1024]{1,0:T(8,128)(2,1)S(1)} %get-tuple-element.139.refs_1_.dz_ref, bf16[512,1024]{1,0:T(8,128)(2,1)S(1)} %get-tuple-element.140.refs_2_.dz_ref, bf16[512,1024]{1,0:T(8,128)(2,1)S(1)} %get-tuple-element.148.refs_3_.dz_ref, ...), custom_call_target="tpu_custom_call" | custom-call | flops 4400000000 | bytes 10000000 | tf_op jit(solution)/shard_map/products/pallas_call | solution.py:264
  112.5 0.4 collective-permute-start.20
  113.0 0.7 collective-permute-start.22
  113.7 3.1 %products.5 = bf16[2,256,1024]{2,1,0:T(8,128)(2,1)S(1)} custom-call(bf16[512,1024]{1,0:T(8,128)(2,1)S(1)} %get-tuple-element.130.refs_0_.dz_ref, bf16[512,1024]{1,0:T(8,128)(2,1)S(1)} %get-tuple-element.139.refs_1_.dz_ref, bf16[512,1024]{1,0:T(8,128)(2,1)S(1)} %get-tuple-element.140.refs_2_.dz_ref, bf16[512,1024]{1,0:T(8,128)(2,1)S(1)} %get-tuple-element.148.refs_3_.dz_ref, ...), custom_call_target="tpu_custom_call" | custom-call | flops 4400000000 | bytes 10000000 | tf_op jit(solution)/shard_map/products/pallas_call | solution.py:264
  117.0 0.7 collective-permute-start.21
  117.7 2.8 %collective-permute-done.22 = bf16[1,128,1024]{2,1,0:T(8,128)(2,1)S(1)} collective-permute-done((bf16[1,128,1024]{2,1,0:T(8,128)(2,1)S(1)}, bf16[1,128,1024]{2,1,0:T(8,128)(2,1)S(1)}, u32[]{:S(2)}, u32[]{:S(2)}) %collective-permute-start.22) | collective-permute-done | bytes 262176 | tf_op jit(solution)/shard_map/ppermute | solution.py:483
  120.6 0.8 collective-permute-start.24
  121.4 3.8 %taps.4 = f32[32,1024]{1,0:T(8,128)S(1)} custom-call(bf16[4,512,1024]{2,1,0:T(8,128)(2,1)S(1)} %get-tuple-element.120.refs_4_.maps_ref, bf16[512,1024]{1,0:T(8,128)(2,1)S(1)} %get-tuple-element.130.refs_0_.dz_ref, bf16[3,256,1024]{2,1,0:T(8,128)(2,1)S(1)} %convert_bitcast_fusion.w_point), custom_call_target="tpu_custom_call" | custom-call | flops 4499999744 | bytes 4000000 | tf_op jit(solution)/shard_map/taps/pallas_call | solution.py:223
  125.5 3.9 %taps.7 = f32[32,1024]{1,0:T(8,128)S(1)} custom-call(bf16[4,512,1024]{2,1,0:T(8,128)(2,1)S(1)} %get-tuple-element.123.refs_7_.maps_ref, bf16[512,1024]{1,0:T(8,128)(2,1)S(1)} %get-tuple-element.148.refs_3_.dz_ref, bf16[3,256,1024]{2,1,0:T(8,128)(2,1)S(1)} %convert_bitcast_fusion.w_point), custom_call_target="tpu_custom_call" | custom-call | flops 4499999744 | bytes 4000000 | tf_op jit(solution)/shard_map/taps/pallas_call | solution.py:223
  129.4 3.9 %taps.5 = f32[32,1024]{1,0:T(8,128)S(1)} custom-call(bf16[4,512,1024]{2,1,0:T(8,128)(2,1)S(1)} %get-tuple-element.121.refs_5_.maps_ref, bf16[512,1024]{1,0:T(8,128)(2,1)S(1)} %get-tuple-element.139.refs_1_.dz_ref, bf16[3,256,1024]{2,1,0:T(8,128)(2,1)S(1)} %convert_bitcast_fusion.w_point), custom_call_target="tpu_custom_call" | custom-call | flops 4499999744 | bytes 4000000 | tf_op jit(solution)/shard_map/taps/pallas_call | solution.py:223
  133.2 3.9 %taps.6 = f32[32,1024]{1,0:T(8,128)S(1)} custom-call(bf16[4,512,1024]{2,1,0:T(8,128)(2,1)S(1)} %get-tuple-element.122.refs_6_.maps_ref, bf16[512,1024]{1,0:T(8,128)(2,1)S(1)} %get-tuple-element.140.refs_2_.dz_ref, bf16[3,256,1024]{2,1,0:T(8,128)(2,1)S(1)} %convert_bitcast_fusion.w_point), custom_call_target="tpu_custom_call" | custom-call | flops 4499999744 | bytes 4000000 | tf_op jit(solution)/shard_map/taps/pallas_call | solution.py:223
  137.4 0.7 maximum_maximum_fusion
  138.1 1.4 collective-permute-start.31
  139.5 0.7 collective-permute-start.32
  140.3 0.9 collective-permute-start.33
  141.2 0.7 collective-permute-start.26
  141.9 0.5 collective-permute-start.25
  142.5 15.1 %collective-permute-done.26 = bf16[2,128,1024]{2,1,0:T(8,128)(2,1)S(1)} collective-permute-done((bf16[2,128,1024]{2,1,0:T(8,128)(2,1)S(1)}, bf16[2,128,1024]{2,1,0:T(8,128)(2,1)S(1)}, u32[]{:S(2)}, u32[]{:S(2)}) %collective-permute-start.26) | collective-permute-done | bytes 524320 | tf_op jit(solution)/shard_map/ppermute | solution.py:483
  157.7 0.9 collective-permute-start.27
  158.9 0.7 pad.23.clone
  159.6 0.7 add_add_fusion.small
  160.7 0.8 copy-done.8
  161.6 10.4 %update.1 = (f32[1,256,1024]{2,1,0:T(8,128)}, f32[1,3,256,1024]{3,2,1,0:T(8,128)}, f32[1,256,2048]{2,1,0:T(8,128)}, f32[1,256,1280]{2,1,0:T(8,128)}, f32[27,1,10...) custom-call(s32[1]{0:T(128)} %bitcast.core_ref, ...), custom_call_target="tpu_custom_call" | custom-call | flops 4000000 | bytes 20000000 | tf_op jit(solution)/shard_map/update/pallas_call | solution.py:410
  (136 shorter events, 4.4 us)
Async XLA Ops:
  0.6 13.7 %copy-start.13 = (s32[4]{0:T(128)S(1)}, s32[4]{0:T(128)}, u32[]{:S(2)}) copy-start(s32[4]{0:T(128)} %param.17) | copy-start | bytes 52
  0.7 19.6 %copy-start.10 = (bf16[1,1,2048,128]{3,2,1,0:T(8,128)(2,1)S(1)}, bf16[1,1,2048,128]{3,2,1,0:T(8,128)(2,1)}, u32[]{:S(2)}) copy-start(bf16[1,1,2048,128]{3,2,1,0:T(8,128)(2,1)} %param.15) | copy-start | bytes 1572868
  3.0 28.2 %all-to-all-start = ((bf16[32,16,1024]{2,1,0:T(8,128)(2,1)}), bf16[32,16,1024]{2,1,0:T(8,128)(2,1)}, u32[]{:S(2)}, u32[]{:S(2)}) async-start(bf16[32,16,1024]{2,1,0:T(8,128)(2,1)} %bitcast.9), calls=%async_computation | async-start | bytes 2097152 | tf_op jit(solution)/shard_map/all_to_all | solution.py:525
  20.5 2.2 %copy-start.2 = (f32[1,256,1024]{2,1,0:T(8,128)S(1)}, f32[1,256,1024]{2,1,0:T(8,128)}, u32[]{:S(2)}) copy-start(f32[1,256,1024]{2,1,0:T(8,128)} %w_plain.1) | copy-start | bytes 3145732
  20.5 2.3 %copy-start.15 = (f32[1,19]{1,0:T(1,128)S(1)}, f32[1,19]{1,0:T(1,128)}, u32[]{:S(2)}) copy-start(f32[1,19]{1,0:T(1,128)} %b_class.1) | copy-start | bytes 232
  22.8 6.3 %copy-start.1 = (f32[1,256,1280]{2,1,0:T(8,128)S(1)}, f32[1,256,1280]{2,1,0:T(8,128)}, u32[]{:S(2)}) copy-start(f32[1,256,1280]{2,1,0:T(8,128)} %w_proj.1) | copy-start | bytes 3932164
  29.1 4.6 %copy-start.12 = (f32[1,5,256]{2,0,1:T(1,128)S(1)}, f32[1,5,256]{2,0,1:T(1,128)}, u32[]{:S(2)}) copy-start(f32[1,5,256]{2,0,1:T(1,128)} %param.23) | copy-start | bytes 15364
  29.1 5.7 %copy-start.11 = (f32[1,19,256]{2,0,1:T(1,128)S(1)}, f32[1,19,256]{2,0,1:T(1,128)}, u32[]{:S(2)}) copy-start(f32[1,19,256]{2,0,1:T(1,128)} %param.26) | copy-start | bytes 58372
  32.1 5.6 %collective-permute-start = (bf16[72,1024]{1,0:T(8,128)(2,1)S(1)}, bf16[72,1024]{1,0:T(8,128)(2,1)S(1)}, u32[]{:S(2)}, u32[]{:S(2)}) collective-permute-start(bf16[72,1024]{1,0:T(8,128)(2,1)S(1)} %pad_maximum_fusion.5), channel_id=1, source_target_pairs={{0,64},{4,68},{8,72},{12,76},{16,80},{20,84},{24,88},{28,92},{32,9... | collective-permute-start | bytes 442376 | tf_op jit(solution)/shard_map/ppermute | solution.py:532
  37.7 6.8 %collective-permute-start.7 = (bf16[64,1024]{1,0:T(8,128)(2,1)S(1)}, bf16[64,1024]{1,0:T(8,128)(2,1)S(1)}, u32[]{:S(2)}, u32[]{:S(2)}) collective-permute-start(bf16[64,1024]{1,0:T(8,128)(2,1)S(1)} %bitcast.82), channel_id=1, source_target_pairs={{0,4},{4,8},{8,12},{12,0},{16,20},{20,24},{24,28},{28,16},{32,36},... | collective-permute-start | bytes 393224 | tf_op jit(solution)/shard_map/ppermute | solution.py:456
  38.2 7.1 %collective-permute-start.8 = (bf16[64,1024]{1,0:T(8,128)(2,1)S(1)}, bf16[64,1024]{1,0:T(8,128)(2,1)S(1)}, u32[]{:S(2)}, u32[]{:S(2)}) collective-permute-start(bf16[64,1024]{1,0:T(8,128)(2,1)S(1)} %bitcast.83), channel_id=1, source_target_pairs={{0,12},{4,0},{8,4},{12,8},{16,28},{20,16},{24,20},{28,24},{32,44},... | collective-permute-start | bytes 393224 | tf_op jit(solution)/shard_map/ppermute | solution.py:457
  40.5 6.5 %collective-permute-start.9 = (bf16[64,1024]{1,0:T(8,128)(2,1)S(1)}, bf16[64,1024]{1,0:T(8,128)(2,1)S(1)}, u32[]{:S(2)}, u32[]{:S(2)}) collective-permute-start(bf16[64,1024]{1,0:T(8,128)(2,1)S(1)} %bitcast.84), channel_id=1, source_target_pairs={{0,8},{4,12},{8,0},{12,4},{16,24},{20,28},{24,16},{28,20},{32,40},... | collective-permute-start | bytes 393224 | tf_op jit(solution)/shard_map/ppermute | solution.py:458
  41.6 20.5 %copy-start.3 = (bf16[256,2048]{1,0:T(8,128)(2,1)S(1)}, bf16[256,2048]{1,0:T(8,128)(2,1)}, u32[]{:S(2)}) copy-start(bf16[256,2048]{1,0:T(8,128)(2,1)} %convert_bitcast_fusion.1) | copy-start | bytes 3145732
  41.7 5.6 %collective-permute-start.1 = (bf16[72,1024]{1,0:T(8,128)(2,1)S(1)}, bf16[72,1024]{1,0:T(8,128)(2,1)S(1)}, u32[]{:S(2)}, u32[]{:S(2)}) collective-permute-start(bf16[72,1024]{1,0:T(8,128)(2,1)S(1)} %pad_maximum_fusion.6), channel_id=1, source_target_pairs={{0,16},{4,20},{8,24},{12,28},{16,32},{20,36},{24,40},{28,44},{32,4... | collective-permute-start | bytes 442376 | tf_op jit(solution)/shard_map/ppermute | solution.py:456
  42.1 6.0 %collective-permute-start.2 = (bf16[72,1024]{1,0:T(8,128)(2,1)S(1)}, bf16[72,1024]{1,0:T(8,128)(2,1)S(1)}, u32[]{:S(2)}, u32[]{:S(2)}) collective-permute-start(bf16[72,1024]{1,0:T(8,128)(2,1)S(1)} %pad_maximum_fusion.6), channel_id=1, source_target_pairs={{0,48},{4,52},{8,56},{12,60},{16,0},{20,4},{24,8},{28,12},{32,16},... | collective-permute-start | bytes 442376 | tf_op jit(solution)/shard_map/ppermute | solution.py:457
  44.5 17.9 %slice-start = ((f32[1,5,256]{2,0,1:T(1,128)}), f32[1,1,256]{2,0,1:T(1,128)S(1)}, s32[]{:S(2)}) async-start(f32[1,5,256]{2,0,1:T(1,128)} %param.23), calls=%async_computation.1 | async-start | bytes 2048 | tf_op jit(solution)/shard_map/slice | solution.py:570
  44.5 6.5 %collective-permute-start.3 = (bf16[72,1024]{1,0:T(8,128)(2,1)S(1)}, bf16[72,1024]{1,0:T(8,128)(2,1)S(1)}, u32[]{:S(2)}, u32[]{:S(2)}) collective-permute-start(bf16[72,1024]{1,0:T(8,128)(2,1)S(1)} %pad_maximum_fusion.6), channel_id=1, source_target_pairs={{0,32},{4,36},{8,40},{12,44},{16,48},{20,52},{24,56},{28,60},{32,0... | collective-permute-start | bytes 442376 | tf_op jit(solution)/shard_map/ppermute | solution.py:458
  45.2 17.4 %copy-start.14 = (f32[1,256]{1,0:T(1,128)S(1)}, f32[1,256]{1,0:T(1,128)}, u32[]{:S(2)}) copy-start(f32[1,256]{1,0:T(1,128)} %b_proj.1) | copy-start | bytes 3076
  45.3 18.4 %copy-start = (f32[1,3,9,1024]{3,0,2,1:T(1,128)S(1)}, f32[1,3,9,1024]{3,0,2,1:T(1,128)}, u32[]{:S(2)}) copy-start(f32[1,3,9,1024]{3,0,2,1:T(1,128)} %param.20) | copy-start | bytes 331780
  51.0 6.7 %collective-permute-start.4 = (bf16[136,1024]{1,0:T(8,128)(2,1)S(1)}, bf16[136,1024]{1,0:T(8,128)(2,1)S(1)}, u32[]{:S(2)}, u32[]{:S(2)}) collective-permute-start(bf16[136,1024]{1,0:T(8,128)(2,1)S(1)} %get-tuple-element.88.piece0), channel_id=1, source_target_pairs={{0,4},{4,8},{8,12},{12,0},{16,20},{20,24},{24,28},{28,16},{32,36},... | collective-permute-start | bytes 835592 | tf_op jit(solution)/shard_map/ppermute | solution.py:456
  51.1 9.4 %collective-permute-start.5 = (bf16[136,1024]{1,0:T(8,128)(2,1)S(1)}, bf16[136,1024]{1,0:T(8,128)(2,1)S(1)}, u32[]{:S(2)}, u32[]{:S(2)}) collective-permute-start(bf16[136,1024]{1,0:T(8,128)(2,1)S(1)} %get-tuple-element.88.piece0), channel_id=1, source_target_pairs={{0,12},{4,0},{8,4},{12,8},{16,28},{20,16},{24,20},{28,24},{32,44},... | collective-permute-start | bytes 835592 | tf_op jit(solution)/shard_map/ppermute | solution.py:457
  53.8 8.3 %collective-permute-start.6 = (bf16[136,1024]{1,0:T(8,128)(2,1)S(1)}, bf16[136,1024]{1,0:T(8,128)(2,1)S(1)}, u32[]{:S(2)}, u32[]{:S(2)}) collective-permute-start(bf16[136,1024]{1,0:T(8,128)(2,1)S(1)} %get-tuple-element.88.piece0), channel_id=1, source_target_pairs={{0,8},{4,12},{8,0},{12,4},{16,24},{20,28},{24,16},{28,20},{32,40},... | collective-permute-start | bytes 835592 | tf_op jit(solution)/shard_map/ppermute | solution.py:458
  53.8 15.8 %collective-permute-start.10 = (bf16[128,1024]{1,0:T(8,128)(2,1)S(1)}, bf16[128,1024]{1,0:T(8,128)(2,1)S(1)}, u32[]{:S(2)}, u32[]{:S(2)}) collective-permute-start(bf16[128,1024]{1,0:T(8,128)(2,1)S(1)} %pad_maximum_fusion.1.piece0), channel_id=1, source_target_pairs={{0,16},{4,20},{8,24},{12,28},{16,32},{20,36},{24,40},{28,44},{32,4... | collective-permute-start | bytes 786440 | tf_op jit(solution)/shard_map/ppermute | solution.py:456
  53.9 15.7 %collective-permute-start.11 = (bf16[128,1024]{1,0:T(8,128)(2,1)S(1)}, bf16[128,1024]{1,0:T(8,128)(2,1)S(1)}, u32[]{:S(2)}, u32[]{:S(2)}) collective-permute-start(bf16[128,1024]{1,0:T(8,128)(2,1)S(1)} %pad_maximum_fusion.1.piece0), channel_id=1, source_target_pairs={{0,48},{4,52},{8,56},{12,60},{16,0},{20,4},{24,8},{28,12},{32,16},... | collective-permute-start | bytes 786440 | tf_op jit(solution)/shard_map/ppermute | solution.py:457
  57.7 11.9 %collective-permute-start.12 = (bf16[128,1024]{1,0:T(8,128)(2,1)S(1)}, bf16[128,1024]{1,0:T(8,128)(2,1)S(1)}, u32[]{:S(2)}, u32[]{:S(2)}) collective-permute-start(bf16[128,1024]{1,0:T(8,128)(2,1)S(1)} %pad_maximum_fusion.1.piece0), channel_id=1, source_target_pairs={{0,32},{4,36},{8,40},{12,44},{16,48},{20,52},{24,56},{28,60},{32,0... | collective-permute-start | bytes 786440 | tf_op jit(solution)/shard_map/ppermute | solution.py:458
  69.6 11.3 %collective-permute-start.16 = (bf16[128,1024]{1,0:T(8,128)(2,1)S(1)}, bf16[128,1024]{1,0:T(8,128)(2,1)S(1)}, u32[]{:S(2)}, u32[]{:S(2)}) collective-permute-start(bf16[128,1024]{1,0:T(8,128)(2,1)S(1)} %pad_maximum_fusion.2.piece0), channel_id=1, source_target_pairs={{0,16},{4,20},{8,24},{12,28},{16,32},{20,36},{24,40},{28,44},{32,4... | collective-permute-start | bytes 786440 | tf_op jit(solution)/shard_map/ppermute | solution.py:456
  69.7 11.8 %collective-permute-start.17 = (bf16[128,1024]{1,0:T(8,128)(2,1)S(1)}, bf16[128,1024]{1,0:T(8,128)(2,1)S(1)}, u32[]{:S(2)}, u32[]{:S(2)}) collective-permute-start(bf16[128,1024]{1,0:T(8,128)(2,1)S(1)} %pad_maximum_fusion.2.piece0), channel_id=1, source_target_pairs={{0,48},{4,52},{8,56},{12,60},{16,0},{20,4},{24,8},{28,12},{32,16},... | collective-permute-start | bytes 786440 | tf_op jit(solution)/shard_map/ppermute | solution.py:457
  72.3 9.1 %collective-permute-start.18 = (bf16[128,1024]{1,0:T(8,128)(2,1)S(1)}, bf16[128,1024]{1,0:T(8,128)(2,1)S(1)}, u32[]{:S(2)}, u32[]{:S(2)}) collective-permute-start(bf16[128,1024]{1,0:T(8,128)(2,1)S(1)} %pad_maximum_fusion.2.piece0), channel_id=1, source_target_pairs={{0,32},{4,36},{8,40},{12,44},{16,48},{20,52},{24,56},{28,60},{32,0... | collective-permute-start | bytes 786440 | tf_op jit(solution)/shard_map/ppermute | solution.py:458
  72.4 14.9 %collective-permute-start.13 = (bf16[128,1024]{1,0:T(8,128)(2,1)S(1)}, bf16[128,1024]{1,0:T(8,128)(2,1)S(1)}, u32[]{:S(2)}, u32[]{:S(2)}) collective-permute-start(bf16[128,1024]{1,0:T(8,128)(2,1)S(1)} %pad_maximum_fusion.piece0), channel_id=1, source_target_pairs={{0,4},{4,8},{8,12},{12,0},{16,20},{20,24},{24,28},{28,16},{32,36},... | collective-permute-start | bytes 786440 | tf_op jit(solution)/shard_map/ppermute | solution.py:456
  72.4 14.9 %collective-permute-start.14 = (bf16[128,1024]{1,0:T(8,128)(2,1)S(1)}, bf16[128,1024]{1,0:T(8,128)(2,1)S(1)}, u32[]{:S(2)}, u32[]{:S(2)}) collective-permute-start(bf16[128,1024]{1,0:T(8,128)(2,1)S(1)} %pad_maximum_fusion.piece0), channel_id=1, source_target_pairs={{0,12},{4,0},{8,4},{12,8},{16,28},{20,16},{24,20},{28,24},{32,44},... | collective-permute-start | bytes 786440 | tf_op jit(solution)/shard_map/ppermute | solution.py:457
  80.9 8.3 %collective-permute-start.15 = (bf16[128,1024]{1,0:T(8,128)(2,1)S(1)}, bf16[128,1024]{1,0:T(8,128)(2,1)S(1)}, u32[]{:S(2)}, u32[]{:S(2)}) collective-permute-start(bf16[128,1024]{1,0:T(8,128)(2,1)S(1)} %pad_maximum_fusion.piece0), channel_id=1, source_target_pairs={{0,8},{4,12},{8,0},{12,4},{16,24},{20,28},{24,16},{28,20},{32,40},... | collective-permute-start | bytes 786440 | tf_op jit(solution)/shard_map/ppermute | solution.py:458
  96.2 41.2 %collective-permute-start.28 = (f32[8,2816]{1,0:T(8,128)S(1)}, f32[8,2816]{1,0:T(8,128)S(1)}, u32[]{:S(2)}, u32[]{:S(2)}) collective-permute-start(f32[8,2816]{1,0:T(8,128)S(1)} %pad.22), channel_id=1, source_target_pairs={{0,1},{1,0},{2,3},{3,2},{4,5},{5,4},{6,7},{7,6},{8,9},{9,8},{10,11... | collective-permute-start | bytes 270344 | tf_op jit(solution)/shard_map/ppermute | solution.py:464
  105.7 31.7 %collective-permute-start.29 = (f32[8,2816]{1,0:T(8,128)S(1)}, f32[8,2816]{1,0:T(8,128)S(1)}, u32[]{:S(2)}, u32[]{:S(2)}) collective-permute-start(f32[8,2816]{1,0:T(8,128)S(1)} %pad.22), channel_id=1, source_target_pairs={{0,2},{1,3},{2,0},{3,1},{4,6},{5,7},{6,4},{7,5},{8,10},{9,11},{10,... | collective-permute-start | bytes 270344 | tf_op jit(solution)/shard_map/ppermute | solution.py:464
  106.5 30.9 %collective-permute-start.30 = (f32[8,2816]{1,0:T(8,128)S(1)}, f32[8,2816]{1,0:T(8,128)S(1)}, u32[]{:S(2)}, u32[]{:S(2)}) collective-permute-start(f32[8,2816]{1,0:T(8,128)S(1)} %pad.22), channel_id=1, source_target_pairs={{0,3},{1,2},{2,1},{3,0},{4,7},{5,6},{6,5},{7,4},{8,11},{9,10},{10,... | collective-permute-start | bytes 270344 | tf_op jit(solution)/shard_map/ppermute | solution.py:464
  109.0 3.4 %collective-permute-start.19 = (bf16[1,128,1024]{2,1,0:T(8,128)(2,1)S(1)}, bf16[1,128,1024]{2,1,0:T(8,128)(2,1)S(1)}, u32[]{:S(2)}, u32[]{:S(2)}) collective-permute-start(bf16[1,128,1024]{2,1,0:T(8,128)(2,1)S(1)} %constant_dynamic-slice_fusion.2), channel_id=1, source_target_pairs={{0,1},{1,0},{2,3},{3,2},{4,5},{5,4},{6,7},{7,6},{8,9},{9,8},{10,11... | collective-permute-start | bytes 786440 | tf_op jit(solution)/shard_map/ppermute | solution.py:479
  112.5 4.3 %collective-permute-start.20 = (bf16[2,128,1024]{2,1,0:T(8,128)(2,1)S(1)}, bf16[2,128,1024]{2,1,0:T(8,128)(2,1)S(1)}, u32[]{:S(2)}, u32[]{:S(2)}) collective-permute-start(bf16[2,128,1024]{2,1,0:T(8,128)(2,1)S(1)} %constant_dynamic-slice_fusion.1), channel_id=1, source_target_pairs={{0,1},{1,0},{2,3},{3,2},{4,5},{5,4},{6,7},{7,6},{8,9},{9,8},{10,11... | collective-permute-start | bytes 1572872 | tf_op jit(solution)/shard_map/ppermute | solution.py:479
  113.0 7.6 %collective-permute-start.22 = (bf16[1,128,1024]{2,1,0:T(8,128)(2,1)S(1)}, bf16[1,128,1024]{2,1,0:T(8,128)(2,1)S(1)}, u32[]{:S(2)}, u32[]{:S(2)}) collective-permute-start(bf16[1,128,1024]{2,1,0:T(8,128)(2,1)S(1)} %add_convert_fusion.5), channel_id=1, source_target_pairs={{0,2},{1,3},{2,0},{3,1},{4,6},{5,7},{6,4},{7,5},{8,10},{9,11},{10,... | collective-permute-start | bytes 786440 | tf_op jit(solution)/shard_map/ppermute | solution.py:483
  117.0 8.2 %collective-permute-start.21 = (bf16[2,128,1024]{2,1,0:T(8,128)(2,1)S(1)}, bf16[2,128,1024]{2,1,0:T(8,128)(2,1)S(1)}, u32[]{:S(2)}, u32[]{:S(2)}) collective-permute-start(bf16[2,128,1024]{2,1,0:T(8,128)(2,1)S(1)} %constant_dynamic-slice_fusion), channel_id=1, source_target_pairs={{0,1},{1,0},{2,3},{3,2},{4,5},{5,4},{6,7},{7,6},{8,9},{9,8},{10,11... | collective-permute-start | bytes 1572872 | tf_op jit(solution)/shard_map/ppermute | solution.py:479
  120.6 38.0 %copy-start.7 = (bf16[1,128,1024]{2,1,0:T(8,128)(2,1)}, bf16[1,128,1024]{2,1,0:T(8,128)(2,1)S(1)}, u32[]{:S(2)}) copy-start(bf16[1,128,1024]{2,1,0:T(8,128)(2,1)S(1)} %add_convert_fusion.4.mine0) | copy-start | bytes 786436
  120.6 16.5 %collective-permute-start.24 = (bf16[2,128,1024]{2,1,0:T(8,128)(2,1)S(1)}, bf16[2,128,1024]{2,1,0:T(8,128)(2,1)S(1)}, u32[]{:S(2)}, u32[]{:S(2)}) collective-permute-start(bf16[2,128,1024]{2,1,0:T(8,128)(2,1)S(1)} %add_convert_fusion.3), channel_id=1, source_target_pairs={{0,2},{1,3},{2,0},{3,1},{4,6},{5,7},{6,4},{7,5},{8,10},{9,11},{10,... | collective-permute-start | bytes 1572872 | tf_op jit(solution)/shard_map/ppermute | solution.py:483
  137.3 21.5 %copy-start.4 = (bf16[2,128,1024]{2,1,0:T(8,128)(2,1)}, bf16[2,128,1024]{2,1,0:T(8,128)(2,1)S(1)}, u32[]{:S(2)}) copy-start(bf16[2,128,1024]{2,1,0:T(8,128)(2,1)S(1)} %add_convert_fusion.1.mine1) | copy-start | bytes 1572868
  138.1 20.5 %collective-permute-start.31 = (bf16[48,1024]{1,0:T(8,128)(2,1)}, bf16[48,1024]{1,0:T(8,128)(2,1)S(1)}, u32[]{:S(2)}, u32[]{:S(2)}) collective-permute-start(bf16[48,1024]{1,0:T(8,128)(2,1)} %maximum_maximum_fusion), channel_id=1, source_target_pairs={{0,1},{1,0},{2,3},{3,2},{4,5},{5,4},{6,7},{7,6},{8,9},{9,8},{10,11... | collective-permute-start | bytes 294920 | tf_op jit(solution)/shard_map/ppermute | solution.py:464
  139.5 20.1 %collective-permute-start.32 = (bf16[48,1024]{1,0:T(8,128)(2,1)}, bf16[48,1024]{1,0:T(8,128)(2,1)S(1)}, u32[]{:S(2)}, u32[]{:S(2)}) collective-permute-start(bf16[48,1024]{1,0:T(8,128)(2,1)} %maximum_maximum_fusion), channel_id=1, source_target_pairs={{0,2},{1,3},{2,0},{3,1},{4,6},{5,7},{6,4},{7,5},{8,10},{9,11},{10,... | collective-permute-start | bytes 294920 | tf_op jit(solution)/shard_map/ppermute | solution.py:464
  140.3 19.3 %collective-permute-start.33 = (bf16[48,1024]{1,0:T(8,128)(2,1)}, bf16[48,1024]{1,0:T(8,128)(2,1)S(1)}, u32[]{:S(2)}, u32[]{:S(2)}) collective-permute-start(bf16[48,1024]{1,0:T(8,128)(2,1)} %maximum_maximum_fusion), channel_id=1, source_target_pairs={{0,3},{1,2},{2,1},{3,0},{4,7},{5,6},{6,5},{7,4},{8,11},{9,10},{10,... | collective-permute-start | bytes 294920 | tf_op jit(solution)/shard_map/ppermute | solution.py:464
  141.2 16.3 %collective-permute-start.26 = (bf16[2,128,1024]{2,1,0:T(8,128)(2,1)S(1)}, bf16[2,128,1024]{2,1,0:T(8,128)(2,1)S(1)}, u32[]{:S(2)}, u32[]{:S(2)}) collective-permute-start(bf16[2,128,1024]{2,1,0:T(8,128)(2,1)S(1)} %add_convert_fusion.2), channel_id=1, source_target_pairs={{0,2},{1,3},{2,0},{3,1},{4,6},{5,7},{6,4},{7,5},{8,10},{9,11},{10,... | collective-permute-start | bytes 1572872 | tf_op jit(solution)/shard_map/ppermute | solution.py:483
  141.9 18.7 %collective-permute-start.25 = (bf16[2,128,1024]{2,1,0:T(8,128)(2,1)S(1)}, bf16[2,128,1024]{2,1,0:T(8,128)(2,1)S(1)}, u32[]{:S(2)}, u32[]{:S(2)}) collective-permute-start(bf16[2,128,1024]{2,1,0:T(8,128)(2,1)S(1)} %add_convert_fusion.1.mine1), channel_id=1, source_target_pairs={{0,1},{1,0},{2,3},{3,2},{4,5},{5,4},{6,7},{7,6},{8,9},{9,8},{10,11... | collective-permute-start | bytes 1572872 | tf_op jit(solution)/shard_map/ppermute | solution.py:619
  157.7 2.9 %copy-start.5 = (bf16[2,128,1024]{2,1,0:T(8,128)(2,1)}, bf16[2,128,1024]{2,1,0:T(8,128)(2,1)S(1)}, u32[]{:S(2)}) copy-start(bf16[2,128,1024]{2,1,0:T(8,128)(2,1)S(1)} %add_convert_fusion.mine2) | copy-start | bytes 1572868
  157.7 2.9 %collective-permute-start.27 = (bf16[2,128,1024]{2,1,0:T(8,128)(2,1)S(1)}, bf16[2,128,1024]{2,1,0:T(8,128)(2,1)S(1)}, u32[]{:S(2)}, u32[]{:S(2)}) collective-permute-start(bf16[2,128,1024]{2,1,0:T(8,128)(2,1)S(1)} %add_convert_fusion.mine2), channel_id=1, source_target_pairs={{0,1},{1,0},{2,3},{3,2},{4,5},{5,4},{6,7},{7,6},{8,9},{9,8},{10,11... | collective-permute-start | bytes 1572872 | tf_op jit(solution)/shard_map/ppermute | solution.py:619
  158.6 2.0 %copy-start.6 = (f32[32,2816]{1,0:T(8,128)}, f32[32,2816]{1,0:T(8,128)S(1)}, u32[]{:S(2)}) copy-start(f32[32,2816]{1,0:T(8,128)S(1)} %maximum_select_fusion.factors) | copy-start | bytes 1081348
  158.7 2.0 %collective-permute-start.23 = (bf16[1,128,1024]{2,1,0:T(8,128)(2,1)S(1)}, bf16[1,128,1024]{2,1,0:T(8,128)(2,1)}, u32[]{:S(2)}, u32[]{:S(2)}) collective-permute-start(bf16[1,128,1024]{2,1,0:T(8,128)(2,1)S(1)} %add_convert_fusion.4.mine0), channel_id=1, source_target_pairs={{0,1},{1,0},{2,3},{3,2},{4,5},{5,4},{6,7},{7,6},{8,9},{9,8},{10,11... | collective-permute-start | bytes 786440 | tf_op jit(solution)/shard_map/ppermute | solution.py:619
  160.6 0.8 copy-start.8
  160.6 1.0 copy-start.9
where the time goes:
time: 173 us; the launch traced here: 172 us
  Pallas kernels  56.7 us (33%)
  starting transfers between devices  51.7 us (30%)
  waiting for transfers between devices  33.8 us (20%)
  between operations  10.3 us (6%)
  other arithmetic  9.09 us (5%)
  local copies, waits for them, and re-layouts  7.94 us (5%)
  matrix products  2.65 us (2%)
    pallas_call x4, Pallas kernels, front(): pl.pallas_call(functools.partial(front_kernel, order), name='front', out_...  23.2 us
    ppermute x3, waiting for transfers between devices, sum_chips(): lax.ppermute(pair, 'batch', CHIPS).astype(F32)  17.9 us
    pallas_call x4, Pallas kernels, depth_taps(): pl.pallas_call(taps_kernel, name='taps', grid=(channels // block,), out_s...  15.4 us
    ppermute x6, starting transfers between devices, gather_ring(): lax.ppermute(block, 'trial', along(-1))  15.3 us
    ppermute x6, starting transfers between devices, from_batch(): lax.ppermute(mine, 'batch', [(b, b ^ other) for b in range(4)])  14.3 us
    all_to_all x1, starting transfers between devices, on_device(): lax.all_to_all(own.reshape(32, 16, channels), 'trial', 0, 0, tiled=True)  11.3 us
    pallas_call x1, Pallas kernels, update(): pl.pallas_call(update_kernel, name='update', out_shape=[jax.ShapeDtypeStr...  10.4 us
    ppermute x6, waiting for transfers between devices, gather_ring(): lax.ppermute(block, 'trial', along(2))  8.05 us
  transfers between devices with their start and end apart: 35, of which 13 were waited for; matrix products, arithmetic and copies ran while one was open for 8% of the time, Pallas kernels for 24%

commit v1 on v0

--- a/solution.py
+++ b/solution.py
@@ -1,4 +1,5 @@
 import functools
+import math
 
 import jax
 import jax.numpy as jnp
@@ -296,7 +297,6 @@
     rest1,
     mine2,
     rest2,
-    left,
     factors,
     small,
     new_plain,
@@ -309,13 +309,14 @@
     new_class,
     new_b_class,
     scale_ref,
+    slopes_ref,
+    left_ref,
 ):
     step = pl.program_id(0)
     pairs = ((mine0, rest0), (mine1, rest1), (mine2, rest2))
     count = factors.shape[0]
-    entries = sum(
-        STEPS * array[...].size for array in (w_plain, w_point, w_pool, w_proj)
-    ) + sum(array[...].size for array in (w_depth, b_branch, b_proj, w_class, b_class))
+    arrays = (w_plain, w_point, w_pool, w_proj, w_depth, b_branch, b_proj, w_class, b_class)
+    entries = sum(math.prod(array.shape) for array in arrays)
 
     def outer_squared(a, b):
         product = dot_exact_nt(a, a) * dot_exact_nt(b, b)
@@ -323,6 +324,9 @@
 
     @pl.when(step == 0)
     def _():
+        slopes_ref[...] = jnp.zeros(slopes_ref.shape, F32)
+        slopes_ref[:count, :] = factors[:, : 2 * HID]
+        left_ref[...] = slopes_ref[...].T
         total = jnp.zeros((16, small.shape[1]), F32)
         for mine, rest in pairs:
             for row in range(0, mine.shape[1], 16):
@@ -343,21 +347,24 @@
     scale = scale_ref[0:1, 0:1]
 
     def large(side):
-        rows = w_plain.shape[1]
+        rows = new_plain.shape[1]
         here = pl.ds(pl.multiple_of(lax.rem(step, STEPS // 2) * rows, rows), rows)
+        there = lax.rem(step + core_ref[0] * (STEPS // 2), STEPS)
+        start = pl.multiple_of(there * rows, rows)
+        there = pl.ds(start, rows)
         proj, low, high = (
             [pair[side][layer, here, :] for layer in range(pair[side].shape[0])] for pair in pairs
         )
         wide = proj[0].shape[-1]
-        new_plain[0] = w_plain[0] - scale * low[0].astype(F32)
-        new_point[0, 0] = w_point[0, 0] - scale * low[1].astype(F32)
-        new_point[0, 1] = w_point[0, 1] - scale * high[0].astype(F32)
-        new_point[0, 2] = w_point[0, 2] - scale * high[1].astype(F32)
-        new_proj[0, :, :wide] = w_proj[0, :, :wide] - scale * proj[0].astype(F32)
-        proj4_grad = dot_exact(left[1, :, :count], factors[:, 2 * HID : 3 * HID])
-        new_proj[0, :, wide:] = w_proj[0, :, wide:] - scale * proj4_grad
-        pool_grad = dot_exact(left[0, :, :count], factors[:, 3 * HID :])
-        new_pool[0] = w_pool[0] - scale * pool_grad
+        new_plain[0] = w_plain[0, there, :] - scale * low[0].astype(F32)
+        new_point[0, 0] = w_point[0, 0, there, :] - scale * low[1].astype(F32)
+        new_point[0, 1] = w_point[0, 1, there, :] - scale * high[0].astype(F32)
+        new_point[0, 2] = w_point[0, 2, there, :] - scale * high[1].astype(F32)
+        new_proj[0, :, :wide] = w_proj[0, there, :wide] - scale * proj[0].astype(F32)
+        proj4_grad = dot_exact(left_ref[pl.ds(HID + start, rows), :count], factors[:, 2 * HID : 3 * HID])
+        new_proj[0, :, wide:] = w_proj[0, there, wide:] - scale * proj4_grad
+        pool_grad = dot_exact(left_ref[pl.ds(start, rows), :count], factors[:, 3 * HID :])
+        new_pool[0] = w_pool[0, there, :] - scale * pool_grad
 
     @pl.when(step < STEPS // 2)
     def _():
@@ -385,9 +392,36 @@
         new_b_class[...] = b_class[...] - scale * small[35:36, :classes]
 
 
-def update(core, rate, params, halves, left, factors, small):
+def fetch_kernel(*refs):
+    count = len(refs) // 3
+    copies = [
+        pltpu.make_async_copy(source, target, done)
+        for source, target, done in zip(refs[:count], refs[count : 2 * count], refs[2 * count :])
+    ]
+    for copy in copies:
+        copy.start()
+    for copy in copies:
+        copy.wait()
+
+
+def fetch(arrays):
+    return pl.pallas_call(
+        fetch_kernel,
+        name="fetch",
+        out_shape=[pltpu.VMEM(array.shape, array.dtype) for array in arrays],
+        in_specs=[pl.BlockSpec(memory_space=pl.ANY)] * len(arrays),
+        out_specs=[VMEM] * len(arrays),
+        scratch_shapes=[pltpu.SemaphoreType.DMA] * len(arrays),
+        compiler_params=pltpu.CompilerParams(vmem_limit_bytes=2**20),
+        cost_estimate=pl.CostEstimate(
+            flops=3_500_000_000, bytes_accessed=8_000_000, transcendentals=0
+        ),
+    )(*arrays)
+
+
+def update(core, rate, params, large, halves, factors, small):
     w_plain, w_depth, w_point, w_pool, b_branch, w_proj, b_proj, w_class, b_class = params
-    inputs = (w_plain, w_point, w_pool, w_proj) + tuple(
+    inputs = tuple(large) + tuple(
         array if array.ndim == 2 else array.reshape(-1, 1, array.shape[-1])
         for array in (w_depth, b_branch, b_proj, w_class, b_class)
     )
@@ -406,7 +440,8 @@
     def whole(shape):
         return pl.BlockSpec(shape, lambda j, core: (0,) * len(shape))
 
-    specs = [by_rows(array.shape) for array in inputs[:4]] + [whole(array.shape) for array in inputs[4:]]
+    small_specs = [whole(array.shape) for array in inputs[4:]]
+    specs = [by_rows(array.shape) for array in inputs[:4]] + small_specs
     new = pl.pallas_call(
         update_kernel,
         name="update",
@@ -415,17 +450,22 @@
             num_scalar_prefetch=1,
             grid=(STEPS,),
             in_specs=[SMEM]
-            + specs
+            + [VMEM] * 4
+            + small_specs
             + [VMEM] * (2 * len(halves))
-            + [pl.BlockSpec((2, rows, LANES), lambda j, core: (0, where(j, core), 0)), VMEM, VMEM],
+            + [VMEM, VMEM],
             out_specs=specs,
-            scratch_shapes=[pltpu.VMEM((8, LANES), F32)],
+            scratch_shapes=[
+                pltpu.VMEM((8, LANES), F32),
+                pltpu.VMEM((LANES, 2 * HID), F32),
+                pltpu.VMEM((2 * HID, LANES), F32),
+            ],
         ),
-        compiler_params=pltpu.CompilerParams(vmem_limit_bytes=60 * 2**20),
+        compiler_params=pltpu.CompilerParams(vmem_limit_bytes=14 * 2**20),
         cost_estimate=pl.CostEstimate(
             flops=4_000_000, bytes_accessed=20_000_000, transcendentals=0
         ),
-    )(core, rate, *inputs, *(array for pair in halves for array in pair), left, factors, small)
+    )(core, rate, *inputs, *(array for pair in halves for array in pair), factors, small)
     order = (0, 4, 1, 2, 5, 3, 6, 7, 8)
     return tuple(new[i].reshape(param.shape) for i, param in zip(order, params))
 
@@ -606,23 +646,20 @@
     low_pair = sum_cores(low_part, core)
     high_part = products(dzs, stacks, 2, 2)
     proj_total = sum_chips(proj_pair)
-    dzs, high_part, low_pair = after((dzs, high_part, low_pair))
+    dzs, high_part, low_pair, factors = after((dzs, high_part, low_pair, factors))
     high_pair = sum_cores(high_part, core)
-    depth_part = depth_taps(stacks[0], dzs[0], point16)
-    dzs, depth_part, high_pair, proj_total = after((dzs, depth_part, high_pair, proj_total))
     low_total = sum_chips(low_pair)
-    for m in range(1, turns):
-        depth_part = depth_part + depth_taps(stacks[m], dzs[m], point16)
-        if m == 2:
-            low_total, depth_part = after((low_total, depth_part))
-    totals = [proj_total, low_total, sum_chips(high_pair)]
-    halves = [(total, lax.ppermute(total, "batch", CORES)) for total in totals]
-
+    taps_parts = [depth_taps(stacks[0], dzs[0], point16)]
+    dzs, taps_parts, high_pair = after((dzs, taps_parts, high_pair))
+    taps_parts.append(depth_taps(stacks[1], dzs[1], point16))
+    dzs, taps_parts, proj_total = after((dzs, taps_parts, proj_total))
+    proj_rest = lax.ppermute(proj_total, "batch", CORES)
+    taps_parts.append(depth_taps(stacks[2], dzs[2], point16))
+    dzs, taps_parts, proj_rest = after((dzs, taps_parts, proj_rest))
+    taps_parts.append(depth_taps(stacks[3], dzs[3], point16))
+    depth_part = sum(taps_parts)
     factors, depth_part = after((factors, depth_part))
     factors = in_order(factors, core, chip)
-    left = jnp.pad(factors[:, : 2 * HID].T, ((0, 0), (0, LANES - factors.shape[0])))
-    left = left.reshape(2, HID, LANES)
-
     dclass = sum(dclass)
     bias_row = jnp.pad(jnp.sum(dbranch4, axis=0)[None], ((2, 5), (0, wide - HID)))
     small = jnp.concatenate(
@@ -633,12 +670,18 @@
         ]
     )
     small = sum_batch_small(small.astype(BF16))
+    high_other = lax.ppermute(high_pair, "batch", CHIPS)
+    large, factors = after(((w_plain, w_point, w_pool, w_proj), factors))
+    high_other, low_total, large, small = after((high_other, low_total, fetch(large), small))
+    high_total = (high_pair.astype(F32) + high_other.astype(F32)).astype(BF16)
+    halves = [(proj_total, proj_rest)]
+    halves += [(total, lax.ppermute(total, "batch", CORES)) for total in (low_total, high_total)]
 
     params = (w_plain, w_depth, w_point, w_pool, b_branch, w_proj, b_proj, w_class, b_class)
 
     step_rate = 0.5 * jnp.exp2(-6.0 * lr_index[0].astype(F32) / 1073741824.0)
     return update(
-        core.reshape(1).astype(jnp.int32), step_rate.reshape(1), params, halves, left, factors, small
+        core.reshape(1).astype(jnp.int32), step_rate.reshape(1), params, large, halves, factors, small
     )
 
 

time: 173 us -> 162 us (0.936)
  waiting for transfers between devices: 33.8 us -> 21.2 us
  starting transfers between devices: 51.7 us -> 57.4 us
  Pallas kernels: 56.7 us -> 53.3 us
    ppermute x3 -> x2, waiting for transfers between devices: 17.9 us -> 2.74 us  [sum_chips(): lax.ppermute(pair, 'batch', CHIPS).astype(F32)]
    ppermute x6, waiting for transfers between devices: 0.02 us -> 7.1 us  [from_batch(): lax.ppermute(mine, 'batch', [(b, b ^ other) for b in range(4)])]
    ppermute x6, starting transfers between devices: 3.03 us -> 7.62 us  [gather_ring(): lax.ppermute(block, 'trial', along(2))]
    pallas_call x1, Pallas kernels: 10.4 us -> 6.27 us  [update(): pl.pallas_call(update_kernel, name='update', out_shape=[jax.ShapeDtypeStr...]
    ppermute x6, waiting for transfers between devices: 2.98 us -> 0.32 us  [gather_ring(): lax.ppermute(block, 'trial', along(-1))]
    ppermute x6, starting transfers between devices: 1.08 us -> 2.97 us  [gather_ring(): lax.ppermute(block, 'trial', along(1))]
    ppermute x6, starting transfers between devices: 15.3 us -> 13.4 us  [gather_ring(): lax.ppermute(block, 'trial', along(-1))]
    unnamed x36 -> x35, local copies, waits for them, and re-layouts: 3.53 us -> 2.56 us
  transfers between devices with their start and end apart: 35 -> 35, of which waited for: 13 -> 14; matrix products, arithmetic and copies ran while one was open for 8% -> 8% of each run, Pallas kernels for 24% -> 26%
where the time goes in v1:
time: 162 us; the launch traced here: 161 us
  starting transfers between devices  57.4 us (35%)
  Pallas kernels  53.3 us (33%)
  waiting for transfers between devices  21.2 us (13%)
  between operations  10.1 us (6%)
  other arithmetic  9.37 us (6%)
  local copies, waits for them, and re-layouts  7.14 us (4%)
  matrix products  2.65 us (2%)
    pallas_call x4, Pallas kernels, front(): pl.pallas_call(functools.partial(front_kernel, order), name='front', out_...  23.4 us
    pallas_call x4, Pallas kernels, depth_taps(): pl.pallas_call(taps_kernel, name='taps', grid=(channels // block,), out_s...  15.3 us
    ppermute x6, starting transfers between devices, from_batch(): lax.ppermute(mine, 'batch', [(b, b ^ other) for b in range(4)])  13.9 us
    ppermute x6, starting transfers between devices, gather_ring(): lax.ppermute(block, 'trial', along(-1))  13.4 us
    all_to_all x1, starting transfers between devices, on_device(): lax.all_to_all(own.reshape(32, 16, channels), 'trial', 0, 0, tiled=True)  11.3 us
    pallas_call x3, Pallas kernels, products(): pl.pallas_call(functools.partial(product_kernel, count, first), name='pro...  7.71 us
    ppermute x6, starting transfers between devices, gather_ring(): lax.ppermute(block, 'trial', along(2))  7.62 us
    ppermute x6, waiting for transfers between devices, from_batch(): lax.ppermute(mine, 'batch', [(b, b ^ other) for b in range(4)])  7.1 us
  transfers between devices with their start and end apart: 35, of which 14 were waited for; matrix products, arithmetic and copies ran while one was open for 8% of the time, Pallas kernels for 26%

profile of v1, /device:TPU:1, one launch (start us, length us, event | category | flops | bytes accessed | tf_op | source)
XLA Modules:
  0.0 161.2 jit_solution(8161682178727230316)
XLA Ops:
  0.7 2.4 %copy.31 = bf16[1,1,1024,512]{2,3,1,0:T(8,128)(2,1)} copy(bf16[1,1,1024,512]{3,2,1,0:T(8,128)(2,1)} %param.14) | data formatting | bytes 2097152 | tf_op args[0]
  3.1 11.3 %all-to-all-start = ((bf16[32,16,1024]{2,1,0:T(8,128)(2,1)}), bf16[32,16,1024]{2,1,0:T(8,128)(2,1)}, u32[]{:S(2)}, u32[]{:S(2)}) async-start(bf16[32,16,1024]{2,1,0:T(8,128)(2,1)} %bitcast.73), calls=%async_computation | async-start | bytes 2097152 | tf_op jit(solution)/shard_map/all_to_all | solution.py:565
  14.4 0.6 fusion.30
  20.3 1.3 convert_reduce_fusion
  21.7 1.4 convert_bitcast_fusion.w_point
  23.1 0.9 convert_bitcast_fusion.3.w_plain
  26.6 0.8 fusion.18
  27.5 2.7 %convert_bitcast_fusion.1 = bf16[256,2048]{1,0:T(8,128)(2,1)} fusion(f32[1,256,2048]{2,1,0:T(8,128)} %refs_2_), kind=kLoop, calls=%fused_computation.11 | loop fusion | flops 524288 | bytes 3145728 | tf_op jit(solution)/shard_map/convert_element_type | solution.py:606
  30.2 0.9 convert_bitcast_fusion.2
  31.3 0.8 constant_dynamic-slice_fusion.8
  32.2 0.7 pad_maximum_fusion.5
  32.9 2.4 %collective-permute-start = (bf16[72,1024]{1,0:T(8,128)(2,1)}, bf16[72,1024]{1,0:T(8,128)(2,1)S(1)}, u32[]{:S(2)}, u32[]{:S(2)}) collective-permute-start(bf16[72,1024]{1,0:T(8,128)(2,1)} %pad_maximum_fusion.5), channel_id=1, source_target_pairs={{0,64},{4,68},{8,72},{12,76},{16,80},{20,84},{24,88},{28,92},{32,9... | collective-permute-start | bytes 442376 | tf_op jit(solution)/shard_map/ppermute | solution.py:572
  35.4 1.9 %slice.251.w_proj = bf16[256,1024]{1,0:T(8,128)(2,1)} slice(bf16[256,1280]{1,0:T(8,128)(2,1)} %convert_bitcast_fusion.2), slice={[0:256], [0:1024]} | slice | bytes 1048576 | tf_op jit(solution)/shard_map/slice | solution.py:623
  37.4 1.2 collective-permute-done
  38.6 1.0 collective-permute-start.7
  39.6 1.7 %collective-permute-start.8 = (bf16[64,1024]{1,0:T(8,128)(2,1)S(1)}, bf16[64,1024]{1,0:T(8,128)(2,1)S(1)}, u32[]{:S(2)}, u32[]{:S(2)}) collective-permute-start(bf16[64,1024]{1,0:T(8,128)(2,1)S(1)} %bitcast.85), channel_id=1, source_target_pairs={{0,12},{4,0},{8,4},{12,8},{16,28},{20,16},{24,20},{28,24},{32,44},... | collective-permute-start | bytes 393224 | tf_op jit(solution)/shard_map/ppermute | solution.py:497
  41.4 1.2 collective-permute-start.9
  42.8 1.3 collective-permute-start.1
  44.0 1.5 collective-permute-start.2
  45.5 1.6 collective-permute-start.3
  47.6 0.7 collective-permute-done.1
  48.4 3.0 %collective-permute-done.3 = bf16[72,1024]{1,0:T(8,128)(2,1)S(1)} collective-permute-done((bf16[72,1024]{1,0:T(8,128)(2,1)S(1)}, bf16[72,1024]{1,0:T(8,128)(2,1)S(1)}, u32[]{:S(2)}, u32[]{:S(2)}) %collective-permute-start.3) | collective-permute-done | bytes 147488 | tf_op jit(solution)/shard_map/ppermute | solution.py:498
  51.6 2.6 %collective-permute-start.5 = (bf16[136,1024]{1,0:T(8,128)(2,1)S(1)}, bf16[136,1024]{1,0:T(8,128)(2,1)S(1)}, u32[]{:S(2)}, u32[]{:S(2)}) collective-permute-start(bf16[136,1024]{1,0:T(8,128)(2,1)S(1)} %get-tuple-element.115.piece0), channel_id=1, source_target_pairs={{0,12},{4,0},{8,4},{12,8},{16,28},{20,16},{24,20},{28,24},{32,44},... | collective-permute-start | bytes 835592 | tf_op jit(solution)/shard_map/ppermute | solution.py:497
  54.5 2.7 %collective-permute-start.11 = (bf16[128,1024]{1,0:T(8,128)(2,1)S(1)}, bf16[128,1024]{1,0:T(8,128)(2,1)S(1)}, u32[]{:S(2)}, u32[]{:S(2)}) collective-permute-start(bf16[128,1024]{1,0:T(8,128)(2,1)S(1)} %pad_maximum_fusion.1.piece0), channel_id=1, source_target_pairs={{0,48},{4,52},{8,56},{12,60},{16,0},{20,4},{24,8},{28,12},{32,16},... | collective-permute-start | bytes 786440 | tf_op jit(solution)/shard_map/ppermute | solution.py:497
  57.2 0.9 collective-permute-done.4.piece1
  58.1 2.2 %collective-permute-start.12 = (bf16[128,1024]{1,0:T(8,128)(2,1)S(1)}, bf16[128,1024]{1,0:T(8,128)(2,1)S(1)}, u32[]{:S(2)}, u32[]{:S(2)}) collective-permute-start(bf16[128,1024]{1,0:T(8,128)(2,1)S(1)} %pad_maximum_fusion.1.piece0), channel_id=1, source_target_pairs={{0,32},{4,36},{8,40},{12,44},{16,48},{20,52},{24,56},{28,60},{32,0... | collective-permute-start | bytes 786440 | tf_op jit(solution)/shard_map/ppermute | solution.py:498
  60.7 1.4 collective-permute-done.6.piece3
  62.6 1.1 convolution_add_fusion
  63.7 5.9 %front.4 = (bf16[4,512,1024]{2,1,0:T(8,128)(2,1)S(1)}, bf16[512,1024]{1,0:T(8,128)(2,1)S(1)}, bf16[512,256]{1,0:T(8,128)(2,1)S(1)}, bf16[512,1024]{1,0:T(8,128)(...) custom-call(s32[3]{0:T(128)S(1)} %pad_add_fusion.where_ref, bf16[136,1024]{1,0:T(8,128)(2,1)S(1)} %get-tuple-element.115.piece0, ...), custom_call_target="tpu_custom_call" | custom-call | flops 6700000256 | bytes 12000000 | tf_op jit(solution)/shard_map/front/pallas_call | solution.py:179
  70.1 2.3 %collective-permute-start.17 = (bf16[128,1024]{1,0:T(8,128)(2,1)S(1)}, bf16[128,1024]{1,0:T(8,128)(2,1)S(1)}, u32[]{:S(2)}, u32[]{:S(2)}) collective-permute-start(bf16[128,1024]{1,0:T(8,128)(2,1)S(1)} %pad_maximum_fusion.2.piece0), channel_id=1, source_target_pairs={{0,48},{4,52},{8,56},{12,60},{16,0},{20,4},{24,8},{28,12},{32,16},... | collective-permute-start | bytes 786440 | tf_op jit(solution)/shard_map/ppermute | solution.py:497
  72.4 2.3 %collective-permute-start.18 = (bf16[128,1024]{1,0:T(8,128)(2,1)S(1)}, bf16[128,1024]{1,0:T(8,128)(2,1)S(1)}, u32[]{:S(2)}, u32[]{:S(2)}) collective-permute-start(bf16[128,1024]{1,0:T(8,128)(2,1)S(1)} %pad_maximum_fusion.2.piece0), channel_id=1, source_target_pairs={{0,32},{4,36},{8,40},{12,44},{16,48},{20,52},{24,56},{28,60},{32,0... | collective-permute-start | bytes 786440 | tf_op jit(solution)/shard_map/ppermute | solution.py:498
  74.7 2.7 %collective-permute-start.14 = (bf16[128,1024]{1,0:T(8,128)(2,1)S(1)}, bf16[128,1024]{1,0:T(8,128)(2,1)S(1)}, u32[]{:S(2)}, u32[]{:S(2)}) collective-permute-start(bf16[128,1024]{1,0:T(8,128)(2,1)S(1)} %pad_maximum_fusion.piece0), channel_id=1, source_target_pairs={{0,12},{4,0},{8,4},{12,8},{16,28},{20,16},{24,20},{28,24},{32,44},... | collective-permute-start | bytes 786440 | tf_op jit(solution)/shard_map/ppermute | solution.py:497
  77.3 5.8 %front.5 = (bf16[4,512,1024]{2,1,0:T(8,128)(2,1)S(1)}, bf16[512,1024]{1,0:T(8,128)(2,1)S(1)}, bf16[512,256]{1,0:T(8,128)(2,1)S(1)}, bf16[512,1024]{1,0:T(8,128)(...) custom-call(s32[3]{0:T(128)S(1)} %pad_add_fusion.where_ref, bf16[128,1024]{1,0:T(8,128)(2,1)S(1)} %pad_maximum_fusion.1.piece0, ...), custom_call_target="tpu_custom_call" | custom-call | flops 6700000256 | bytes 12000000 | tf_op jit(solution)/shard_map/front/pallas_call | solution.py:179
  83.3 5.9 %front.7 = (bf16[4,512,1024]{2,1,0:T(8,128)(2,1)S(1)}, bf16[512,1024]{1,0:T(8,128)(2,1)S(1)}, bf16[512,256]{1,0:T(8,128)(2,1)S(1)}, bf16[512,1024]{1,0:T(8,128)(...) custom-call(s32[3]{0:T(128)S(1)} %pad_add_fusion.where_ref, bf16[128,1024]{1,0:T(8,128)(2,1)S(1)} %pad_maximum_fusion.2.piece0, ...), custom_call_target="tpu_custom_call" | custom-call | flops 6700000256 | bytes 12000000 | tf_op jit(solution)/shard_map/front/pallas_call | solution.py:179
  89.2 1.7 %collective-permute-done.15.piece3 = bf16[128,1024]{1,0:T(8,128)(2,1)S(1)} collective-permute-done((bf16[128,1024]{1,0:T(8,128)(2,1)S(1)}, bf16[128,1024]{1,0:T(8,128)(2,1)S(1)}, u32[]{:S(2)}, u32[]{:S(2)}) %collective-permute-start.15) | collective-permute-done | bytes 262176 | tf_op jit(solution)/shard_map/ppermute | solution.py:498
  90.9 5.9 %front.6 = (bf16[4,512,1024]{2,1,0:T(8,128)(2,1)S(1)}, bf16[512,1024]{1,0:T(8,128)(2,1)S(1)}, bf16[512,256]{1,0:T(8,128)(2,1)S(1)}, bf16[512,1024]{1,0:T(8,128)(...) custom-call(s32[3]{0:T(128)S(1)} %pad_add_fusion.where_ref, bf16[128,1024]{1,0:T(8,128)(2,1)S(1)} %pad_maximum_fusion.piece0, ...), custom_call_target="tpu_custom_call" | custom-call | flops 6700000256 | bytes 12000000 | tf_op jit(solution)/shard_map/front/pallas_call | solution.py:179
  96.8 1.1 fusion.28
  98.0 9.7 %collective-permute-start.21 = (f32[8,2816]{1,0:T(8,128)S(1)}, f32[8,2816]{1,0:T(8,128)S(1)}, u32[]{:S(2)}, u32[]{:S(2)}) collective-permute-start(f32[8,2816]{1,0:T(8,128)S(1)} %pad.18), channel_id=1, source_target_pairs={{0,1},{1,0},{2,3},{3,2},{4,5},{5,4},{6,7},{7,6},{8,9},{9,8},{10,11... | collective-permute-start | bytes 270344 | tf_op jit(solution)/shard_map/ppermute | solution.py:504
  107.7 0.7 collective-permute-start.22
  108.4 1.0 collective-permute-start.23
  109.4 1.5 products.3
  111.2 3.1 %products.4 = bf16[2,256,1024]{2,1,0:T(8,128)(2,1)S(1)} custom-call(bf16[512,1024]{1,0:T(8,128)(2,1)S(1)} %get-tuple-element.161.refs_0_.dz_ref, bf16[512,1024]{1,0:T(8,128)(2,1)S(1)} %get-tuple-element.172.refs_1_.dz_ref, bf16[512,1024]{1,0:T(8,128)(2,1)S(1)} %get-tuple-element.177.refs_2_.dz_ref, bf16[512,1024]{1,0:T(8,128)(2,1)S(1)} %get-tuple-element.185.refs_3_.dz_ref, ...), custom_call_target="tpu_custom_call" | custom-call | flops 4400000000 | bytes 10000000 | tf_op jit(solution)/shard_map/products/pallas_call | solution.py:265
  114.5 0.5 collective-permute-start.20
  115.0 0.7 collective-permute-start.27
  115.7 3.1 %products.5 = bf16[2,256,1024]{2,1,0:T(8,128)(2,1)S(1)} custom-call(bf16[512,1024]{1,0:T(8,128)(2,1)S(1)} %get-tuple-element.161.refs_0_.dz_ref, bf16[512,1024]{1,0:T(8,128)(2,1)S(1)} %get-tuple-element.172.refs_1_.dz_ref, bf16[512,1024]{1,0:T(8,128)(2,1)S(1)} %get-tuple-element.177.refs_2_.dz_ref, bf16[512,1024]{1,0:T(8,128)(2,1)S(1)} %get-tuple-element.185.refs_3_.dz_ref, ...), custom_call_target="tpu_custom_call" | custom-call | flops 4400000000 | bytes 10000000 | tf_op jit(solution)/shard_map/products/pallas_call | solution.py:265
  119.1 0.7 collective-permute-start.24
  119.8 2.7 %collective-permute-done.27 = bf16[1,128,1024]{2,1,0:T(8,128)(2,1)S(1)} collective-permute-done((bf16[1,128,1024]{2,1,0:T(8,128)(2,1)S(1)}, bf16[1,128,1024]{2,1,0:T(8,128)(2,1)S(1)}, u32[]{:S(2)}, u32[]{:S(2)}) %collective-permute-start.27) | collective-permute-done | bytes 262176 | tf_op jit(solution)/shard_map/ppermute | solution.py:523
  122.6 0.8 collective-permute-start.26
  123.4 3.8 %taps.4 = f32[32,1024]{1,0:T(8,128)S(1)} custom-call(bf16[4,512,1024]{2,1,0:T(8,128)(2,1)S(1)} %get-tuple-element.147.refs_4_.maps_ref, bf16[512,1024]{1,0:T(8,128)(2,1)S(1)} %get-tuple-element.161.refs_0_.dz_ref, bf16[3,256,1024]{2,1,0:T(8,128)(2,1)S(1)} %copy-done.2), custom_call_target="tpu_custom_call" | custom-call | flops 4499999744 | bytes 4000000 | tf_op jit(solution)/shard_map/taps/pallas_call | solution.py:224
  127.5 3.8 %taps.5 = f32[32,1024]{1,0:T(8,128)S(1)} custom-call(bf16[4,512,1024]{2,1,0:T(8,128)(2,1)S(1)} %get-tuple-element.148.refs_5_.maps_ref, bf16[512,1024]{1,0:T(8,128)(2,1)S(1)} %get-tuple-element.172.refs_1_.dz_ref, bf16[3,256,1024]{2,1,0:T(8,128)(2,1)S(1)} %copy-done.2), custom_call_target="tpu_custom_call" | custom-call | flops 4499999744 | bytes 4000000 | tf_op jit(solution)/shard_map/taps/pallas_call | solution.py:224
  131.3 1.5 collective-permute-start.28
  132.8 0.7 collective-permute-start.25
  133.6 3.8 %taps.6 = f32[32,1024]{1,0:T(8,128)S(1)} custom-call(bf16[4,512,1024]{2,1,0:T(8,128)(2,1)S(1)} %get-tuple-element.149.refs_6_.maps_ref, bf16[512,1024]{1,0:T(8,128)(2,1)S(1)} %get-tuple-element.177.refs_2_.dz_ref, bf16[3,256,1024]{2,1,0:T(8,128)(2,1)S(1)} %copy-done.2), custom_call_target="tpu_custom_call" | custom-call | flops 4499999744 | bytes 4000000 | tf_op jit(solution)/shard_map/taps/pallas_call | solution.py:224
  137.6 3.8 %taps.7 = f32[32,1024]{1,0:T(8,128)S(1)} custom-call(bf16[4,512,1024]{2,1,0:T(8,128)(2,1)S(1)} %get-tuple-element.150.refs_7_.maps_ref, bf16[512,1024]{1,0:T(8,128)(2,1)S(1)} %get-tuple-element.185.refs_3_.dz_ref, bf16[3,256,1024]{2,1,0:T(8,128)(2,1)S(1)} %copy-done.2), custom_call_target="tpu_custom_call" | custom-call | flops 4499999744 | bytes 4000000 | tf_op jit(solution)/shard_map/taps/pallas_call | solution.py:224
  141.6 0.7 collective-permute-start.29
  142.3 0.7 collective-permute-start.30
  143.0 1.0 collective-permute-start.31
  144.1 0.6 fetch.1
  144.7 4.3 %collective-permute-done.30 = bf16[48,1024]{1,0:T(8,128)(2,1)S(1)} collective-permute-done((bf16[48,1024]{1,0:T(8,128)(2,1)S(1)}, bf16[48,1024]{1,0:T(8,128)(2,1)S(1)}, u32[]{:S(2)}, u32[]{:S(2)}) %collective-permute-start.30) | collective-permute-done | bytes 98336 | tf_op jit(solution)/shard_map/ppermute | solution.py:504
  148.9 2.8 %collective-permute-done.31 = bf16[48,1024]{1,0:T(8,128)(2,1)S(1)} collective-permute-done((bf16[48,1024]{1,0:T(8,128)(2,1)S(1)}, bf16[48,1024]{1,0:T(8,128)(2,1)S(1)}, u32[]{:S(2)}, u32[]{:S(2)}) %collective-permute-start.31) | collective-permute-done | bytes 98336 | tf_op jit(solution)/shard_map/ppermute | solution.py:504
  152.1 0.5 collective-permute-start.32
  153.3 0.7 collective-permute-done.33.rest2
  154.0 0.7 collective-permute-done.32.rest1
  154.8 6.3 %update.1 = (f32[1,256,1024]{2,1,0:T(8,128)}, f32[1,3,256,1024]{3,2,1,0:T(8,128)}, f32[1,256,2048]{2,1,0:T(8,128)}, f32[1,256,1280]{2,1,0:T(8,128)}, f32[27,1,10...) custom-call(s32[1]{0:T(128)} %bitcast.core_ref, ...), custom_call_target="tpu_custom_call" | custom-call | flops 4000000 | bytes 20000000 | tf_op jit(solution)/shard_map/update/pallas_call | solution.py:445
  (133 shorter events, 5.0 us)
Async XLA Ops:
  0.6 13.8 %copy-start.15 = (s32[4]{0:T(128)S(1)}, s32[4]{0:T(128)}, u32[]{:S(2)}) copy-start(s32[4]{0:T(128)} %param.17) | copy-start | bytes 52
  0.7 21.0 %copy-start = (f32[1,3,256,1024]{3,2,1,0:T(8,128)S(1)}, f32[1,3,256,1024]{3,2,1,0:T(8,128)}, u32[]{:S(2)}) copy-start(f32[1,3,256,1024]{3,2,1,0:T(8,128)} %refs_1_) | copy-start | bytes 9437188
  3.1 28.2 %all-to-all-start = ((bf16[32,16,1024]{2,1,0:T(8,128)(2,1)}), bf16[32,16,1024]{2,1,0:T(8,128)(2,1)}, u32[]{:S(2)}, u32[]{:S(2)}) async-start(bf16[32,16,1024]{2,1,0:T(8,128)(2,1)} %bitcast.73), calls=%async_computation | async-start | bytes 2097152 | tf_op jit(solution)/shard_map/all_to_all | solution.py:565
  21.7 1.4 copy-start.5
  21.7 2.3 %copy-start.13 = (f32[1,19]{1,0:T(1,128)S(1)}, f32[1,19]{1,0:T(1,128)}, u32[]{:S(2)}) copy-start(f32[1,19]{1,0:T(1,128)} %b_class.1) | copy-start | bytes 232
  26.6 3.6 %copy-start.3 = (f32[1,256,1280]{2,1,0:T(8,128)S(1)}, f32[1,256,1280]{2,1,0:T(8,128)}, u32[]{:S(2)}) copy-start(f32[1,256,1280]{2,1,0:T(8,128)} %refs_3_) | copy-start | bytes 3932164
  30.2 5.2 %copy-start.11 = (f32[1,5,256]{2,0,1:T(1,128)S(1)}, f32[1,5,256]{2,0,1:T(1,128)}, u32[]{:S(2)}) copy-start(f32[1,5,256]{2,0,1:T(1,128)} %param.23) | copy-start | bytes 15364
  30.2 7.1 %copy-start.10 = (f32[1,19,256]{2,0,1:T(1,128)S(1)}, f32[1,19,256]{2,0,1:T(1,128)}, u32[]{:S(2)}) copy-start(f32[1,19,256]{2,0,1:T(1,128)} %param.26) | copy-start | bytes 58372
  32.9 5.7 %collective-permute-start = (bf16[72,1024]{1,0:T(8,128)(2,1)}, bf16[72,1024]{1,0:T(8,128)(2,1)S(1)}, u32[]{:S(2)}, u32[]{:S(2)}) collective-permute-start(bf16[72,1024]{1,0:T(8,128)(2,1)} %pad_maximum_fusion.5), channel_id=1, source_target_pairs={{0,64},{4,68},{8,72},{12,76},{16,80},{20,84},{24,88},{28,92},{32,9... | collective-permute-start | bytes 442376 | tf_op jit(solution)/shard_map/ppermute | solution.py:572
  38.6 6.9 %collective-permute-start.7 = (bf16[64,1024]{1,0:T(8,128)(2,1)S(1)}, bf16[64,1024]{1,0:T(8,128)(2,1)S(1)}, u32[]{:S(2)}, u32[]{:S(2)}) collective-permute-start(bf16[64,1024]{1,0:T(8,128)(2,1)S(1)} %bitcast.84), channel_id=1, source_target_pairs={{0,4},{4,8},{8,12},{12,0},{16,20},{20,24},{24,28},{28,16},{32,36},... | collective-permute-start | bytes 393224 | tf_op jit(solution)/shard_map/ppermute | solution.py:496
  39.6 7.5 %collective-permute-start.8 = (bf16[64,1024]{1,0:T(8,128)(2,1)S(1)}, bf16[64,1024]{1,0:T(8,128)(2,1)S(1)}, u32[]{:S(2)}, u32[]{:S(2)}) collective-permute-start(bf16[64,1024]{1,0:T(8,128)(2,1)S(1)} %bitcast.85), channel_id=1, source_target_pairs={{0,12},{4,0},{8,4},{12,8},{16,28},{20,16},{24,20},{28,24},{32,44},... | collective-permute-start | bytes 393224 | tf_op jit(solution)/shard_map/ppermute | solution.py:497
  41.4 6.3 %collective-permute-start.9 = (bf16[64,1024]{1,0:T(8,128)(2,1)S(1)}, bf16[64,1024]{1,0:T(8,128)(2,1)S(1)}, u32[]{:S(2)}, u32[]{:S(2)}) collective-permute-start(bf16[64,1024]{1,0:T(8,128)(2,1)S(1)} %bitcast.86), channel_id=1, source_target_pairs={{0,8},{4,12},{8,0},{12,4},{16,24},{20,28},{24,16},{28,20},{32,40},... | collective-permute-start | bytes 393224 | tf_op jit(solution)/shard_map/ppermute | solution.py:498
  42.6 19.4 %copy-start.14 = (bf16[256,2048]{1,0:T(8,128)(2,1)S(1)}, bf16[256,2048]{1,0:T(8,128)(2,1)}, u32[]{:S(2)}) copy-start(bf16[256,2048]{1,0:T(8,128)(2,1)} %convert_bitcast_fusion.1) | copy-start | bytes 3145732
  42.8 5.6 %collective-permute-start.1 = (bf16[72,1024]{1,0:T(8,128)(2,1)S(1)}, bf16[72,1024]{1,0:T(8,128)(2,1)S(1)}, u32[]{:S(2)}, u32[]{:S(2)}) collective-permute-start(bf16[72,1024]{1,0:T(8,128)(2,1)S(1)} %pad_maximum_fusion.6), channel_id=1, source_target_pairs={{0,16},{4,20},{8,24},{12,28},{16,32},{20,36},{24,40},{28,44},{32,4... | collective-permute-start | bytes 442376 | tf_op jit(solution)/shard_map/ppermute | solution.py:496
  44.0 4.3 %collective-permute-start.2 = (bf16[72,1024]{1,0:T(8,128)(2,1)S(1)}, bf16[72,1024]{1,0:T(8,128)(2,1)S(1)}, u32[]{:S(2)}, u32[]{:S(2)}) collective-permute-start(bf16[72,1024]{1,0:T(8,128)(2,1)S(1)} %pad_maximum_fusion.6), channel_id=1, source_target_pairs={{0,48},{4,52},{8,56},{12,60},{16,0},{20,4},{24,8},{28,12},{32,16},... | collective-permute-start | bytes 442376 | tf_op jit(solution)/shard_map/ppermute | solution.py:497
  45.5 16.8 %slice-start = ((f32[1,5,256]{2,0,1:T(1,128)}), f32[1,1,256]{2,0,1:T(1,128)S(1)}, s32[]{:S(2)}) async-start(f32[1,5,256]{2,0,1:T(1,128)} %param.23), calls=%async_computation.1 | async-start | bytes 2048 | tf_op jit(solution)/shard_map/slice | solution.py:610
  45.5 5.9 %collective-permute-start.3 = (bf16[72,1024]{1,0:T(8,128)(2,1)S(1)}, bf16[72,1024]{1,0:T(8,128)(2,1)S(1)}, u32[]{:S(2)}, u32[]{:S(2)}) collective-permute-start(bf16[72,1024]{1,0:T(8,128)(2,1)S(1)} %pad_maximum_fusion.6), channel_id=1, source_target_pairs={{0,32},{4,36},{8,40},{12,44},{16,48},{20,52},{24,56},{28,60},{32,0... | collective-permute-start | bytes 442376 | tf_op jit(solution)/shard_map/ppermute | solution.py:498
  47.1 15.5 %copy-start.12 = (f32[1,256]{1,0:T(1,128)S(1)}, f32[1,256]{1,0:T(1,128)}, u32[]{:S(2)}) copy-start(f32[1,256]{1,0:T(1,128)} %b_proj.1) | copy-start | bytes 3076
  47.1 16.5 %copy-start.2 = (bf16[3,256,1024]{2,1,0:T(8,128)(2,1)S(1)}, bf16[3,256,1024]{2,1,0:T(8,128)(2,1)}, u32[]{:S(2)}) copy-start(bf16[3,256,1024]{2,1,0:T(8,128)(2,1)} %convert_bitcast_fusion.w_point) | copy-start | bytes 4718596
  47.2 16.5 %copy-start.7 = (bf16[256,1024]{1,0:T(8,128)(2,1)S(1)}, bf16[256,1024]{1,0:T(8,128)(2,1)}, u32[]{:S(2)}) copy-start(bf16[256,1024]{1,0:T(8,128)(2,1)} %convert_bitcast_fusion.3.w_plain) | copy-start | bytes 1572868
  47.2 16.5 %copy-start.8 = (bf16[256,1024]{1,0:T(8,128)(2,1)S(1)}, bf16[256,1024]{1,0:T(8,128)(2,1)}, u32[]{:S(2)}) copy-start(bf16[256,1024]{1,0:T(8,128)(2,1)} %slice.251.w_proj) | copy-start | bytes 1572868
  47.2 16.5 %copy-start.9 = (f32[1,3,9,1024]{3,0,2,1:T(1,128)S(1)}, f32[1,3,9,1024]{3,0,2,1:T(1,128)}, u32[]{:S(2)}) copy-start(f32[1,3,9,1024]{3,0,2,1:T(1,128)} %param.20) | copy-start | bytes 331780
  51.4 6.7 %collective-permute-start.4 = (bf16[136,1024]{1,0:T(8,128)(2,1)S(1)}, bf16[136,1024]{1,0:T(8,128)(2,1)S(1)}, u32[]{:S(2)}, u32[]{:S(2)}) collective-permute-start(bf16[136,1024]{1,0:T(8,128)(2,1)S(1)} %get-tuple-element.115.piece0), channel_id=1, source_target_pairs={{0,4},{4,8},{8,12},{12,0},{16,20},{20,24},{24,28},{28,16},{32,36},... | collective-permute-start | bytes 835592 | tf_op jit(solution)/shard_map/ppermute | solution.py:496
  51.6 9.1 %collective-permute-start.5 = (bf16[136,1024]{1,0:T(8,128)(2,1)S(1)}, bf16[136,1024]{1,0:T(8,128)(2,1)S(1)}, u32[]{:S(2)}, u32[]{:S(2)}) collective-permute-start(bf16[136,1024]{1,0:T(8,128)(2,1)S(1)} %get-tuple-element.115.piece0), channel_id=1, source_target_pairs={{0,12},{4,0},{8,4},{12,8},{16,28},{20,16},{24,20},{28,24},{32,44},... | collective-permute-start | bytes 835592 | tf_op jit(solution)/shard_map/ppermute | solution.py:497
  54.2 7.9 %collective-permute-start.6 = (bf16[136,1024]{1,0:T(8,128)(2,1)S(1)}, bf16[136,1024]{1,0:T(8,128)(2,1)S(1)}, u32[]{:S(2)}, u32[]{:S(2)}) collective-permute-start(bf16[136,1024]{1,0:T(8,128)(2,1)S(1)} %get-tuple-element.115.piece0), channel_id=1, source_target_pairs={{0,8},{4,12},{8,0},{12,4},{16,24},{20,28},{24,16},{28,20},{32,40},... | collective-permute-start | bytes 835592 | tf_op jit(solution)/shard_map/ppermute | solution.py:498
  54.4 15.1 %collective-permute-start.10 = (bf16[128,1024]{1,0:T(8,128)(2,1)S(1)}, bf16[128,1024]{1,0:T(8,128)(2,1)S(1)}, u32[]{:S(2)}, u32[]{:S(2)}) collective-permute-start(bf16[128,1024]{1,0:T(8,128)(2,1)S(1)} %pad_maximum_fusion.1.piece0), channel_id=1, source_target_pairs={{0,16},{4,20},{8,24},{12,28},{16,32},{20,36},{24,40},{28,44},{32,4... | collective-permute-start | bytes 786440 | tf_op jit(solution)/shard_map/ppermute | solution.py:496
  54.5 15.1 %collective-permute-start.11 = (bf16[128,1024]{1,0:T(8,128)(2,1)S(1)}, bf16[128,1024]{1,0:T(8,128)(2,1)S(1)}, u32[]{:S(2)}, u32[]{:S(2)}) collective-permute-start(bf16[128,1024]{1,0:T(8,128)(2,1)S(1)} %pad_maximum_fusion.1.piece0), channel_id=1, source_target_pairs={{0,48},{4,52},{8,56},{12,60},{16,0},{20,4},{24,8},{28,12},{32,16},... | collective-permute-start | bytes 786440 | tf_op jit(solution)/shard_map/ppermute | solution.py:497
  58.1 11.5 %collective-permute-start.12 = (bf16[128,1024]{1,0:T(8,128)(2,1)S(1)}, bf16[128,1024]{1,0:T(8,128)(2,1)S(1)}, u32[]{:S(2)}, u32[]{:S(2)}) collective-permute-start(bf16[128,1024]{1,0:T(8,128)(2,1)S(1)} %pad_maximum_fusion.1.piece0), channel_id=1, source_target_pairs={{0,32},{4,36},{8,40},{12,44},{16,48},{20,52},{24,56},{28,60},{32,0... | collective-permute-start | bytes 786440 | tf_op jit(solution)/shard_map/ppermute | solution.py:498
  69.6 13.6 %collective-permute-start.16 = (bf16[128,1024]{1,0:T(8,128)(2,1)S(1)}, bf16[128,1024]{1,0:T(8,128)(2,1)S(1)}, u32[]{:S(2)}, u32[]{:S(2)}) collective-permute-start(bf16[128,1024]{1,0:T(8,128)(2,1)S(1)} %pad_maximum_fusion.2.piece0), channel_id=1, source_target_pairs={{0,16},{4,20},{8,24},{12,28},{16,32},{20,36},{24,40},{28,44},{32,4... | collective-permute-start | bytes 786440 | tf_op jit(solution)/shard_map/ppermute | solution.py:496
  70.1 13.2 %collective-permute-start.17 = (bf16[128,1024]{1,0:T(8,128)(2,1)S(1)}, bf16[128,1024]{1,0:T(8,128)(2,1)S(1)}, u32[]{:S(2)}, u32[]{:S(2)}) collective-permute-start(bf16[128,1024]{1,0:T(8,128)(2,1)S(1)} %pad_maximum_fusion.2.piece0), channel_id=1, source_target_pairs={{0,48},{4,52},{8,56},{12,60},{16,0},{20,4},{24,8},{28,12},{32,16},... | collective-permute-start | bytes 786440 | tf_op jit(solution)/shard_map/ppermute | solution.py:497
  72.4 11.0 %collective-permute-start.18 = (bf16[128,1024]{1,0:T(8,128)(2,1)S(1)}, bf16[128,1024]{1,0:T(8,128)(2,1)S(1)}, u32[]{:S(2)}, u32[]{:S(2)}) collective-permute-start(bf16[128,1024]{1,0:T(8,128)(2,1)S(1)} %pad_maximum_fusion.2.piece0), channel_id=1, source_target_pairs={{0,32},{4,36},{8,40},{12,44},{16,48},{20,52},{24,56},{28,60},{32,0... | collective-permute-start | bytes 786440 | tf_op jit(solution)/shard_map/ppermute | solution.py:498
  74.7 14.6 %collective-permute-start.13 = (bf16[128,1024]{1,0:T(8,128)(2,1)S(1)}, bf16[128,1024]{1,0:T(8,128)(2,1)S(1)}, u32[]{:S(2)}, u32[]{:S(2)}) collective-permute-start(bf16[128,1024]{1,0:T(8,128)(2,1)S(1)} %pad_maximum_fusion.piece0), channel_id=1, source_target_pairs={{0,4},{4,8},{8,12},{12,0},{16,20},{20,24},{24,28},{28,16},{32,36},... | collective-permute-start | bytes 786440 | tf_op jit(solution)/shard_map/ppermute | solution.py:496
  74.7 14.6 %collective-permute-start.14 = (bf16[128,1024]{1,0:T(8,128)(2,1)S(1)}, bf16[128,1024]{1,0:T(8,128)(2,1)S(1)}, u32[]{:S(2)}, u32[]{:S(2)}) collective-permute-start(bf16[128,1024]{1,0:T(8,128)(2,1)S(1)} %pad_maximum_fusion.piece0), channel_id=1, source_target_pairs={{0,12},{4,0},{8,4},{12,8},{16,28},{20,16},{24,20},{28,24},{32,44},... | collective-permute-start | bytes 786440 | tf_op jit(solution)/shard_map/ppermute | solution.py:497
  83.2 7.7 %collective-permute-start.15 = (bf16[128,1024]{1,0:T(8,128)(2,1)S(1)}, bf16[128,1024]{1,0:T(8,128)(2,1)S(1)}, u32[]{:S(2)}, u32[]{:S(2)}) collective-permute-start(bf16[128,1024]{1,0:T(8,128)(2,1)S(1)} %pad_maximum_fusion.piece0), channel_id=1, source_target_pairs={{0,8},{4,12},{8,0},{12,4},{16,24},{20,28},{24,16},{28,20},{32,40},... | collective-permute-start | bytes 786440 | tf_op jit(solution)/shard_map/ppermute | solution.py:498
  98.0 21.0 %collective-permute-start.21 = (f32[8,2816]{1,0:T(8,128)S(1)}, f32[8,2816]{1,0:T(8,128)S(1)}, u32[]{:S(2)}, u32[]{:S(2)}) collective-permute-start(f32[8,2816]{1,0:T(8,128)S(1)} %pad.18), channel_id=1, source_target_pairs={{0,1},{1,0},{2,3},{3,2},{4,5},{5,4},{6,7},{7,6},{8,9},{9,8},{10,11... | collective-permute-start | bytes 270344 | tf_op jit(solution)/shard_map/ppermute | solution.py:504
  107.7 11.3 %collective-permute-start.22 = (f32[8,2816]{1,0:T(8,128)S(1)}, f32[8,2816]{1,0:T(8,128)S(1)}, u32[]{:S(2)}, u32[]{:S(2)}) collective-permute-start(f32[8,2816]{1,0:T(8,128)S(1)} %pad.18), channel_id=1, source_target_pairs={{0,2},{1,3},{2,0},{3,1},{4,6},{5,7},{6,4},{7,5},{8,10},{9,11},{10,... | collective-permute-start | bytes 270344 | tf_op jit(solution)/shard_map/ppermute | solution.py:504
  108.4 10.6 %collective-permute-start.23 = (f32[8,2816]{1,0:T(8,128)S(1)}, f32[8,2816]{1,0:T(8,128)S(1)}, u32[]{:S(2)}, u32[]{:S(2)}) collective-permute-start(f32[8,2816]{1,0:T(8,128)S(1)} %pad.18), channel_id=1, source_target_pairs={{0,3},{1,2},{2,1},{3,0},{4,7},{5,6},{6,5},{7,4},{8,11},{9,10},{10,... | collective-permute-start | bytes 270344 | tf_op jit(solution)/shard_map/ppermute | solution.py:504
  111.0 3.3 %collective-permute-start.19 = (bf16[1,128,1024]{2,1,0:T(8,128)(2,1)S(1)}, bf16[1,128,1024]{2,1,0:T(8,128)(2,1)S(1)}, u32[]{:S(2)}, u32[]{:S(2)}) collective-permute-start(bf16[1,128,1024]{2,1,0:T(8,128)(2,1)S(1)} %constant_dynamic-slice_fusion.2), channel_id=1, source_target_pairs={{0,1},{1,0},{2,3},{3,2},{4,5},{5,4},{6,7},{7,6},{8,9},{9,8},{10,11... | collective-permute-start | bytes 786440 | tf_op jit(solution)/shard_map/ppermute | solution.py:519
  114.5 4.3 %collective-permute-start.20 = (bf16[2,128,1024]{2,1,0:T(8,128)(2,1)S(1)}, bf16[2,128,1024]{2,1,0:T(8,128)(2,1)S(1)}, u32[]{:S(2)}, u32[]{:S(2)}) collective-permute-start(bf16[2,128,1024]{2,1,0:T(8,128)(2,1)S(1)} %constant_dynamic-slice_fusion.1), channel_id=1, source_target_pairs={{0,1},{1,0},{2,3},{3,2},{4,5},{5,4},{6,7},{7,6},{8,9},{9,8},{10,11... | collective-permute-start | bytes 1572872 | tf_op jit(solution)/shard_map/ppermute | solution.py:519
  115.0 7.6 %collective-permute-start.27 = (bf16[1,128,1024]{2,1,0:T(8,128)(2,1)S(1)}, bf16[1,128,1024]{2,1,0:T(8,128)(2,1)S(1)}, u32[]{:S(2)}, u32[]{:S(2)}) collective-permute-start(bf16[1,128,1024]{2,1,0:T(8,128)(2,1)S(1)} %add_convert_fusion.5), channel_id=1, source_target_pairs={{0,2},{1,3},{2,0},{3,1},{4,6},{5,7},{6,4},{7,5},{8,10},{9,11},{10,... | collective-permute-start | bytes 786440 | tf_op jit(solution)/shard_map/ppermute | solution.py:523
  119.1 8.2 %collective-permute-start.24 = (bf16[2,128,1024]{2,1,0:T(8,128)(2,1)S(1)}, bf16[2,128,1024]{2,1,0:T(8,128)(2,1)S(1)}, u32[]{:S(2)}, u32[]{:S(2)}) collective-permute-start(bf16[2,128,1024]{2,1,0:T(8,128)(2,1)S(1)} %constant_dynamic-slice_fusion), channel_id=1, source_target_pairs={{0,1},{1,0},{2,3},{3,2},{4,5},{5,4},{6,7},{7,6},{8,9},{9,8},{10,11... | collective-permute-start | bytes 1572872 | tf_op jit(solution)/shard_map/ppermute | solution.py:519
  122.6 14.8 %collective-permute-start.26 = (bf16[2,128,1024]{2,1,0:T(8,128)(2,1)S(1)}, bf16[2,128,1024]{2,1,0:T(8,128)(2,1)S(1)}, u32[]{:S(2)}, u32[]{:S(2)}) collective-permute-start(bf16[2,128,1024]{2,1,0:T(8,128)(2,1)S(1)} %add_convert_fusion.3), channel_id=1, source_target_pairs={{0,2},{1,3},{2,0},{3,1},{4,6},{5,7},{6,4},{7,5},{8,10},{9,11},{10,... | collective-permute-start | bytes 1572872 | tf_op jit(solution)/shard_map/ppermute | solution.py:523
  131.3 6.3 %collective-permute-start.28 = (bf16[1,128,1024]{2,1,0:T(8,128)(2,1)S(1)}, bf16[1,128,1024]{2,1,0:T(8,128)(2,1)S(1)}, u32[]{:S(2)}, u32[]{:S(2)}) collective-permute-start(bf16[1,128,1024]{2,1,0:T(8,128)(2,1)S(1)} %add_convert_fusion.4.mine0), channel_id=1, source_target_pairs={{0,1},{1,0},{2,3},{3,2},{4,5},{5,4},{6,7},{7,6},{8,9},{9,8},{10,11... | collective-permute-start | bytes 786440 | tf_op jit(solution)/shard_map/ppermute | solution.py:656
  132.8 19.0 %collective-permute-start.25 = (bf16[2,128,1024]{2,1,0:T(8,128)(2,1)S(1)}, bf16[2,128,1024]{2,1,0:T(8,128)(2,1)S(1)}, u32[]{:S(2)}, u32[]{:S(2)}) collective-permute-start(bf16[2,128,1024]{2,1,0:T(8,128)(2,1)S(1)} %add_convert_fusion.2), channel_id=1, source_target_pairs={{0,2},{1,3},{2,0},{3,1},{4,6},{5,7},{6,4},{7,5},{8,10},{9,11},{10,... | collective-permute-start | bytes 1572872 | tf_op jit(solution)/shard_map/ppermute | solution.py:673
  137.6 6.5 %copy-start.4 = (f32[1,256,1280]{2,1,0:T(8,128)S(1)}, f32[1,256,1280]{2,1,0:T(8,128)}, u32[]{:S(2)}) copy-start(f32[1,256,1280]{2,1,0:T(8,128)} %refs_3_) | copy-start | bytes 3932164
  137.6 6.5 %copy-start.6 = (f32[1,256,1024]{2,1,0:T(8,128)S(1)}, f32[1,256,1024]{2,1,0:T(8,128)}, u32[]{:S(2)}) copy-start(f32[1,256,1024]{2,1,0:T(8,128)} %refs_0_) | copy-start | bytes 3145732
  141.5 2.6 %copy-start.1 = (f32[1,256,2048]{2,1,0:T(8,128)S(1)}, f32[1,256,2048]{2,1,0:T(8,128)}, u32[]{:S(2)}) copy-start(f32[1,256,2048]{2,1,0:T(8,128)} %refs_2_) | copy-start | bytes 6291460
  141.6 3.1 %collective-permute-start.29 = (bf16[48,1024]{1,0:T(8,128)(2,1)S(1)}, bf16[48,1024]{1,0:T(8,128)(2,1)S(1)}, u32[]{:S(2)}, u32[]{:S(2)}) collective-permute-start(bf16[48,1024]{1,0:T(8,128)(2,1)S(1)} %maximum_maximum_fusion), channel_id=1, source_target_pairs={{0,1},{1,0},{2,3},{3,2},{4,5},{5,4},{6,7},{7,6},{8,9},{9,8},{10,11... | collective-permute-start | bytes 294920 | tf_op jit(solution)/shard_map/ppermute | solution.py:504
  142.3 6.7 %collective-permute-start.30 = (bf16[48,1024]{1,0:T(8,128)(2,1)S(1)}, bf16[48,1024]{1,0:T(8,128)(2,1)S(1)}, u32[]{:S(2)}, u32[]{:S(2)}) collective-permute-start(bf16[48,1024]{1,0:T(8,128)(2,1)S(1)} %maximum_maximum_fusion), channel_id=1, source_target_pairs={{0,2},{1,3},{2,0},{3,1},{4,6},{5,7},{6,4},{7,5},{8,10},{9,11},{10,... | collective-permute-start | bytes 294920 | tf_op jit(solution)/shard_map/ppermute | solution.py:504
  143.0 8.8 %collective-permute-start.31 = (bf16[48,1024]{1,0:T(8,128)(2,1)S(1)}, bf16[48,1024]{1,0:T(8,128)(2,1)S(1)}, u32[]{:S(2)}, u32[]{:S(2)}) collective-permute-start(bf16[48,1024]{1,0:T(8,128)(2,1)S(1)} %maximum_maximum_fusion), channel_id=1, source_target_pairs={{0,3},{1,2},{2,1},{3,0},{4,7},{5,6},{6,5},{7,4},{8,11},{9,10},{10,... | collective-permute-start | bytes 294920 | tf_op jit(solution)/shard_map/ppermute | solution.py:504
  152.1 2.0 %collective-permute-start.33 = (bf16[2,128,1024]{2,1,0:T(8,128)(2,1)S(1)}, bf16[2,128,1024]{2,1,0:T(8,128)(2,1)S(1)}, u32[]{:S(2)}, u32[]{:S(2)}) collective-permute-start(bf16[2,128,1024]{2,1,0:T(8,128)(2,1)S(1)} %add_convert_fusion.mine2), channel_id=1, source_target_pairs={{0,1},{1,0},{2,3},{3,2},{4,5},{5,4},{6,7},{7,6},{8,9},{9,8},{10,11... | collective-permute-start | bytes 1572872 | tf_op jit(solution)/shard_map/ppermute | solution.py:678
  152.1 2.6 %collective-permute-start.32 = (bf16[2,128,1024]{2,1,0:T(8,128)(2,1)S(1)}, bf16[2,128,1024]{2,1,0:T(8,128)(2,1)S(1)}, u32[]{:S(2)}, u32[]{:S(2)}) collective-permute-start(bf16[2,128,1024]{2,1,0:T(8,128)(2,1)S(1)} %add_convert_fusion.1.mine1), channel_id=1, source_target_pairs={{0,1},{1,0},{2,3},{3,2},{4,5},{5,4},{6,7},{7,6},{8,9},{9,8},{10,11... | collective-permute-start | bytes 1572872 | tf_op jit(solution)/shard_map/ppermute | solution.py:678

commit v2 on v1

--- a/solution.py
+++ b/solution.py
@@ -524,8 +524,9 @@
 
 
 def sum_batch_small(partial):
-    near, beside, across, beyond = [part.astype(F32) for part in from_batch(partial)]
-    return (near + beside) + (across + beyond)
+    pair = partial.astype(F32) + lax.ppermute(partial, "batch", CORES).astype(F32)
+    pair = pair.astype(BF16)
+    return pair.astype(F32) + lax.ppermute(pair, "batch", CHIPS).astype(F32)
 
 
 def pick(table, plan, turn_ids):
@@ -637,15 +638,15 @@
     dbranch4 = jnp.where(branch4 > 0, dbranch4, 0.0)
     factors = [dbranch4, dbias_proj, branch4] + pooled
     factors = jnp.concatenate([part.astype(F32) for part in factors], axis=1)
-    factors = from_batch(jnp.pad(factors, ((0, 8 - turns), (0, 0))))
+    factors = from_batch(factors)
     proj_part = products(dpres, joined, 0, 1)
-    dzs, proj_part = after((dzs, proj_part))
     proj_pair = sum_cores(proj_part, core)
+    dzs, proj_pair = after((dzs, proj_pair))
     low_part = products(dzs, stacks, 0, 2)
-    dzs, low_part, proj_pair = after((dzs, low_part, proj_pair))
+    proj_total = sum_chips(proj_pair)
+    dzs, low_part, proj_total = after((dzs, low_part, proj_total))
     low_pair = sum_cores(low_part, core)
     high_part = products(dzs, stacks, 2, 2)
-    proj_total = sum_chips(proj_pair)
     dzs, high_part, low_pair, factors = after((dzs, high_part, low_pair, factors))
     high_pair = sum_cores(high_part, core)
     low_total = sum_chips(low_pair)
@@ -659,6 +660,7 @@
     taps_parts.append(depth_taps(stacks[3], dzs[3], point16))
     depth_part = sum(taps_parts)
     factors, depth_part = after((factors, depth_part))
+    factors = [jnp.pad(part, ((0, 8 - turns), (0, 0))) for part in factors]
     factors = in_order(factors, core, chip)
     dclass = sum(dclass)
     bias_row = jnp.pad(jnp.sum(dbranch4, axis=0)[None], ((2, 5), (0, wide - HID)))

time: 162 us -> 162 us (level)
    ppermute x6 -> x3, starting transfers between devices: 13.9 us -> 2.22 us  [from_batch(): lax.ppermute(mine, 'batch', [(b, b ^ other) for b in range(4)])]
    ppermute x3, starting transfers between devices: 1.4 us -> 10.7 us  [sum_cores(): lax.ppermute(other, 'batch', CORES).astype(F32)]
    ppermute x6 -> x3, waiting for transfers between devices: 7.1 us -> 0.01 us  [from_batch(): lax.ppermute(mine, 'batch', [(b, b ^ other) for b in range(4)])]
    ppermute x0 -> x2, waiting for transfers between devices: none -> 5.45 us  [the longest x1 4.66 us: sum_batch_small(): return pair.astype(F32) + lax.ppermute(pair, 'batch', CHIPS).astype(F32)]
    ppermute x0 -> x2, starting transfers between devices: none -> 2.11 us  [the longest x1 1.29 us: sum_batch_small(): lax.ppermute(partial, 'batch', CORES).astype(F32)]
    ppermute x2, waiting for transfers between devices: 2.74 us -> 4.41 us  [sum_chips(): lax.ppermute(pair, 'batch', CHIPS).astype(F32)]
  transfers between devices with their start and end apart: 35 -> 34, of which waited for: 14 -> 14; matrix products, arithmetic and copies ran while one was open for 8% -> 8% of each run, Pallas kernels for 26% -> 25%
where the time goes in v2:
time: 162 us; the launch traced here: 161 us
  starting transfers between devices  57.3 us (35%)
  Pallas kernels  53.3 us (33%)
  waiting for transfers between devices  21.3 us (13%)
  between operations  10.1 us (6%)
  other arithmetic  9.37 us (6%)
  local copies, waits for them, and re-layouts  7.18 us (4%)
  matrix products  2.65 us (2%)
    pallas_call x4, Pallas kernels, front(): pl.pallas_call(functools.partial(front_kernel, order), name='front', out_...  23.4 us
    pallas_call x4, Pallas kernels, depth_taps(): pl.pallas_call(taps_kernel, name='taps', grid=(channels // block,), out_s...  15.3 us
    ppermute x6, starting transfers between devices, gather_ring(): lax.ppermute(block, 'trial', along(-1))  13.4 us
    all_to_all x1, starting transfers between devices, on_device(): lax.all_to_all(own.reshape(32, 16, channels), 'trial', 0, 0, tiled=True)  11.3 us
    ppermute x3, starting transfers between devices, sum_cores(): lax.ppermute(other, 'batch', CORES).astype(F32)  10.7 us
    pallas_call x3, Pallas kernels, products(): pl.pallas_call(functools.partial(product_kernel, count, first), name='pro...  7.73 us
    ppermute x6, starting transfers between devices, gather_ring(): lax.ppermute(block, 'trial', along(2))  7.62 us
    ppermute x6, waiting for transfers between devices, gather_ring(): lax.ppermute(block, 'trial', along(2))  6.56 us
  transfers between devices with their start and end apart: 34, of which 14 were waited for; matrix products, arithmetic and copies ran while one was open for 8% of the time, Pallas kernels for 25%

profile of v2, /device:TPU:1, one launch (start us, length us, event | category | flops | bytes accessed | tf_op | source)
XLA Modules:
  0.0 161.2 jit_solution(7319867525401072321)
XLA Ops:
  0.7 2.4 %copy.31 = bf16[1,1,1024,512]{2,3,1,0:T(8,128)(2,1)} copy(bf16[1,1,1024,512]{3,2,1,0:T(8,128)(2,1)} %param.14) | data formatting | bytes 2097152 | tf_op args[0]
  3.1 11.3 %all-to-all-start = ((bf16[32,16,1024]{2,1,0:T(8,128)(2,1)}), bf16[32,16,1024]{2,1,0:T(8,128)(2,1)}, u32[]{:S(2)}, u32[]{:S(2)}) async-start(bf16[32,16,1024]{2,1,0:T(8,128)(2,1)} %bitcast.73), calls=%async_computation | async-start | bytes 2097152 | tf_op jit(solution)/shard_map/all_to_all | solution.py:566
  14.4 0.6 fusion.30
  20.3 1.3 convert_reduce_fusion
  21.7 1.4 convert_bitcast_fusion.w_point
  23.1 0.9 convert_bitcast_fusion.3.w_plain
  26.6 0.8 fusion.18
  27.5 2.7 %convert_bitcast_fusion.1 = bf16[256,2048]{1,0:T(8,128)(2,1)} fusion(f32[1,256,2048]{2,1,0:T(8,128)} %refs_2_), kind=kLoop, calls=%fused_computation.11 | loop fusion | flops 524288 | bytes 3145728 | tf_op jit(solution)/shard_map/convert_element_type | solution.py:607
  30.2 0.9 convert_bitcast_fusion.2
  31.3 0.8 constant_dynamic-slice_fusion.8
  32.2 0.7 pad_maximum_fusion.5
  32.8 2.5 %collective-permute-start = (bf16[72,1024]{1,0:T(8,128)(2,1)}, bf16[72,1024]{1,0:T(8,128)(2,1)S(1)}, u32[]{:S(2)}, u32[]{:S(2)}) collective-permute-start(bf16[72,1024]{1,0:T(8,128)(2,1)} %pad_maximum_fusion.5), channel_id=1, source_target_pairs={{0,64},{4,68},{8,72},{12,76},{16,80},{20,84},{24,88},{28,92},{32,9... | collective-permute-start | bytes 442376 | tf_op jit(solution)/shard_map/ppermute | solution.py:573
  35.4 1.9 %slice.251.w_proj = bf16[256,1024]{1,0:T(8,128)(2,1)} slice(bf16[256,1280]{1,0:T(8,128)(2,1)} %convert_bitcast_fusion.2), slice={[0:256], [0:1024]} | slice | bytes 1048576 | tf_op jit(solution)/shard_map/slice | solution.py:624
  37.4 1.2 collective-permute-done
  38.6 1.0 collective-permute-start.7
  39.6 1.7 %collective-permute-start.8 = (bf16[64,1024]{1,0:T(8,128)(2,1)S(1)}, bf16[64,1024]{1,0:T(8,128)(2,1)S(1)}, u32[]{:S(2)}, u32[]{:S(2)}) collective-permute-start(bf16[64,1024]{1,0:T(8,128)(2,1)S(1)} %bitcast.85), channel_id=1, source_target_pairs={{0,12},{4,0},{8,4},{12,8},{16,28},{20,16},{24,20},{28,24},{32,44},... | collective-permute-start | bytes 393224 | tf_op jit(solution)/shard_map/ppermute | solution.py:497
  41.4 1.2 collective-permute-start.9
  42.8 1.3 collective-permute-start.1
  44.0 1.5 collective-permute-start.2
  45.5 1.6 collective-permute-start.3
  47.2 0.4 collective-permute-done.9
  47.6 0.7 collective-permute-done.1
  48.4 3.0 %collective-permute-done.3 = bf16[72,1024]{1,0:T(8,128)(2,1)S(1)} collective-permute-done((bf16[72,1024]{1,0:T(8,128)(2,1)S(1)}, bf16[72,1024]{1,0:T(8,128)(2,1)S(1)}, u32[]{:S(2)}, u32[]{:S(2)}) %collective-permute-start.3) | collective-permute-done | bytes 147488 | tf_op jit(solution)/shard_map/ppermute | solution.py:498
  51.6 2.6 %collective-permute-start.5 = (bf16[136,1024]{1,0:T(8,128)(2,1)S(1)}, bf16[136,1024]{1,0:T(8,128)(2,1)S(1)}, u32[]{:S(2)}, u32[]{:S(2)}) collective-permute-start(bf16[136,1024]{1,0:T(8,128)(2,1)S(1)} %get-tuple-element.115.piece0), channel_id=1, source_target_pairs={{0,12},{4,0},{8,4},{12,8},{16,28},{20,16},{24,20},{28,24},{32,44},... | collective-permute-start | bytes 835592 | tf_op jit(solution)/shard_map/ppermute | solution.py:497
  54.5 2.7 %collective-permute-start.11 = (bf16[128,1024]{1,0:T(8,128)(2,1)S(1)}, bf16[128,1024]{1,0:T(8,128)(2,1)S(1)}, u32[]{:S(2)}, u32[]{:S(2)}) collective-permute-start(bf16[128,1024]{1,0:T(8,128)(2,1)S(1)} %pad_maximum_fusion.1.piece0), channel_id=1, source_target_pairs={{0,48},{4,52},{8,56},{12,60},{16,0},{20,4},{24,8},{28,12},{32,16},... | collective-permute-start | bytes 786440 | tf_op jit(solution)/shard_map/ppermute | solution.py:497
  57.2 0.9 collective-permute-done.4.piece1
  58.1 2.2 %collective-permute-start.12 = (bf16[128,1024]{1,0:T(8,128)(2,1)S(1)}, bf16[128,1024]{1,0:T(8,128)(2,1)S(1)}, u32[]{:S(2)}, u32[]{:S(2)}) collective-permute-start(bf16[128,1024]{1,0:T(8,128)(2,1)S(1)} %pad_maximum_fusion.1.piece0), channel_id=1, source_target_pairs={{0,32},{4,36},{8,40},{12,44},{16,48},{20,52},{24,56},{28,60},{32,0... | collective-permute-start | bytes 786440 | tf_op jit(solution)/shard_map/ppermute | solution.py:498
  60.7 1.4 collective-permute-done.6.piece3
  62.6 1.1 convolution_add_fusion
  63.7 5.9 %front.4 = (bf16[4,512,1024]{2,1,0:T(8,128)(2,1)S(1)}, bf16[512,1024]{1,0:T(8,128)(2,1)S(1)}, bf16[512,256]{1,0:T(8,128)(2,1)S(1)}, bf16[512,1024]{1,0:T(8,128)(...) custom-call(s32[3]{0:T(128)S(1)} %pad_add_fusion.where_ref, bf16[136,1024]{1,0:T(8,128)(2,1)S(1)} %get-tuple-element.115.piece0, ...), custom_call_target="tpu_custom_call" | custom-call | flops 6700000256 | bytes 12000000 | tf_op jit(solution)/shard_map/front/pallas_call | solution.py:179
  69.6 0.5 collective-permute-start.16
  70.1 2.3 %collective-permute-start.17 = (bf16[128,1024]{1,0:T(8,128)(2,1)S(1)}, bf16[128,1024]{1,0:T(8,128)(2,1)S(1)}, u32[]{:S(2)}, u32[]{:S(2)}) collective-permute-start(bf16[128,1024]{1,0:T(8,128)(2,1)S(1)} %pad_maximum_fusion.2.piece0), channel_id=1, source_target_pairs={{0,48},{4,52},{8,56},{12,60},{16,0},{20,4},{24,8},{28,12},{32,16},... | collective-permute-start | bytes 786440 | tf_op jit(solution)/shard_map/ppermute | solution.py:497
  72.4 2.3 %collective-permute-start.18 = (bf16[128,1024]{1,0:T(8,128)(2,1)S(1)}, bf16[128,1024]{1,0:T(8,128)(2,1)S(1)}, u32[]{:S(2)}, u32[]{:S(2)}) collective-permute-start(bf16[128,1024]{1,0:T(8,128)(2,1)S(1)} %pad_maximum_fusion.2.piece0), channel_id=1, source_target_pairs={{0,32},{4,36},{8,40},{12,44},{16,48},{20,52},{24,56},{28,60},{32,0... | collective-permute-start | bytes 786440 | tf_op jit(solution)/shard_map/ppermute | solution.py:498
  74.7 2.7 %collective-permute-start.14 = (bf16[128,1024]{1,0:T(8,128)(2,1)S(1)}, bf16[128,1024]{1,0:T(8,128)(2,1)S(1)}, u32[]{:S(2)}, u32[]{:S(2)}) collective-permute-start(bf16[128,1024]{1,0:T(8,128)(2,1)S(1)} %pad_maximum_fusion.piece0), channel_id=1, source_target_pairs={{0,12},{4,0},{8,4},{12,8},{16,28},{20,16},{24,20},{28,24},{32,44},... | collective-permute-start | bytes 786440 | tf_op jit(solution)/shard_map/ppermute | solution.py:497
  77.3 5.8 %front.5 = (bf16[4,512,1024]{2,1,0:T(8,128)(2,1)S(1)}, bf16[512,1024]{1,0:T(8,128)(2,1)S(1)}, bf16[512,256]{1,0:T(8,128)(2,1)S(1)}, bf16[512,1024]{1,0:T(8,128)(...) custom-call(s32[3]{0:T(128)S(1)} %pad_add_fusion.where_ref, bf16[128,1024]{1,0:T(8,128)(2,1)S(1)} %pad_maximum_fusion.1.piece0, ...), custom_call_target="tpu_custom_call" | custom-call | flops 6700000256 | bytes 12000000 | tf_op jit(solution)/shard_map/front/pallas_call | solution.py:179
  83.3 5.9 %front.7 = (bf16[4,512,1024]{2,1,0:T(8,128)(2,1)S(1)}, bf16[512,1024]{1,0:T(8,128)(2,1)S(1)}, bf16[512,256]{1,0:T(8,128)(2,1)S(1)}, bf16[512,1024]{1,0:T(8,128)(...) custom-call(s32[3]{0:T(128)S(1)} %pad_add_fusion.where_ref, bf16[128,1024]{1,0:T(8,128)(2,1)S(1)} %pad_maximum_fusion.2.piece0, ...), custom_call_target="tpu_custom_call" | custom-call | flops 6700000256 | bytes 12000000 | tf_op jit(solution)/shard_map/front/pallas_call | solution.py:179
  89.2 1.7 %collective-permute-done.15.piece3 = bf16[128,1024]{1,0:T(8,128)(2,1)S(1)} collective-permute-done((bf16[128,1024]{1,0:T(8,128)(2,1)S(1)}, bf16[128,1024]{1,0:T(8,128)(2,1)S(1)}, u32[]{:S(2)}, u32[]{:S(2)}) %collective-permute-start.15) | collective-permute-done | bytes 262176 | tf_op jit(solution)/shard_map/ppermute | solution.py:498
  90.9 5.9 %front.6 = (bf16[4,512,1024]{2,1,0:T(8,128)(2,1)S(1)}, bf16[512,1024]{1,0:T(8,128)(2,1)S(1)}, bf16[512,256]{1,0:T(8,128)(2,1)S(1)}, bf16[512,1024]{1,0:T(8,128)(...) custom-call(s32[3]{0:T(128)S(1)} %pad_add_fusion.where_ref, bf16[128,1024]{1,0:T(8,128)(2,1)S(1)} %pad_maximum_fusion.piece0, ...), custom_call_target="tpu_custom_call" | custom-call | flops 6700000256 | bytes 12000000 | tf_op jit(solution)/shard_map/front/pallas_call | solution.py:179
  96.8 1.1 fusion.28
  98.0 1.5 products.3
  99.5 9.7 %collective-permute-start.19 = (bf16[1,128,1024]{2,1,0:T(8,128)(2,1)S(1)}, bf16[1,128,1024]{2,1,0:T(8,128)(2,1)S(1)}, u32[]{:S(2)}, u32[]{:S(2)}) collective-permute-start(bf16[1,128,1024]{2,1,0:T(8,128)(2,1)S(1)} %constant_dynamic-slice_fusion.2), channel_id=1, source_target_pairs={{0,1},{1,0},{2,3},{3,2},{4,5},{5,4},{6,7},{7,6},{8,9},{9,8},{10,11... | collective-permute-start | bytes 786440 | tf_op jit(solution)/shard_map/ppermute | solution.py:519
  109.4 0.8 collective-permute-start.23
  110.2 1.3 collective-permute-start.24
  111.6 0.8 collective-permute-start.20
  112.4 3.1 %products.4 = bf16[2,256,1024]{2,1,0:T(8,128)(2,1)S(1)} custom-call(bf16[512,1024]{1,0:T(8,128)(2,1)S(1)} %get-tuple-element.161.refs_0_.dz_ref, bf16[512,1024]{1,0:T(8,128)(2,1)S(1)} %get-tuple-element.172.refs_1_.dz_ref, bf16[512,1024]{1,0:T(8,128)(2,1)S(1)} %get-tuple-element.177.refs_2_.dz_ref, bf16[512,1024]{1,0:T(8,128)(2,1)S(1)} %get-tuple-element.185.refs_3_.dz_ref, ...), custom_call_target="tpu_custom_call" | custom-call | flops 4400000000 | bytes 10000000 | tf_op jit(solution)/shard_map/products/pallas_call | solution.py:265
  115.5 4.4 %collective-permute-done.20 = bf16[1,128,1024]{2,1,0:T(8,128)(2,1)S(1)} collective-permute-done((bf16[1,128,1024]{2,1,0:T(8,128)(2,1)S(1)}, bf16[1,128,1024]{2,1,0:T(8,128)(2,1)S(1)}, u32[]{:S(2)}, u32[]{:S(2)}) %collective-permute-start.20) | collective-permute-done | bytes 262176 | tf_op jit(solution)/shard_map/ppermute | solution.py:523
  120.0 0.9 collective-permute-start.21
  120.9 3.1 %products.5 = bf16[2,256,1024]{2,1,0:T(8,128)(2,1)S(1)} custom-call(bf16[512,1024]{1,0:T(8,128)(2,1)S(1)} %get-tuple-element.161.refs_0_.dz_ref, bf16[512,1024]{1,0:T(8,128)(2,1)S(1)} %get-tuple-element.172.refs_1_.dz_ref, bf16[512,1024]{1,0:T(8,128)(2,1)S(1)} %get-tuple-element.177.refs_2_.dz_ref, bf16[512,1024]{1,0:T(8,128)(2,1)S(1)} %get-tuple-element.185.refs_3_.dz_ref, ...), custom_call_target="tpu_custom_call" | custom-call | flops 4400000000 | bytes 10000000 | tf_op jit(solution)/shard_map/products/pallas_call | solution.py:265
  124.5 0.8 collective-permute-start.27
  125.3 3.8 %taps.4 = f32[32,1024]{1,0:T(8,128)S(1)} custom-call(bf16[4,512,1024]{2,1,0:T(8,128)(2,1)S(1)} %get-tuple-element.147.refs_4_.maps_ref, bf16[512,1024]{1,0:T(8,128)(2,1)S(1)} %get-tuple-element.161.refs_0_.dz_ref, bf16[3,256,1024]{2,1,0:T(8,128)(2,1)S(1)} %copy-done.2), custom_call_target="tpu_custom_call" | custom-call | flops 4499999744 | bytes 4000000 | tf_op jit(solution)/shard_map/taps/pallas_call | solution.py:224
  129.3 3.8 %taps.5 = f32[32,1024]{1,0:T(8,128)S(1)} custom-call(bf16[4,512,1024]{2,1,0:T(8,128)(2,1)S(1)} %get-tuple-element.148.refs_5_.maps_ref, bf16[512,1024]{1,0:T(8,128)(2,1)S(1)} %get-tuple-element.172.refs_1_.dz_ref, bf16[3,256,1024]{2,1,0:T(8,128)(2,1)S(1)} %copy-done.2), custom_call_target="tpu_custom_call" | custom-call | flops 4499999744 | bytes 4000000 | tf_op jit(solution)/shard_map/taps/pallas_call | solution.py:224
  133.1 0.8 collective-permute-start.28
  133.9 0.7 collective-permute-start.26
  134.6 3.8 %taps.6 = f32[32,1024]{1,0:T(8,128)S(1)} custom-call(bf16[4,512,1024]{2,1,0:T(8,128)(2,1)S(1)} %get-tuple-element.149.refs_6_.maps_ref, bf16[512,1024]{1,0:T(8,128)(2,1)S(1)} %get-tuple-element.177.refs_2_.dz_ref, bf16[3,256,1024]{2,1,0:T(8,128)(2,1)S(1)} %copy-done.2), custom_call_target="tpu_custom_call" | custom-call | flops 4499999744 | bytes 4000000 | tf_op jit(solution)/shard_map/taps/pallas_call | solution.py:224
  138.7 3.8 %taps.7 = f32[32,1024]{1,0:T(8,128)S(1)} custom-call(bf16[4,512,1024]{2,1,0:T(8,128)(2,1)S(1)} %get-tuple-element.150.refs_7_.maps_ref, bf16[512,1024]{1,0:T(8,128)(2,1)S(1)} %get-tuple-element.185.refs_3_.dz_ref, bf16[3,256,1024]{2,1,0:T(8,128)(2,1)S(1)} %copy-done.2), custom_call_target="tpu_custom_call" | custom-call | flops 4499999744 | bytes 4000000 | tf_op jit(solution)/shard_map/taps/pallas_call | solution.py:224
  142.6 1.3 collective-permute-start.29
  144.1 0.8 collective-permute-done.29
  144.9 0.8 collective-permute-start.30
  145.7 0.5 fetch.1
  146.3 4.7 %collective-permute-done.30 = bf16[48,1024]{1,0:T(8,128)(2,1)S(1)} collective-permute-done((bf16[48,1024]{1,0:T(8,128)(2,1)S(1)}, bf16[48,1024]{1,0:T(8,128)(2,1)S(1)}, u32[]{:S(2)}, u32[]{:S(2)}) %collective-permute-start.30) | collective-permute-done | bytes 98336 | tf_op jit(solution)/shard_map/ppermute | solution.py:529
  151.2 1.3 collective-permute-start.32
  153.3 0.8 collective-permute-done.32.rest2
  154.0 0.7 collective-permute-done.31.rest1
  154.8 6.3 %update.1 = (f32[1,256,1024]{2,1,0:T(8,128)}, f32[1,3,256,1024]{3,2,1,0:T(8,128)}, f32[1,256,2048]{2,1,0:T(8,128)}, f32[1,256,1280]{2,1,0:T(8,128)}, f32[27,1,10...) custom-call(s32[1]{0:T(128)} %bitcast.core_ref, ...), custom_call_target="tpu_custom_call" | custom-call | flops 4000000 | bytes 20000000 | tf_op jit(solution)/shard_map/update/pallas_call | solution.py:445
  (135 shorter events, 4.2 us)
Async XLA Ops:
  0.6 13.8 %copy-start.15 = (s32[4]{0:T(128)S(1)}, s32[4]{0:T(128)}, u32[]{:S(2)}) copy-start(s32[4]{0:T(128)} %param.17) | copy-start | bytes 52
  0.7 21.0 %copy-start = (f32[1,3,256,1024]{3,2,1,0:T(8,128)S(1)}, f32[1,3,256,1024]{3,2,1,0:T(8,128)}, u32[]{:S(2)}) copy-start(f32[1,3,256,1024]{3,2,1,0:T(8,128)} %refs_1_) | copy-start | bytes 9437188
  3.1 28.2 %all-to-all-start = ((bf16[32,16,1024]{2,1,0:T(8,128)(2,1)}), bf16[32,16,1024]{2,1,0:T(8,128)(2,1)}, u32[]{:S(2)}, u32[]{:S(2)}) async-start(bf16[32,16,1024]{2,1,0:T(8,128)(2,1)} %bitcast.73), calls=%async_computation | async-start | bytes 2097152 | tf_op jit(solution)/shard_map/all_to_all | solution.py:566
  21.7 1.4 copy-start.5
  21.7 2.3 %copy-start.13 = (f32[1,19]{1,0:T(1,128)S(1)}, f32[1,19]{1,0:T(1,128)}, u32[]{:S(2)}) copy-start(f32[1,19]{1,0:T(1,128)} %b_class.1) | copy-start | bytes 232
  26.6 3.6 %copy-start.3 = (f32[1,256,1280]{2,1,0:T(8,128)S(1)}, f32[1,256,1280]{2,1,0:T(8,128)}, u32[]{:S(2)}) copy-start(f32[1,256,1280]{2,1,0:T(8,128)} %refs_3_) | copy-start | bytes 3932164
  30.2 5.2 %copy-start.11 = (f32[1,5,256]{2,0,1:T(1,128)S(1)}, f32[1,5,256]{2,0,1:T(1,128)}, u32[]{:S(2)}) copy-start(f32[1,5,256]{2,0,1:T(1,128)} %param.23) | copy-start | bytes 15364
  30.2 7.0 %copy-start.10 = (f32[1,19,256]{2,0,1:T(1,128)S(1)}, f32[1,19,256]{2,0,1:T(1,128)}, u32[]{:S(2)}) copy-start(f32[1,19,256]{2,0,1:T(1,128)} %param.26) | copy-start | bytes 58372
  32.8 5.7 %collective-permute-start = (bf16[72,1024]{1,0:T(8,128)(2,1)}, bf16[72,1024]{1,0:T(8,128)(2,1)S(1)}, u32[]{:S(2)}, u32[]{:S(2)}) collective-permute-start(bf16[72,1024]{1,0:T(8,128)(2,1)} %pad_maximum_fusion.5), channel_id=1, source_target_pairs={{0,64},{4,68},{8,72},{12,76},{16,80},{20,84},{24,88},{28,92},{32,9... | collective-permute-start | bytes 442376 | tf_op jit(solution)/shard_map/ppermute | solution.py:573
  38.6 6.9 %collective-permute-start.7 = (bf16[64,1024]{1,0:T(8,128)(2,1)S(1)}, bf16[64,1024]{1,0:T(8,128)(2,1)S(1)}, u32[]{:S(2)}, u32[]{:S(2)}) collective-permute-start(bf16[64,1024]{1,0:T(8,128)(2,1)S(1)} %bitcast.84), channel_id=1, source_target_pairs={{0,4},{4,8},{8,12},{12,0},{16,20},{20,24},{24,28},{28,16},{32,36},... | collective-permute-start | bytes 393224 | tf_op jit(solution)/shard_map/ppermute | solution.py:496
  39.6 7.5 %collective-permute-start.8 = (bf16[64,1024]{1,0:T(8,128)(2,1)S(1)}, bf16[64,1024]{1,0:T(8,128)(2,1)S(1)}, u32[]{:S(2)}, u32[]{:S(2)}) collective-permute-start(bf16[64,1024]{1,0:T(8,128)(2,1)S(1)} %bitcast.85), channel_id=1, source_target_pairs={{0,12},{4,0},{8,4},{12,8},{16,28},{20,16},{24,20},{28,24},{32,44},... | collective-permute-start | bytes 393224 | tf_op jit(solution)/shard_map/ppermute | solution.py:497
  41.4 6.3 %collective-permute-start.9 = (bf16[64,1024]{1,0:T(8,128)(2,1)S(1)}, bf16[64,1024]{1,0:T(8,128)(2,1)S(1)}, u32[]{:S(2)}, u32[]{:S(2)}) collective-permute-start(bf16[64,1024]{1,0:T(8,128)(2,1)S(1)} %bitcast.86), channel_id=1, source_target_pairs={{0,8},{4,12},{8,0},{12,4},{16,24},{20,28},{24,16},{28,20},{32,40},... | collective-permute-start | bytes 393224 | tf_op jit(solution)/shard_map/ppermute | solution.py:498
  42.6 19.4 %copy-start.14 = (bf16[256,2048]{1,0:T(8,128)(2,1)S(1)}, bf16[256,2048]{1,0:T(8,128)(2,1)}, u32[]{:S(2)}) copy-start(bf16[256,2048]{1,0:T(8,128)(2,1)} %convert_bitcast_fusion.1) | copy-start | bytes 3145732
  42.8 5.6 %collective-permute-start.1 = (bf16[72,1024]{1,0:T(8,128)(2,1)S(1)}, bf16[72,1024]{1,0:T(8,128)(2,1)S(1)}, u32[]{:S(2)}, u32[]{:S(2)}) collective-permute-start(bf16[72,1024]{1,0:T(8,128)(2,1)S(1)} %pad_maximum_fusion.6), channel_id=1, source_target_pairs={{0,16},{4,20},{8,24},{12,28},{16,32},{20,36},{24,40},{28,44},{32,4... | collective-permute-start | bytes 442376 | tf_op jit(solution)/shard_map/ppermute | solution.py:496
  44.0 4.3 %collective-permute-start.2 = (bf16[72,1024]{1,0:T(8,128)(2,1)S(1)}, bf16[72,1024]{1,0:T(8,128)(2,1)S(1)}, u32[]{:S(2)}, u32[]{:S(2)}) collective-permute-start(bf16[72,1024]{1,0:T(8,128)(2,1)S(1)} %pad_maximum_fusion.6), channel_id=1, source_target_pairs={{0,48},{4,52},{8,56},{12,60},{16,0},{20,4},{24,8},{28,12},{32,16},... | collective-permute-start | bytes 442376 | tf_op jit(solution)/shard_map/ppermute | solution.py:497
  45.5 16.8 %slice-start = ((f32[1,5,256]{2,0,1:T(1,128)}), f32[1,1,256]{2,0,1:T(1,128)S(1)}, s32[]{:S(2)}) async-start(f32[1,5,256]{2,0,1:T(1,128)} %param.23), calls=%async_computation.1 | async-start | bytes 2048 | tf_op jit(solution)/shard_map/slice | solution.py:611
  45.5 5.9 %collective-permute-start.3 = (bf16[72,1024]{1,0:T(8,128)(2,1)S(1)}, bf16[72,1024]{1,0:T(8,128)(2,1)S(1)}, u32[]{:S(2)}, u32[]{:S(2)}) collective-permute-start(bf16[72,1024]{1,0:T(8,128)(2,1)S(1)} %pad_maximum_fusion.6), channel_id=1, source_target_pairs={{0,32},{4,36},{8,40},{12,44},{16,48},{20,52},{24,56},{28,60},{32,0... | collective-permute-start | bytes 442376 | tf_op jit(solution)/shard_map/ppermute | solution.py:498
  47.1 15.5 %copy-start.12 = (f32[1,256]{1,0:T(1,128)S(1)}, f32[1,256]{1,0:T(1,128)}, u32[]{:S(2)}) copy-start(f32[1,256]{1,0:T(1,128)} %b_proj.1) | copy-start | bytes 3076
  47.1 16.5 %copy-start.2 = (bf16[3,256,1024]{2,1,0:T(8,128)(2,1)S(1)}, bf16[3,256,1024]{2,1,0:T(8,128)(2,1)}, u32[]{:S(2)}) copy-start(bf16[3,256,1024]{2,1,0:T(8,128)(2,1)} %convert_bitcast_fusion.w_point) | copy-start | bytes 4718596
  47.2 16.5 %copy-start.7 = (bf16[256,1024]{1,0:T(8,128)(2,1)S(1)}, bf16[256,1024]{1,0:T(8,128)(2,1)}, u32[]{:S(2)}) copy-start(bf16[256,1024]{1,0:T(8,128)(2,1)} %convert_bitcast_fusion.3.w_plain) | copy-start | bytes 1572868
  47.2 16.5 %copy-start.8 = (bf16[256,1024]{1,0:T(8,128)(2,1)S(1)}, bf16[256,1024]{1,0:T(8,128)(2,1)}, u32[]{:S(2)}) copy-start(bf16[256,1024]{1,0:T(8,128)(2,1)} %slice.251.w_proj) | copy-start | bytes 1572868
  47.2 16.5 %copy-start.9 = (f32[1,3,9,1024]{3,0,2,1:T(1,128)S(1)}, f32[1,3,9,1024]{3,0,2,1:T(1,128)}, u32[]{:S(2)}) copy-start(f32[1,3,9,1024]{3,0,2,1:T(1,128)} %param.20) | copy-start | bytes 331780
  51.4 6.7 %collective-permute-start.4 = (bf16[136,1024]{1,0:T(8,128)(2,1)S(1)}, bf16[136,1024]{1,0:T(8,128)(2,1)S(1)}, u32[]{:S(2)}, u32[]{:S(2)}) collective-permute-start(bf16[136,1024]{1,0:T(8,128)(2,1)S(1)} %get-tuple-element.115.piece0), channel_id=1, source_target_pairs={{0,4},{4,8},{8,12},{12,0},{16,20},{20,24},{24,28},{28,16},{32,36},... | collective-permute-start | bytes 835592 | tf_op jit(solution)/shard_map/ppermute | solution.py:496
  51.6 9.1 %collective-permute-start.5 = (bf16[136,1024]{1,0:T(8,128)(2,1)S(1)}, bf16[136,1024]{1,0:T(8,128)(2,1)S(1)}, u32[]{:S(2)}, u32[]{:S(2)}) collective-permute-start(bf16[136,1024]{1,0:T(8,128)(2,1)S(1)} %get-tuple-element.115.piece0), channel_id=1, source_target_pairs={{0,12},{4,0},{8,4},{12,8},{16,28},{20,16},{24,20},{28,24},{32,44},... | collective-permute-start | bytes 835592 | tf_op jit(solution)/shard_map/ppermute | solution.py:497
  54.2 7.9 %collective-permute-start.6 = (bf16[136,1024]{1,0:T(8,128)(2,1)S(1)}, bf16[136,1024]{1,0:T(8,128)(2,1)S(1)}, u32[]{:S(2)}, u32[]{:S(2)}) collective-permute-start(bf16[136,1024]{1,0:T(8,128)(2,1)S(1)} %get-tuple-element.115.piece0), channel_id=1, source_target_pairs={{0,8},{4,12},{8,0},{12,4},{16,24},{20,28},{24,16},{28,20},{32,40},... | collective-permute-start | bytes 835592 | tf_op jit(solution)/shard_map/ppermute | solution.py:498
  54.4 15.2 %collective-permute-start.10 = (bf16[128,1024]{1,0:T(8,128)(2,1)S(1)}, bf16[128,1024]{1,0:T(8,128)(2,1)S(1)}, u32[]{:S(2)}, u32[]{:S(2)}) collective-permute-start(bf16[128,1024]{1,0:T(8,128)(2,1)S(1)} %pad_maximum_fusion.1.piece0), channel_id=1, source_target_pairs={{0,16},{4,20},{8,24},{12,28},{16,32},{20,36},{24,40},{28,44},{32,4... | collective-permute-start | bytes 786440 | tf_op jit(solution)/shard_map/ppermute | solution.py:496
  54.5 15.1 %collective-permute-start.11 = (bf16[128,1024]{1,0:T(8,128)(2,1)S(1)}, bf16[128,1024]{1,0:T(8,128)(2,1)S(1)}, u32[]{:S(2)}, u32[]{:S(2)}) collective-permute-start(bf16[128,1024]{1,0:T(8,128)(2,1)S(1)} %pad_maximum_fusion.1.piece0), channel_id=1, source_target_pairs={{0,48},{4,52},{8,56},{12,60},{16,0},{20,4},{24,8},{28,12},{32,16},... | collective-permute-start | bytes 786440 | tf_op jit(solution)/shard_map/ppermute | solution.py:497
  58.1 11.5 %collective-permute-start.12 = (bf16[128,1024]{1,0:T(8,128)(2,1)S(1)}, bf16[128,1024]{1,0:T(8,128)(2,1)S(1)}, u32[]{:S(2)}, u32[]{:S(2)}) collective-permute-start(bf16[128,1024]{1,0:T(8,128)(2,1)S(1)} %pad_maximum_fusion.1.piece0), channel_id=1, source_target_pairs={{0,32},{4,36},{8,40},{12,44},{16,48},{20,52},{24,56},{28,60},{32,0... | collective-permute-start | bytes 786440 | tf_op jit(solution)/shard_map/ppermute | solution.py:498
  69.6 13.6 %collective-permute-start.16 = (bf16[128,1024]{1,0:T(8,128)(2,1)S(1)}, bf16[128,1024]{1,0:T(8,128)(2,1)S(1)}, u32[]{:S(2)}, u32[]{:S(2)}) collective-permute-start(bf16[128,1024]{1,0:T(8,128)(2,1)S(1)} %pad_maximum_fusion.2.piece0), channel_id=1, source_target_pairs={{0,16},{4,20},{8,24},{12,28},{16,32},{20,36},{24,40},{28,44},{32,4... | collective-permute-start | bytes 786440 | tf_op jit(solution)/shard_map/ppermute | solution.py:496
  70.1 13.2 %collective-permute-start.17 = (bf16[128,1024]{1,0:T(8,128)(2,1)S(1)}, bf16[128,1024]{1,0:T(8,128)(2,1)S(1)}, u32[]{:S(2)}, u32[]{:S(2)}) collective-permute-start(bf16[128,1024]{1,0:T(8,128)(2,1)S(1)} %pad_maximum_fusion.2.piece0), channel_id=1, source_target_pairs={{0,48},{4,52},{8,56},{12,60},{16,0},{20,4},{24,8},{28,12},{32,16},... | collective-permute-start | bytes 786440 | tf_op jit(solution)/shard_map/ppermute | solution.py:497
  72.4 11.0 %collective-permute-start.18 = (bf16[128,1024]{1,0:T(8,128)(2,1)S(1)}, bf16[128,1024]{1,0:T(8,128)(2,1)S(1)}, u32[]{:S(2)}, u32[]{:S(2)}) collective-permute-start(bf16[128,1024]{1,0:T(8,128)(2,1)S(1)} %pad_maximum_fusion.2.piece0), channel_id=1, source_target_pairs={{0,32},{4,36},{8,40},{12,44},{16,48},{20,52},{24,56},{28,60},{32,0... | collective-permute-start | bytes 786440 | tf_op jit(solution)/shard_map/ppermute | solution.py:498
  74.7 14.6 %collective-permute-start.13 = (bf16[128,1024]{1,0:T(8,128)(2,1)S(1)}, bf16[128,1024]{1,0:T(8,128)(2,1)S(1)}, u32[]{:S(2)}, u32[]{:S(2)}) collective-permute-start(bf16[128,1024]{1,0:T(8,128)(2,1)S(1)} %pad_maximum_fusion.piece0), channel_id=1, source_target_pairs={{0,4},{4,8},{8,12},{12,0},{16,20},{20,24},{24,28},{28,16},{32,36},... | collective-permute-start | bytes 786440 | tf_op jit(solution)/shard_map/ppermute | solution.py:496
  74.7 14.6 %collective-permute-start.14 = (bf16[128,1024]{1,0:T(8,128)(2,1)S(1)}, bf16[128,1024]{1,0:T(8,128)(2,1)S(1)}, u32[]{:S(2)}, u32[]{:S(2)}) collective-permute-start(bf16[128,1024]{1,0:T(8,128)(2,1)S(1)} %pad_maximum_fusion.piece0), channel_id=1, source_target_pairs={{0,12},{4,0},{8,4},{12,8},{16,28},{20,16},{24,20},{28,24},{32,44},... | collective-permute-start | bytes 786440 | tf_op jit(solution)/shard_map/ppermute | solution.py:497
  83.2 7.7 %collective-permute-start.15 = (bf16[128,1024]{1,0:T(8,128)(2,1)S(1)}, bf16[128,1024]{1,0:T(8,128)(2,1)S(1)}, u32[]{:S(2)}, u32[]{:S(2)}) collective-permute-start(bf16[128,1024]{1,0:T(8,128)(2,1)S(1)} %pad_maximum_fusion.piece0), channel_id=1, source_target_pairs={{0,8},{4,12},{8,0},{12,4},{16,24},{20,28},{24,16},{28,20},{32,40},... | collective-permute-start | bytes 786440 | tf_op jit(solution)/shard_map/ppermute | solution.py:498
  99.5 11.9 %collective-permute-start.19 = (bf16[1,128,1024]{2,1,0:T(8,128)(2,1)S(1)}, bf16[1,128,1024]{2,1,0:T(8,128)(2,1)S(1)}, u32[]{:S(2)}, u32[]{:S(2)}) collective-permute-start(bf16[1,128,1024]{2,1,0:T(8,128)(2,1)S(1)} %constant_dynamic-slice_fusion.2), channel_id=1, source_target_pairs={{0,1},{1,0},{2,3},{3,2},{4,5},{5,4},{6,7},{7,6},{8,9},{9,8},{10,11... | collective-permute-start | bytes 786440 | tf_op jit(solution)/shard_map/ppermute | solution.py:519
  109.3 15.0 %collective-permute-start.22 = (f32[4,2816]{1,0:T(4,128)S(1)}, f32[4,2816]{1,0:T(4,128)S(1)}, u32[]{:S(2)}, u32[]{:S(2)}) collective-permute-start(f32[4,2816]{1,0:T(4,128)S(1)} %constant_dynamic-update-slice_fusion.2), channel_id=1, source_target_pairs={{0,1},{1,0},{2,3},{3,2},{4,5},{5,4},{6,7},{7,6},{8,9},{9,8},{10,11... | collective-permute-start | bytes 135176 | tf_op jit(solution)/shard_map/ppermute | solution.py:504
  109.4 14.9 %collective-permute-start.23 = (f32[4,2816]{1,0:T(4,128)S(1)}, f32[4,2816]{1,0:T(4,128)S(1)}, u32[]{:S(2)}, u32[]{:S(2)}) collective-permute-start(f32[4,2816]{1,0:T(4,128)S(1)} %constant_dynamic-update-slice_fusion.2), channel_id=1, source_target_pairs={{0,2},{1,3},{2,0},{3,1},{4,6},{5,7},{6,4},{7,5},{8,10},{9,11},{10,... | collective-permute-start | bytes 135176 | tf_op jit(solution)/shard_map/ppermute | solution.py:504
  110.2 14.1 %collective-permute-start.24 = (f32[4,2816]{1,0:T(4,128)S(1)}, f32[4,2816]{1,0:T(4,128)S(1)}, u32[]{:S(2)}, u32[]{:S(2)}) collective-permute-start(f32[4,2816]{1,0:T(4,128)S(1)} %constant_dynamic-update-slice_fusion.2), channel_id=1, source_target_pairs={{0,3},{1,2},{2,1},{3,0},{4,7},{5,6},{6,5},{7,4},{8,11},{9,10},{10,... | collective-permute-start | bytes 135176 | tf_op jit(solution)/shard_map/ppermute | solution.py:504
  111.6 8.3 %collective-permute-start.20 = (bf16[1,128,1024]{2,1,0:T(8,128)(2,1)S(1)}, bf16[1,128,1024]{2,1,0:T(8,128)(2,1)S(1)}, u32[]{:S(2)}, u32[]{:S(2)}) collective-permute-start(bf16[1,128,1024]{2,1,0:T(8,128)(2,1)S(1)} %add_convert_fusion.5), channel_id=1, source_target_pairs={{0,2},{1,3},{2,0},{3,1},{4,6},{5,7},{6,4},{7,5},{8,10},{9,11},{10,... | collective-permute-start | bytes 786440 | tf_op jit(solution)/shard_map/ppermute | solution.py:523
  120.0 4.0 %collective-permute-start.21 = (bf16[2,128,1024]{2,1,0:T(8,128)(2,1)S(1)}, bf16[2,128,1024]{2,1,0:T(8,128)(2,1)S(1)}, u32[]{:S(2)}, u32[]{:S(2)}) collective-permute-start(bf16[2,128,1024]{2,1,0:T(8,128)(2,1)S(1)} %constant_dynamic-slice_fusion.1), channel_id=1, source_target_pairs={{0,1},{1,0},{2,3},{3,2},{4,5},{5,4},{6,7},{7,6},{8,9},{9,8},{10,11... | collective-permute-start | bytes 1572872 | tf_op jit(solution)/shard_map/ppermute | solution.py:519
  124.3 4.8 %collective-permute-start.25 = (bf16[2,128,1024]{2,1,0:T(8,128)(2,1)S(1)}, bf16[2,128,1024]{2,1,0:T(8,128)(2,1)S(1)}, u32[]{:S(2)}, u32[]{:S(2)}) collective-permute-start(bf16[2,128,1024]{2,1,0:T(8,128)(2,1)S(1)} %constant_dynamic-slice_fusion), channel_id=1, source_target_pairs={{0,1},{1,0},{2,3},{3,2},{4,5},{5,4},{6,7},{7,6},{8,9},{9,8},{10,11... | collective-permute-start | bytes 1572872 | tf_op jit(solution)/shard_map/ppermute | solution.py:519
  124.5 14.0 %collective-permute-start.27 = (bf16[2,128,1024]{2,1,0:T(8,128)(2,1)S(1)}, bf16[2,128,1024]{2,1,0:T(8,128)(2,1)S(1)}, u32[]{:S(2)}, u32[]{:S(2)}) collective-permute-start(bf16[2,128,1024]{2,1,0:T(8,128)(2,1)S(1)} %add_convert_fusion.3), channel_id=1, source_target_pairs={{0,2},{1,3},{2,0},{3,1},{4,6},{5,7},{6,4},{7,5},{8,10},{9,11},{10,... | collective-permute-start | bytes 1572872 | tf_op jit(solution)/shard_map/ppermute | solution.py:523
  133.1 5.5 %collective-permute-start.28 = (bf16[1,128,1024]{2,1,0:T(8,128)(2,1)S(1)}, bf16[1,128,1024]{2,1,0:T(8,128)(2,1)S(1)}, u32[]{:S(2)}, u32[]{:S(2)}) collective-permute-start(bf16[1,128,1024]{2,1,0:T(8,128)(2,1)S(1)} %add_convert_fusion.4.mine0), channel_id=1, source_target_pairs={{0,1},{1,0},{2,3},{3,2},{4,5},{5,4},{6,7},{7,6},{8,9},{9,8},{10,11... | collective-permute-start | bytes 786440 | tf_op jit(solution)/shard_map/ppermute | solution.py:657
  133.9 17.1 %collective-permute-start.26 = (bf16[2,128,1024]{2,1,0:T(8,128)(2,1)S(1)}, bf16[2,128,1024]{2,1,0:T(8,128)(2,1)S(1)}, u32[]{:S(2)}, u32[]{:S(2)}) collective-permute-start(bf16[2,128,1024]{2,1,0:T(8,128)(2,1)S(1)} %add_convert_fusion.2), channel_id=1, source_target_pairs={{0,2},{1,3},{2,0},{3,1},{4,6},{5,7},{6,4},{7,5},{8,10},{9,11},{10,... | collective-permute-start | bytes 1572872 | tf_op jit(solution)/shard_map/ppermute | solution.py:675
  138.7 7.0 %copy-start.4 = (f32[1,256,1280]{2,1,0:T(8,128)S(1)}, f32[1,256,1280]{2,1,0:T(8,128)}, u32[]{:S(2)}) copy-start(f32[1,256,1280]{2,1,0:T(8,128)} %refs_3_) | copy-start | bytes 3932164
  138.7 7.0 %copy-start.6 = (f32[1,256,1024]{2,1,0:T(8,128)S(1)}, f32[1,256,1024]{2,1,0:T(8,128)}, u32[]{:S(2)}) copy-start(f32[1,256,1024]{2,1,0:T(8,128)} %refs_0_) | copy-start | bytes 3145732
  142.6 3.2 %copy-start.1 = (f32[1,256,2048]{2,1,0:T(8,128)S(1)}, f32[1,256,2048]{2,1,0:T(8,128)}, u32[]{:S(2)}) copy-start(f32[1,256,2048]{2,1,0:T(8,128)} %refs_2_) | copy-start | bytes 6291460
  142.6 2.2 %collective-permute-start.29 = (bf16[48,1024]{1,0:T(8,128)(2,1)S(1)}, bf16[48,1024]{1,0:T(8,128)(2,1)S(1)}, u32[]{:S(2)}, u32[]{:S(2)}) collective-permute-start(bf16[48,1024]{1,0:T(8,128)(2,1)S(1)} %maximum_maximum_fusion), channel_id=1, source_target_pairs={{0,1},{1,0},{2,3},{3,2},{4,5},{5,4},{6,7},{7,6},{8,9},{9,8},{10,11... | collective-permute-start | bytes 294920 | tf_op jit(solution)/shard_map/ppermute | solution.py:527
  144.9 6.0 %collective-permute-start.30 = (bf16[48,1024]{1,0:T(8,128)(2,1)S(1)}, bf16[48,1024]{1,0:T(8,128)(2,1)S(1)}, u32[]{:S(2)}, u32[]{:S(2)}) collective-permute-start(bf16[48,1024]{1,0:T(8,128)(2,1)S(1)} %add_convert_fusion.6), channel_id=1, source_target_pairs={{0,2},{1,3},{2,0},{3,1},{4,6},{5,7},{6,4},{7,5},{8,10},{9,11},{10,... | collective-permute-start | bytes 294920 | tf_op jit(solution)/shard_map/ppermute | solution.py:529
  151.2 2.9 %collective-permute-start.32 = (bf16[2,128,1024]{2,1,0:T(8,128)(2,1)S(1)}, bf16[2,128,1024]{2,1,0:T(8,128)(2,1)S(1)}, u32[]{:S(2)}, u32[]{:S(2)}) collective-permute-start(bf16[2,128,1024]{2,1,0:T(8,128)(2,1)S(1)} %add_convert_fusion.mine2), channel_id=1, source_target_pairs={{0,1},{1,0},{2,3},{3,2},{4,5},{5,4},{6,7},{7,6},{8,9},{9,8},{10,11... | collective-permute-start | bytes 1572872 | tf_op jit(solution)/shard_map/ppermute | solution.py:680
  152.5 2.3 %collective-permute-start.31 = (bf16[2,128,1024]{2,1,0:T(8,128)(2,1)S(1)}, bf16[2,128,1024]{2,1,0:T(8,128)(2,1)S(1)}, u32[]{:S(2)}, u32[]{:S(2)}) collective-permute-start(bf16[2,128,1024]{2,1,0:T(8,128)(2,1)S(1)} %add_convert_fusion.1.mine1), channel_id=1, source_target_pairs={{0,1},{1,0},{2,3},{3,2},{4,5},{5,4},{6,7},{7,6},{8,9},{9,8},{10,11... | collective-permute-start | bytes 1572872 | tf_op jit(solution)/shard_map/ppermute | solution.py:680

commit v3 on v2

--- a/solution.py
+++ b/solution.py
@@ -276,7 +276,7 @@
     )(*lefts, *rights)
 
 
-STEPS = 4
+STEPS = 8
 
 
 def update_kernel(

time: 162 us -> 163 us (level)
  transfers between devices with their start and end apart: 34 -> 34, of which waited for: 14 -> 14; matrix products, arithmetic and copies ran while one was open for 8% -> 8% of each run, Pallas kernels for 25% -> 24%
where the time goes in v3:
time: 163 us; the launch traced here: 162 us
  starting transfers between devices  57.3 us (35%)
  Pallas kernels  54.1 us (33%)
  waiting for transfers between devices  21.3 us (13%)
  between operations  10.1 us (6%)
  other arithmetic  9.37 us (6%)
  local copies, waits for them, and re-layouts  7.18 us (4%)
  matrix products  2.65 us (2%)
    pallas_call x4, Pallas kernels, front(): pl.pallas_call(functools.partial(front_kernel, order), name='front', out_...  23.4 us
    pallas_call x4, Pallas kernels, depth_taps(): pl.pallas_call(taps_kernel, name='taps', grid=(channels // block,), out_s...  15.3 us
    ppermute x6, starting transfers between devices, gather_ring(): lax.ppermute(block, 'trial', along(-1))  13.4 us
    all_to_all x1, starting transfers between devices, on_device(): lax.all_to_all(own.reshape(32, 16, channels), 'trial', 0, 0, tiled=True)  11.3 us
    ppermute x3, starting transfers between devices, sum_cores(): lax.ppermute(other, 'batch', CORES).astype(F32)  10.7 us
    pallas_call x3, Pallas kernels, products(): pl.pallas_call(functools.partial(product_kernel, count, first), name='pro...  7.73 us
    ppermute x6, starting transfers between devices, gather_ring(): lax.ppermute(block, 'trial', along(2))  7.62 us
    pallas_call x1, Pallas kernels, update(): pl.pallas_call(update_kernel, name='update', out_shape=[jax.ShapeDtypeStr...  7.08 us
  transfers between devices with their start and end apart: 34, of which 14 were waited for; matrix products, arithmetic and copies ran while one was open for 8% of the time, Pallas kernels for 24%

profile of v3, /device:TPU:1, one launch (start us, length us, event | category | flops | bytes accessed | tf_op | source)
XLA Modules:
  0.0 162.0 jit_solution(17849663172101364750)
XLA Ops:
  0.7 2.4 %copy.31 = bf16[1,1,1024,512]{2,3,1,0:T(8,128)(2,1)} copy(bf16[1,1,1024,512]{3,2,1,0:T(8,128)(2,1)} %param.14) | data formatting | bytes 2097152 | tf_op args[0]
  3.1 11.3 %all-to-all-start = ((bf16[32,16,1024]{2,1,0:T(8,128)(2,1)}), bf16[32,16,1024]{2,1,0:T(8,128)(2,1)}, u32[]{:S(2)}, u32[]{:S(2)}) async-start(bf16[32,16,1024]{2,1,0:T(8,128)(2,1)} %bitcast.73), calls=%async_computation | async-start | bytes 2097152 | tf_op jit(solution)/shard_map/all_to_all | solution.py:566
  14.4 0.6 fusion.30
  20.3 1.3 convert_reduce_fusion
  21.7 1.4 convert_bitcast_fusion.w_point
  23.1 0.9 convert_bitcast_fusion.3.w_plain
  26.6 0.8 fusion.18
  27.5 2.7 %convert_bitcast_fusion.1 = bf16[256,2048]{1,0:T(8,128)(2,1)} fusion(f32[1,256,2048]{2,1,0:T(8,128)} %refs_2_), kind=kLoop, calls=%fused_computation.11 | loop fusion | flops 524288 | bytes 3145728 | tf_op jit(solution)/shard_map/convert_element_type | solution.py:607
  30.2 0.9 convert_bitcast_fusion.2
  31.3 0.8 constant_dynamic-slice_fusion.8
  32.2 0.7 pad_maximum_fusion.5
  32.8 2.5 %collective-permute-start = (bf16[72,1024]{1,0:T(8,128)(2,1)}, bf16[72,1024]{1,0:T(8,128)(2,1)S(1)}, u32[]{:S(2)}, u32[]{:S(2)}) collective-permute-start(bf16[72,1024]{1,0:T(8,128)(2,1)} %pad_maximum_fusion.5), channel_id=1, source_target_pairs={{0,64},{4,68},{8,72},{12,76},{16,80},{20,84},{24,88},{28,92},{32,9... | collective-permute-start | bytes 442376 | tf_op jit(solution)/shard_map/ppermute | solution.py:573
  35.4 1.9 %slice.251.w_proj = bf16[256,1024]{1,0:T(8,128)(2,1)} slice(bf16[256,1280]{1,0:T(8,128)(2,1)} %convert_bitcast_fusion.2), slice={[0:256], [0:1024]} | slice | bytes 1048576 | tf_op jit(solution)/shard_map/slice | solution.py:624
  37.4 1.2 collective-permute-done
  38.6 1.0 collective-permute-start.7
  39.6 1.7 %collective-permute-start.8 = (bf16[64,1024]{1,0:T(8,128)(2,1)S(1)}, bf16[64,1024]{1,0:T(8,128)(2,1)S(1)}, u32[]{:S(2)}, u32[]{:S(2)}) collective-permute-start(bf16[64,1024]{1,0:T(8,128)(2,1)S(1)} %bitcast.85), channel_id=1, source_target_pairs={{0,12},{4,0},{8,4},{12,8},{16,28},{20,16},{24,20},{28,24},{32,44},... | collective-permute-start | bytes 393224 | tf_op jit(solution)/shard_map/ppermute | solution.py:497
  41.4 1.2 collective-permute-start.9
  42.8 1.3 collective-permute-start.1
  44.0 1.5 collective-permute-start.2
  45.5 1.6 collective-permute-start.3
  47.2 0.4 collective-permute-done.9
  47.6 0.7 collective-permute-done.1
  48.4 3.0 %collective-permute-done.3 = bf16[72,1024]{1,0:T(8,128)(2,1)S(1)} collective-permute-done((bf16[72,1024]{1,0:T(8,128)(2,1)S(1)}, bf16[72,1024]{1,0:T(8,128)(2,1)S(1)}, u32[]{:S(2)}, u32[]{:S(2)}) %collective-permute-start.3) | collective-permute-done | bytes 147488 | tf_op jit(solution)/shard_map/ppermute | solution.py:498
  51.6 2.6 %collective-permute-start.5 = (bf16[136,1024]{1,0:T(8,128)(2,1)S(1)}, bf16[136,1024]{1,0:T(8,128)(2,1)S(1)}, u32[]{:S(2)}, u32[]{:S(2)}) collective-permute-start(bf16[136,1024]{1,0:T(8,128)(2,1)S(1)} %get-tuple-element.115.piece0), channel_id=1, source_target_pairs={{0,12},{4,0},{8,4},{12,8},{16,28},{20,16},{24,20},{28,24},{32,44},... | collective-permute-start | bytes 835592 | tf_op jit(solution)/shard_map/ppermute | solution.py:497
  54.5 2.7 %collective-permute-start.11 = (bf16[128,1024]{1,0:T(8,128)(2,1)S(1)}, bf16[128,1024]{1,0:T(8,128)(2,1)S(1)}, u32[]{:S(2)}, u32[]{:S(2)}) collective-permute-start(bf16[128,1024]{1,0:T(8,128)(2,1)S(1)} %pad_maximum_fusion.1.piece0), channel_id=1, source_target_pairs={{0,48},{4,52},{8,56},{12,60},{16,0},{20,4},{24,8},{28,12},{32,16},... | collective-permute-start | bytes 786440 | tf_op jit(solution)/shard_map/ppermute | solution.py:497
  57.2 0.9 collective-permute-done.4.piece1
  58.1 2.2 %collective-permute-start.12 = (bf16[128,1024]{1,0:T(8,128)(2,1)S(1)}, bf16[128,1024]{1,0:T(8,128)(2,1)S(1)}, u32[]{:S(2)}, u32[]{:S(2)}) collective-permute-start(bf16[128,1024]{1,0:T(8,128)(2,1)S(1)} %pad_maximum_fusion.1.piece0), channel_id=1, source_target_pairs={{0,32},{4,36},{8,40},{12,44},{16,48},{20,52},{24,56},{28,60},{32,0... | collective-permute-start | bytes 786440 | tf_op jit(solution)/shard_map/ppermute | solution.py:498
  60.7 1.4 collective-permute-done.6.piece3
  62.6 1.1 convolution_add_fusion
  63.7 5.9 %front.4 = (bf16[4,512,1024]{2,1,0:T(8,128)(2,1)S(1)}, bf16[512,1024]{1,0:T(8,128)(2,1)S(1)}, bf16[512,256]{1,0:T(8,128)(2,1)S(1)}, bf16[512,1024]{1,0:T(8,128)(...) custom-call(s32[3]{0:T(128)S(1)} %pad_add_fusion.where_ref, bf16[136,1024]{1,0:T(8,128)(2,1)S(1)} %get-tuple-element.115.piece0, ...), custom_call_target="tpu_custom_call" | custom-call | flops 6700000256 | bytes 12000000 | tf_op jit(solution)/shard_map/front/pallas_call | solution.py:179
  69.6 0.5 collective-permute-start.16
  70.1 2.3 %collective-permute-start.17 = (bf16[128,1024]{1,0:T(8,128)(2,1)S(1)}, bf16[128,1024]{1,0:T(8,128)(2,1)S(1)}, u32[]{:S(2)}, u32[]{:S(2)}) collective-permute-start(bf16[128,1024]{1,0:T(8,128)(2,1)S(1)} %pad_maximum_fusion.2.piece0), channel_id=1, source_target_pairs={{0,48},{4,52},{8,56},{12,60},{16,0},{20,4},{24,8},{28,12},{32,16},... | collective-permute-start | bytes 786440 | tf_op jit(solution)/shard_map/ppermute | solution.py:497
  72.4 2.3 %collective-permute-start.18 = (bf16[128,1024]{1,0:T(8,128)(2,1)S(1)}, bf16[128,1024]{1,0:T(8,128)(2,1)S(1)}, u32[]{:S(2)}, u32[]{:S(2)}) collective-permute-start(bf16[128,1024]{1,0:T(8,128)(2,1)S(1)} %pad_maximum_fusion.2.piece0), channel_id=1, source_target_pairs={{0,32},{4,36},{8,40},{12,44},{16,48},{20,52},{24,56},{28,60},{32,0... | collective-permute-start | bytes 786440 | tf_op jit(solution)/shard_map/ppermute | solution.py:498
  74.7 2.7 %collective-permute-start.14 = (bf16[128,1024]{1,0:T(8,128)(2,1)S(1)}, bf16[128,1024]{1,0:T(8,128)(2,1)S(1)}, u32[]{:S(2)}, u32[]{:S(2)}) collective-permute-start(bf16[128,1024]{1,0:T(8,128)(2,1)S(1)} %pad_maximum_fusion.piece0), channel_id=1, source_target_pairs={{0,12},{4,0},{8,4},{12,8},{16,28},{20,16},{24,20},{28,24},{32,44},... | collective-permute-start | bytes 786440 | tf_op jit(solution)/shard_map/ppermute | solution.py:497
  77.3 5.8 %front.5 = (bf16[4,512,1024]{2,1,0:T(8,128)(2,1)S(1)}, bf16[512,1024]{1,0:T(8,128)(2,1)S(1)}, bf16[512,256]{1,0:T(8,128)(2,1)S(1)}, bf16[512,1024]{1,0:T(8,128)(...) custom-call(s32[3]{0:T(128)S(1)} %pad_add_fusion.where_ref, bf16[128,1024]{1,0:T(8,128)(2,1)S(1)} %pad_maximum_fusion.1.piece0, ...), custom_call_target="tpu_custom_call" | custom-call | flops 6700000256 | bytes 12000000 | tf_op jit(solution)/shard_map/front/pallas_call | solution.py:179
  83.3 5.9 %front.7 = (bf16[4,512,1024]{2,1,0:T(8,128)(2,1)S(1)}, bf16[512,1024]{1,0:T(8,128)(2,1)S(1)}, bf16[512,256]{1,0:T(8,128)(2,1)S(1)}, bf16[512,1024]{1,0:T(8,128)(...) custom-call(s32[3]{0:T(128)S(1)} %pad_add_fusion.where_ref, bf16[128,1024]{1,0:T(8,128)(2,1)S(1)} %pad_maximum_fusion.2.piece0, ...), custom_call_target="tpu_custom_call" | custom-call | flops 6700000256 | bytes 12000000 | tf_op jit(solution)/shard_map/front/pallas_call | solution.py:179
  89.2 1.7 %collective-permute-done.15.piece3 = bf16[128,1024]{1,0:T(8,128)(2,1)S(1)} collective-permute-done((bf16[128,1024]{1,0:T(8,128)(2,1)S(1)}, bf16[128,1024]{1,0:T(8,128)(2,1)S(1)}, u32[]{:S(2)}, u32[]{:S(2)}) %collective-permute-start.15) | collective-permute-done | bytes 262176 | tf_op jit(solution)/shard_map/ppermute | solution.py:498
  90.9 5.9 %front.6 = (bf16[4,512,1024]{2,1,0:T(8,128)(2,1)S(1)}, bf16[512,1024]{1,0:T(8,128)(2,1)S(1)}, bf16[512,256]{1,0:T(8,128)(2,1)S(1)}, bf16[512,1024]{1,0:T(8,128)(...) custom-call(s32[3]{0:T(128)S(1)} %pad_add_fusion.where_ref, bf16[128,1024]{1,0:T(8,128)(2,1)S(1)} %pad_maximum_fusion.piece0, ...), custom_call_target="tpu_custom_call" | custom-call | flops 6700000256 | bytes 12000000 | tf_op jit(solution)/shard_map/front/pallas_call | solution.py:179
  96.8 1.1 fusion.28
  98.0 1.5 products.3
  99.5 9.7 %collective-permute-start.19 = (bf16[1,128,1024]{2,1,0:T(8,128)(2,1)S(1)}, bf16[1,128,1024]{2,1,0:T(8,128)(2,1)S(1)}, u32[]{:S(2)}, u32[]{:S(2)}) collective-permute-start(bf16[1,128,1024]{2,1,0:T(8,128)(2,1)S(1)} %constant_dynamic-slice_fusion.2), channel_id=1, source_target_pairs={{0,1},{1,0},{2,3},{3,2},{4,5},{5,4},{6,7},{7,6},{8,9},{9,8},{10,11... | collective-permute-start | bytes 786440 | tf_op jit(solution)/shard_map/ppermute | solution.py:519
  109.4 0.8 collective-permute-start.23
  110.2 1.3 collective-permute-start.24
  111.6 0.8 collective-permute-start.20
  112.4 3.1 %products.4 = bf16[2,256,1024]{2,1,0:T(8,128)(2,1)S(1)} custom-call(bf16[512,1024]{1,0:T(8,128)(2,1)S(1)} %get-tuple-element.161.refs_0_.dz_ref, bf16[512,1024]{1,0:T(8,128)(2,1)S(1)} %get-tuple-element.172.refs_1_.dz_ref, bf16[512,1024]{1,0:T(8,128)(2,1)S(1)} %get-tuple-element.177.refs_2_.dz_ref, bf16[512,1024]{1,0:T(8,128)(2,1)S(1)} %get-tuple-element.185.refs_3_.dz_ref, ...), custom_call_target="tpu_custom_call" | custom-call | flops 4400000000 | bytes 10000000 | tf_op jit(solution)/shard_map/products/pallas_call | solution.py:265
  115.5 4.4 %collective-permute-done.20 = bf16[1,128,1024]{2,1,0:T(8,128)(2,1)S(1)} collective-permute-done((bf16[1,128,1024]{2,1,0:T(8,128)(2,1)S(1)}, bf16[1,128,1024]{2,1,0:T(8,128)(2,1)S(1)}, u32[]{:S(2)}, u32[]{:S(2)}) %collective-permute-start.20) | collective-permute-done | bytes 262176 | tf_op jit(solution)/shard_map/ppermute | solution.py:523
  120.0 0.9 collective-permute-start.21
  120.9 3.1 %products.5 = bf16[2,256,1024]{2,1,0:T(8,128)(2,1)S(1)} custom-call(bf16[512,1024]{1,0:T(8,128)(2,1)S(1)} %get-tuple-element.161.refs_0_.dz_ref, bf16[512,1024]{1,0:T(8,128)(2,1)S(1)} %get-tuple-element.172.refs_1_.dz_ref, bf16[512,1024]{1,0:T(8,128)(2,1)S(1)} %get-tuple-element.177.refs_2_.dz_ref, bf16[512,1024]{1,0:T(8,128)(2,1)S(1)} %get-tuple-element.185.refs_3_.dz_ref, ...), custom_call_target="tpu_custom_call" | custom-call | flops 4400000000 | bytes 10000000 | tf_op jit(solution)/shard_map/products/pallas_call | solution.py:265
  124.5 0.8 collective-permute-start.27
  125.3 3.8 %taps.4 = f32[32,1024]{1,0:T(8,128)S(1)} custom-call(bf16[4,512,1024]{2,1,0:T(8,128)(2,1)S(1)} %get-tuple-element.147.refs_4_.maps_ref, bf16[512,1024]{1,0:T(8,128)(2,1)S(1)} %get-tuple-element.161.refs_0_.dz_ref, bf16[3,256,1024]{2,1,0:T(8,128)(2,1)S(1)} %copy-done.2), custom_call_target="tpu_custom_call" | custom-call | flops 4499999744 | bytes 4000000 | tf_op jit(solution)/shard_map/taps/pallas_call | solution.py:224
  129.3 3.8 %taps.5 = f32[32,1024]{1,0:T(8,128)S(1)} custom-call(bf16[4,512,1024]{2,1,0:T(8,128)(2,1)S(1)} %get-tuple-element.148.refs_5_.maps_ref, bf16[512,1024]{1,0:T(8,128)(2,1)S(1)} %get-tuple-element.172.refs_1_.dz_ref, bf16[3,256,1024]{2,1,0:T(8,128)(2,1)S(1)} %copy-done.2), custom_call_target="tpu_custom_call" | custom-call | flops 4499999744 | bytes 4000000 | tf_op jit(solution)/shard_map/taps/pallas_call | solution.py:224
  133.1 0.8 collective-permute-start.28
  133.9 0.7 collective-permute-start.26
  134.6 3.8 %taps.6 = f32[32,1024]{1,0:T(8,128)S(1)} custom-call(bf16[4,512,1024]{2,1,0:T(8,128)(2,1)S(1)} %get-tuple-element.149.refs_6_.maps_ref, bf16[512,1024]{1,0:T(8,128)(2,1)S(1)} %get-tuple-element.177.refs_2_.dz_ref, bf16[3,256,1024]{2,1,0:T(8,128)(2,1)S(1)} %copy-done.2), custom_call_target="tpu_custom_call" | custom-call | flops 4499999744 | bytes 4000000 | tf_op jit(solution)/shard_map/taps/pallas_call | solution.py:224
  138.7 3.8 %taps.7 = f32[32,1024]{1,0:T(8,128)S(1)} custom-call(bf16[4,512,1024]{2,1,0:T(8,128)(2,1)S(1)} %get-tuple-element.150.refs_7_.maps_ref, bf16[512,1024]{1,0:T(8,128)(2,1)S(1)} %get-tuple-element.185.refs_3_.dz_ref, bf16[3,256,1024]{2,1,0:T(8,128)(2,1)S(1)} %copy-done.2), custom_call_target="tpu_custom_call" | custom-call | flops 4499999744 | bytes 4000000 | tf_op jit(solution)/shard_map/taps/pallas_call | solution.py:224
  142.6 1.3 collective-permute-start.29
  144.1 0.8 collective-permute-done.29
  144.9 0.8 collective-permute-start.30
  145.7 0.5 fetch.1
  146.3 4.7 %collective-permute-done.30 = bf16[48,1024]{1,0:T(8,128)(2,1)S(1)} collective-permute-done((bf16[48,1024]{1,0:T(8,128)(2,1)S(1)}, bf16[48,1024]{1,0:T(8,128)(2,1)S(1)}, u32[]{:S(2)}, u32[]{:S(2)}) %collective-permute-start.30) | collective-permute-done | bytes 98336 | tf_op jit(solution)/shard_map/ppermute | solution.py:529
  151.2 1.3 collective-permute-start.32
  153.3 0.8 collective-permute-done.32.rest2
  154.0 0.7 collective-permute-done.31.rest1
  154.8 7.1 %update.1 = (f32[1,256,1024]{2,1,0:T(8,128)}, f32[1,3,256,1024]{3,2,1,0:T(8,128)}, f32[1,256,2048]{2,1,0:T(8,128)}, f32[1,256,1280]{2,1,0:T(8,128)}, f32[27,1,10...) custom-call(s32[1]{0:T(128)} %bitcast.core_ref, ...), custom_call_target="tpu_custom_call" | custom-call | flops 4000000 | bytes 20000000 | tf_op jit(solution)/shard_map/update/pallas_call | solution.py:445
  (135 shorter events, 4.2 us)
Async XLA Ops:
  0.6 13.8 %copy-start.15 = (s32[4]{0:T(128)S(1)}, s32[4]{0:T(128)}, u32[]{:S(2)}) copy-start(s32[4]{0:T(128)} %param.17) | copy-start | bytes 52
  0.7 21.0 %copy-start = (f32[1,3,256,1024]{3,2,1,0:T(8,128)S(1)}, f32[1,3,256,1024]{3,2,1,0:T(8,128)}, u32[]{:S(2)}) copy-start(f32[1,3,256,1024]{3,2,1,0:T(8,128)} %refs_1_) | copy-start | bytes 9437188
  3.1 28.2 %all-to-all-start = ((bf16[32,16,1024]{2,1,0:T(8,128)(2,1)}), bf16[32,16,1024]{2,1,0:T(8,128)(2,1)}, u32[]{:S(2)}, u32[]{:S(2)}) async-start(bf16[32,16,1024]{2,1,0:T(8,128)(2,1)} %bitcast.73), calls=%async_computation | async-start | bytes 2097152 | tf_op jit(solution)/shard_map/all_to_all | solution.py:566
  21.7 1.4 copy-start.5
  21.7 2.3 %copy-start.13 = (f32[1,19]{1,0:T(1,128)S(1)}, f32[1,19]{1,0:T(1,128)}, u32[]{:S(2)}) copy-start(f32[1,19]{1,0:T(1,128)} %b_class.1) | copy-start | bytes 232
  26.6 3.6 %copy-start.3 = (f32[1,256,1280]{2,1,0:T(8,128)S(1)}, f32[1,256,1280]{2,1,0:T(8,128)}, u32[]{:S(2)}) copy-start(f32[1,256,1280]{2,1,0:T(8,128)} %refs_3_) | copy-start | bytes 3932164
  30.2 5.2 %copy-start.11 = (f32[1,5,256]{2,0,1:T(1,128)S(1)}, f32[1,5,256]{2,0,1:T(1,128)}, u32[]{:S(2)}) copy-start(f32[1,5,256]{2,0,1:T(1,128)} %param.23) | copy-start | bytes 15364
  30.2 7.0 %copy-start.10 = (f32[1,19,256]{2,0,1:T(1,128)S(1)}, f32[1,19,256]{2,0,1:T(1,128)}, u32[]{:S(2)}) copy-start(f32[1,19,256]{2,0,1:T(1,128)} %param.26) | copy-start | bytes 58372
  32.8 5.7 %collective-permute-start = (bf16[72,1024]{1,0:T(8,128)(2,1)}, bf16[72,1024]{1,0:T(8,128)(2,1)S(1)}, u32[]{:S(2)}, u32[]{:S(2)}) collective-permute-start(bf16[72,1024]{1,0:T(8,128)(2,1)} %pad_maximum_fusion.5), channel_id=1, source_target_pairs={{0,64},{4,68},{8,72},{12,76},{16,80},{20,84},{24,88},{28,92},{32,9... | collective-permute-start | bytes 442376 | tf_op jit(solution)/shard_map/ppermute | solution.py:573
  38.6 6.9 %collective-permute-start.7 = (bf16[64,1024]{1,0:T(8,128)(2,1)S(1)}, bf16[64,1024]{1,0:T(8,128)(2,1)S(1)}, u32[]{:S(2)}, u32[]{:S(2)}) collective-permute-start(bf16[64,1024]{1,0:T(8,128)(2,1)S(1)} %bitcast.84), channel_id=1, source_target_pairs={{0,4},{4,8},{8,12},{12,0},{16,20},{20,24},{24,28},{28,16},{32,36},... | collective-permute-start | bytes 393224 | tf_op jit(solution)/shard_map/ppermute | solution.py:496
  39.6 7.5 %collective-permute-start.8 = (bf16[64,1024]{1,0:T(8,128)(2,1)S(1)}, bf16[64,1024]{1,0:T(8,128)(2,1)S(1)}, u32[]{:S(2)}, u32[]{:S(2)}) collective-permute-start(bf16[64,1024]{1,0:T(8,128)(2,1)S(1)} %bitcast.85), channel_id=1, source_target_pairs={{0,12},{4,0},{8,4},{12,8},{16,28},{20,16},{24,20},{28,24},{32,44},... | collective-permute-start | bytes 393224 | tf_op jit(solution)/shard_map/ppermute | solution.py:497
  41.4 6.3 %collective-permute-start.9 = (bf16[64,1024]{1,0:T(8,128)(2,1)S(1)}, bf16[64,1024]{1,0:T(8,128)(2,1)S(1)}, u32[]{:S(2)}, u32[]{:S(2)}) collective-permute-start(bf16[64,1024]{1,0:T(8,128)(2,1)S(1)} %bitcast.86), channel_id=1, source_target_pairs={{0,8},{4,12},{8,0},{12,4},{16,24},{20,28},{24,16},{28,20},{32,40},... | collective-permute-start | bytes 393224 | tf_op jit(solution)/shard_map/ppermute | solution.py:498
  42.6 19.4 %copy-start.14 = (bf16[256,2048]{1,0:T(8,128)(2,1)S(1)}, bf16[256,2048]{1,0:T(8,128)(2,1)}, u32[]{:S(2)}) copy-start(bf16[256,2048]{1,0:T(8,128)(2,1)} %convert_bitcast_fusion.1) | copy-start | bytes 3145732
  42.8 5.6 %collective-permute-start.1 = (bf16[72,1024]{1,0:T(8,128)(2,1)S(1)}, bf16[72,1024]{1,0:T(8,128)(2,1)S(1)}, u32[]{:S(2)}, u32[]{:S(2)}) collective-permute-start(bf16[72,1024]{1,0:T(8,128)(2,1)S(1)} %pad_maximum_fusion.6), channel_id=1, source_target_pairs={{0,16},{4,20},{8,24},{12,28},{16,32},{20,36},{24,40},{28,44},{32,4... | collective-permute-start | bytes 442376 | tf_op jit(solution)/shard_map/ppermute | solution.py:496
  44.0 4.3 %collective-permute-start.2 = (bf16[72,1024]{1,0:T(8,128)(2,1)S(1)}, bf16[72,1024]{1,0:T(8,128)(2,1)S(1)}, u32[]{:S(2)}, u32[]{:S(2)}) collective-permute-start(bf16[72,1024]{1,0:T(8,128)(2,1)S(1)} %pad_maximum_fusion.6), channel_id=1, source_target_pairs={{0,48},{4,52},{8,56},{12,60},{16,0},{20,4},{24,8},{28,12},{32,16},... | collective-permute-start | bytes 442376 | tf_op jit(solution)/shard_map/ppermute | solution.py:497
  45.5 16.8 %slice-start = ((f32[1,5,256]{2,0,1:T(1,128)}), f32[1,1,256]{2,0,1:T(1,128)S(1)}, s32[]{:S(2)}) async-start(f32[1,5,256]{2,0,1:T(1,128)} %param.23), calls=%async_computation.1 | async-start | bytes 2048 | tf_op jit(solution)/shard_map/slice | solution.py:611
  45.5 5.9 %collective-permute-start.3 = (bf16[72,1024]{1,0:T(8,128)(2,1)S(1)}, bf16[72,1024]{1,0:T(8,128)(2,1)S(1)}, u32[]{:S(2)}, u32[]{:S(2)}) collective-permute-start(bf16[72,1024]{1,0:T(8,128)(2,1)S(1)} %pad_maximum_fusion.6), channel_id=1, source_target_pairs={{0,32},{4,36},{8,40},{12,44},{16,48},{20,52},{24,56},{28,60},{32,0... | collective-permute-start | bytes 442376 | tf_op jit(solution)/shard_map/ppermute | solution.py:498
  47.1 15.5 %copy-start.12 = (f32[1,256]{1,0:T(1,128)S(1)}, f32[1,256]{1,0:T(1,128)}, u32[]{:S(2)}) copy-start(f32[1,256]{1,0:T(1,128)} %b_proj.1) | copy-start | bytes 3076
  47.1 16.5 %copy-start.2 = (bf16[3,256,1024]{2,1,0:T(8,128)(2,1)S(1)}, bf16[3,256,1024]{2,1,0:T(8,128)(2,1)}, u32[]{:S(2)}) copy-start(bf16[3,256,1024]{2,1,0:T(8,128)(2,1)} %convert_bitcast_fusion.w_point) | copy-start | bytes 4718596
  47.2 16.5 %copy-start.7 = (bf16[256,1024]{1,0:T(8,128)(2,1)S(1)}, bf16[256,1024]{1,0:T(8,128)(2,1)}, u32[]{:S(2)}) copy-start(bf16[256,1024]{1,0:T(8,128)(2,1)} %convert_bitcast_fusion.3.w_plain) | copy-start | bytes 1572868
  47.2 16.5 %copy-start.8 = (bf16[256,1024]{1,0:T(8,128)(2,1)S(1)}, bf16[256,1024]{1,0:T(8,128)(2,1)}, u32[]{:S(2)}) copy-start(bf16[256,1024]{1,0:T(8,128)(2,1)} %slice.251.w_proj) | copy-start | bytes 1572868
  47.2 16.5 %copy-start.9 = (f32[1,3,9,1024]{3,0,2,1:T(1,128)S(1)}, f32[1,3,9,1024]{3,0,2,1:T(1,128)}, u32[]{:S(2)}) copy-start(f32[1,3,9,1024]{3,0,2,1:T(1,128)} %param.20) | copy-start | bytes 331780
  51.4 6.7 %collective-permute-start.4 = (bf16[136,1024]{1,0:T(8,128)(2,1)S(1)}, bf16[136,1024]{1,0:T(8,128)(2,1)S(1)}, u32[]{:S(2)}, u32[]{:S(2)}) collective-permute-start(bf16[136,1024]{1,0:T(8,128)(2,1)S(1)} %get-tuple-element.115.piece0), channel_id=1, source_target_pairs={{0,4},{4,8},{8,12},{12,0},{16,20},{20,24},{24,28},{28,16},{32,36},... | collective-permute-start | bytes 835592 | tf_op jit(solution)/shard_map/ppermute | solution.py:496
  51.6 9.1 %collective-permute-start.5 = (bf16[136,1024]{1,0:T(8,128)(2,1)S(1)}, bf16[136,1024]{1,0:T(8,128)(2,1)S(1)}, u32[]{:S(2)}, u32[]{:S(2)}) collective-permute-start(bf16[136,1024]{1,0:T(8,128)(2,1)S(1)} %get-tuple-element.115.piece0), channel_id=1, source_target_pairs={{0,12},{4,0},{8,4},{12,8},{16,28},{20,16},{24,20},{28,24},{32,44},... | collective-permute-start | bytes 835592 | tf_op jit(solution)/shard_map/ppermute | solution.py:497
  54.2 7.9 %collective-permute-start.6 = (bf16[136,1024]{1,0:T(8,128)(2,1)S(1)}, bf16[136,1024]{1,0:T(8,128)(2,1)S(1)}, u32[]{:S(2)}, u32[]{:S(2)}) collective-permute-start(bf16[136,1024]{1,0:T(8,128)(2,1)S(1)} %get-tuple-element.115.piece0), channel_id=1, source_target_pairs={{0,8},{4,12},{8,0},{12,4},{16,24},{20,28},{24,16},{28,20},{32,40},... | collective-permute-start | bytes 835592 | tf_op jit(solution)/shard_map/ppermute | solution.py:498
  54.4 15.2 %collective-permute-start.10 = (bf16[128,1024]{1,0:T(8,128)(2,1)S(1)}, bf16[128,1024]{1,0:T(8,128)(2,1)S(1)}, u32[]{:S(2)}, u32[]{:S(2)}) collective-permute-start(bf16[128,1024]{1,0:T(8,128)(2,1)S(1)} %pad_maximum_fusion.1.piece0), channel_id=1, source_target_pairs={{0,16},{4,20},{8,24},{12,28},{16,32},{20,36},{24,40},{28,44},{32,4... | collective-permute-start | bytes 786440 | tf_op jit(solution)/shard_map/ppermute | solution.py:496
  54.5 15.1 %collective-permute-start.11 = (bf16[128,1024]{1,0:T(8,128)(2,1)S(1)}, bf16[128,1024]{1,0:T(8,128)(2,1)S(1)}, u32[]{:S(2)}, u32[]{:S(2)}) collective-permute-start(bf16[128,1024]{1,0:T(8,128)(2,1)S(1)} %pad_maximum_fusion.1.piece0), channel_id=1, source_target_pairs={{0,48},{4,52},{8,56},{12,60},{16,0},{20,4},{24,8},{28,12},{32,16},... | collective-permute-start | bytes 786440 | tf_op jit(solution)/shard_map/ppermute | solution.py:497
  58.1 11.5 %collective-permute-start.12 = (bf16[128,1024]{1,0:T(8,128)(2,1)S(1)}, bf16[128,1024]{1,0:T(8,128)(2,1)S(1)}, u32[]{:S(2)}, u32[]{:S(2)}) collective-permute-start(bf16[128,1024]{1,0:T(8,128)(2,1)S(1)} %pad_maximum_fusion.1.piece0), channel_id=1, source_target_pairs={{0,32},{4,36},{8,40},{12,44},{16,48},{20,52},{24,56},{28,60},{32,0... | collective-permute-start | bytes 786440 | tf_op jit(solution)/shard_map/ppermute | solution.py:498
  69.6 13.6 %collective-permute-start.16 = (bf16[128,1024]{1,0:T(8,128)(2,1)S(1)}, bf16[128,1024]{1,0:T(8,128)(2,1)S(1)}, u32[]{:S(2)}, u32[]{:S(2)}) collective-permute-start(bf16[128,1024]{1,0:T(8,128)(2,1)S(1)} %pad_maximum_fusion.2.piece0), channel_id=1, source_target_pairs={{0,16},{4,20},{8,24},{12,28},{16,32},{20,36},{24,40},{28,44},{32,4... | collective-permute-start | bytes 786440 | tf_op jit(solution)/shard_map/ppermute | solution.py:496
  70.1 13.2 %collective-permute-start.17 = (bf16[128,1024]{1,0:T(8,128)(2,1)S(1)}, bf16[128,1024]{1,0:T(8,128)(2,1)S(1)}, u32[]{:S(2)}, u32[]{:S(2)}) collective-permute-start(bf16[128,1024]{1,0:T(8,128)(2,1)S(1)} %pad_maximum_fusion.2.piece0), channel_id=1, source_target_pairs={{0,48},{4,52},{8,56},{12,60},{16,0},{20,4},{24,8},{28,12},{32,16},... | collective-permute-start | bytes 786440 | tf_op jit(solution)/shard_map/ppermute | solution.py:497
  72.4 11.0 %collective-permute-start.18 = (bf16[128,1024]{1,0:T(8,128)(2,1)S(1)}, bf16[128,1024]{1,0:T(8,128)(2,1)S(1)}, u32[]{:S(2)}, u32[]{:S(2)}) collective-permute-start(bf16[128,1024]{1,0:T(8,128)(2,1)S(1)} %pad_maximum_fusion.2.piece0), channel_id=1, source_target_pairs={{0,32},{4,36},{8,40},{12,44},{16,48},{20,52},{24,56},{28,60},{32,0... | collective-permute-start | bytes 786440 | tf_op jit(solution)/shard_map/ppermute | solution.py:498
  74.7 14.6 %collective-permute-start.13 = (bf16[128,1024]{1,0:T(8,128)(2,1)S(1)}, bf16[128,1024]{1,0:T(8,128)(2,1)S(1)}, u32[]{:S(2)}, u32[]{:S(2)}) collective-permute-start(bf16[128,1024]{1,0:T(8,128)(2,1)S(1)} %pad_maximum_fusion.piece0), channel_id=1, source_target_pairs={{0,4},{4,8},{8,12},{12,0},{16,20},{20,24},{24,28},{28,16},{32,36},... | collective-permute-start | bytes 786440 | tf_op jit(solution)/shard_map/ppermute | solution.py:496
  74.7 14.6 %collective-permute-start.14 = (bf16[128,1024]{1,0:T(8,128)(2,1)S(1)}, bf16[128,1024]{1,0:T(8,128)(2,1)S(1)}, u32[]{:S(2)}, u32[]{:S(2)}) collective-permute-start(bf16[128,1024]{1,0:T(8,128)(2,1)S(1)} %pad_maximum_fusion.piece0), channel_id=1, source_target_pairs={{0,12},{4,0},{8,4},{12,8},{16,28},{20,16},{24,20},{28,24},{32,44},... | collective-permute-start | bytes 786440 | tf_op jit(solution)/shard_map/ppermute | solution.py:497
  83.2 7.7 %collective-permute-start.15 = (bf16[128,1024]{1,0:T(8,128)(2,1)S(1)}, bf16[128,1024]{1,0:T(8,128)(2,1)S(1)}, u32[]{:S(2)}, u32[]{:S(2)}) collective-permute-start(bf16[128,1024]{1,0:T(8,128)(2,1)S(1)} %pad_maximum_fusion.piece0), channel_id=1, source_target_pairs={{0,8},{4,12},{8,0},{12,4},{16,24},{20,28},{24,16},{28,20},{32,40},... | collective-permute-start | bytes 786440 | tf_op jit(solution)/shard_map/ppermute | solution.py:498
  99.5 11.9 %collective-permute-start.19 = (bf16[1,128,1024]{2,1,0:T(8,128)(2,1)S(1)}, bf16[1,128,1024]{2,1,0:T(8,128)(2,1)S(1)}, u32[]{:S(2)}, u32[]{:S(2)}) collective-permute-start(bf16[1,128,1024]{2,1,0:T(8,128)(2,1)S(1)} %constant_dynamic-slice_fusion.2), channel_id=1, source_target_pairs={{0,1},{1,0},{2,3},{3,2},{4,5},{5,4},{6,7},{7,6},{8,9},{9,8},{10,11... | collective-permute-start | bytes 786440 | tf_op jit(solution)/shard_map/ppermute | solution.py:519
  109.3 15.0 %collective-permute-start.22 = (f32[4,2816]{1,0:T(4,128)S(1)}, f32[4,2816]{1,0:T(4,128)S(1)}, u32[]{:S(2)}, u32[]{:S(2)}) collective-permute-start(f32[4,2816]{1,0:T(4,128)S(1)} %constant_dynamic-update-slice_fusion.2), channel_id=1, source_target_pairs={{0,1},{1,0},{2,3},{3,2},{4,5},{5,4},{6,7},{7,6},{8,9},{9,8},{10,11... | collective-permute-start | bytes 135176 | tf_op jit(solution)/shard_map/ppermute | solution.py:504
  109.4 14.9 %collective-permute-start.23 = (f32[4,2816]{1,0:T(4,128)S(1)}, f32[4,2816]{1,0:T(4,128)S(1)}, u32[]{:S(2)}, u32[]{:S(2)}) collective-permute-start(f32[4,2816]{1,0:T(4,128)S(1)} %constant_dynamic-update-slice_fusion.2), channel_id=1, source_target_pairs={{0,2},{1,3},{2,0},{3,1},{4,6},{5,7},{6,4},{7,5},{8,10},{9,11},{10,... | collective-permute-start | bytes 135176 | tf_op jit(solution)/shard_map/ppermute | solution.py:504
  110.2 14.1 %collective-permute-start.24 = (f32[4,2816]{1,0:T(4,128)S(1)}, f32[4,2816]{1,0:T(4,128)S(1)}, u32[]{:S(2)}, u32[]{:S(2)}) collective-permute-start(f32[4,2816]{1,0:T(4,128)S(1)} %constant_dynamic-update-slice_fusion.2), channel_id=1, source_target_pairs={{0,3},{1,2},{2,1},{3,0},{4,7},{5,6},{6,5},{7,4},{8,11},{9,10},{10,... | collective-permute-start | bytes 135176 | tf_op jit(solution)/shard_map/ppermute | solution.py:504
  111.6 8.3 %collective-permute-start.20 = (bf16[1,128,1024]{2,1,0:T(8,128)(2,1)S(1)}, bf16[1,128,1024]{2,1,0:T(8,128)(2,1)S(1)}, u32[]{:S(2)}, u32[]{:S(2)}) collective-permute-start(bf16[1,128,1024]{2,1,0:T(8,128)(2,1)S(1)} %add_convert_fusion.5), channel_id=1, source_target_pairs={{0,2},{1,3},{2,0},{3,1},{4,6},{5,7},{6,4},{7,5},{8,10},{9,11},{10,... | collective-permute-start | bytes 786440 | tf_op jit(solution)/shard_map/ppermute | solution.py:523
  120.0 4.0 %collective-permute-start.21 = (bf16[2,128,1024]{2,1,0:T(8,128)(2,1)S(1)}, bf16[2,128,1024]{2,1,0:T(8,128)(2,1)S(1)}, u32[]{:S(2)}, u32[]{:S(2)}) collective-permute-start(bf16[2,128,1024]{2,1,0:T(8,128)(2,1)S(1)} %constant_dynamic-slice_fusion.1), channel_id=1, source_target_pairs={{0,1},{1,0},{2,3},{3,2},{4,5},{5,4},{6,7},{7,6},{8,9},{9,8},{10,11... | collective-permute-start | bytes 1572872 | tf_op jit(solution)/shard_map/ppermute | solution.py:519
  124.3 4.8 %collective-permute-start.25 = (bf16[2,128,1024]{2,1,0:T(8,128)(2,1)S(1)}, bf16[2,128,1024]{2,1,0:T(8,128)(2,1)S(1)}, u32[]{:S(2)}, u32[]{:S(2)}) collective-permute-start(bf16[2,128,1024]{2,1,0:T(8,128)(2,1)S(1)} %constant_dynamic-slice_fusion), channel_id=1, source_target_pairs={{0,1},{1,0},{2,3},{3,2},{4,5},{5,4},{6,7},{7,6},{8,9},{9,8},{10,11... | collective-permute-start | bytes 1572872 | tf_op jit(solution)/shard_map/ppermute | solution.py:519
  124.5 14.0 %collective-permute-start.27 = (bf16[2,128,1024]{2,1,0:T(8,128)(2,1)S(1)}, bf16[2,128,1024]{2,1,0:T(8,128)(2,1)S(1)}, u32[]{:S(2)}, u32[]{:S(2)}) collective-permute-start(bf16[2,128,1024]{2,1,0:T(8,128)(2,1)S(1)} %add_convert_fusion.3), channel_id=1, source_target_pairs={{0,2},{1,3},{2,0},{3,1},{4,6},{5,7},{6,4},{7,5},{8,10},{9,11},{10,... | collective-permute-start | bytes 1572872 | tf_op jit(solution)/shard_map/ppermute | solution.py:523
  133.1 5.5 %collective-permute-start.28 = (bf16[1,128,1024]{2,1,0:T(8,128)(2,1)S(1)}, bf16[1,128,1024]{2,1,0:T(8,128)(2,1)S(1)}, u32[]{:S(2)}, u32[]{:S(2)}) collective-permute-start(bf16[1,128,1024]{2,1,0:T(8,128)(2,1)S(1)} %add_convert_fusion.4.mine0), channel_id=1, source_target_pairs={{0,1},{1,0},{2,3},{3,2},{4,5},{5,4},{6,7},{7,6},{8,9},{9,8},{10,11... | collective-permute-start | bytes 786440 | tf_op jit(solution)/shard_map/ppermute | solution.py:657
  133.9 17.1 %collective-permute-start.26 = (bf16[2,128,1024]{2,1,0:T(8,128)(2,1)S(1)}, bf16[2,128,1024]{2,1,0:T(8,128)(2,1)S(1)}, u32[]{:S(2)}, u32[]{:S(2)}) collective-permute-start(bf16[2,128,1024]{2,1,0:T(8,128)(2,1)S(1)} %add_convert_fusion.2), channel_id=1, source_target_pairs={{0,2},{1,3},{2,0},{3,1},{4,6},{5,7},{6,4},{7,5},{8,10},{9,11},{10,... | collective-permute-start | bytes 1572872 | tf_op jit(solution)/shard_map/ppermute | solution.py:675
  138.7 7.0 %copy-start.4 = (f32[1,256,1280]{2,1,0:T(8,128)S(1)}, f32[1,256,1280]{2,1,0:T(8,128)}, u32[]{:S(2)}) copy-start(f32[1,256,1280]{2,1,0:T(8,128)} %refs_3_) | copy-start | bytes 3932164
  138.7 7.0 %copy-start.6 = (f32[1,256,1024]{2,1,0:T(8,128)S(1)}, f32[1,256,1024]{2,1,0:T(8,128)}, u32[]{:S(2)}) copy-start(f32[1,256,1024]{2,1,0:T(8,128)} %refs_0_) | copy-start | bytes 3145732
  142.6 3.2 %copy-start.1 = (f32[1,256,2048]{2,1,0:T(8,128)S(1)}, f32[1,256,2048]{2,1,0:T(8,128)}, u32[]{:S(2)}) copy-start(f32[1,256,2048]{2,1,0:T(8,128)} %refs_2_) | copy-start | bytes 6291460
  142.6 2.2 %collective-permute-start.29 = (bf16[48,1024]{1,0:T(8,128)(2,1)S(1)}, bf16[48,1024]{1,0:T(8,128)(2,1)S(1)}, u32[]{:S(2)}, u32[]{:S(2)}) collective-permute-start(bf16[48,1024]{1,0:T(8,128)(2,1)S(1)} %maximum_maximum_fusion), channel_id=1, source_target_pairs={{0,1},{1,0},{2,3},{3,2},{4,5},{5,4},{6,7},{7,6},{8,9},{9,8},{10,11... | collective-permute-start | bytes 294920 | tf_op jit(solution)/shard_map/ppermute | solution.py:527
  144.9 6.0 %collective-permute-start.30 = (bf16[48,1024]{1,0:T(8,128)(2,1)S(1)}, bf16[48,1024]{1,0:T(8,128)(2,1)S(1)}, u32[]{:S(2)}, u32[]{:S(2)}) collective-permute-start(bf16[48,1024]{1,0:T(8,128)(2,1)S(1)} %add_convert_fusion.6), channel_id=1, source_target_pairs={{0,2},{1,3},{2,0},{3,1},{4,6},{5,7},{6,4},{7,5},{8,10},{9,11},{10,... | collective-permute-start | bytes 294920 | tf_op jit(solution)/shard_map/ppermute | solution.py:529
  151.2 2.9 %collective-permute-start.32 = (bf16[2,128,1024]{2,1,0:T(8,128)(2,1)S(1)}, bf16[2,128,1024]{2,1,0:T(8,128)(2,1)S(1)}, u32[]{:S(2)}, u32[]{:S(2)}) collective-permute-start(bf16[2,128,1024]{2,1,0:T(8,128)(2,1)S(1)} %add_convert_fusion.mine2), channel_id=1, source_target_pairs={{0,1},{1,0},{2,3},{3,2},{4,5},{5,4},{6,7},{7,6},{8,9},{9,8},{10,11... | collective-permute-start | bytes 1572872 | tf_op jit(solution)/shard_map/ppermute | solution.py:680
  152.5 2.3 %collective-permute-start.31 = (bf16[2,128,1024]{2,1,0:T(8,128)(2,1)S(1)}, bf16[2,128,1024]{2,1,0:T(8,128)(2,1)S(1)}, u32[]{:S(2)}, u32[]{:S(2)}) collective-permute-start(bf16[2,128,1024]{2,1,0:T(8,128)(2,1)S(1)} %add_convert_fusion.1.mine1), channel_id=1, source_target_pairs={{0,1},{1,0},{2,3},{3,2},{4,5},{5,4},{6,7},{7,6},{8,9},{9,8},{10,11... | collective-permute-start | bytes 1572872 | tf_op jit(solution)/shard_map/ppermute | solution.py:680
